TPU v7x, 512 devices: a whole 4x8x8 slice. The times are simulated.
512 devices in a mesh: dp: 32 (over x, y), seq: 16 (over z, core).
Axes of the slice: x: 4, y: 8, z: 8, core: 2. Of those that a mesh axis runs over, the one named last changes fastest.
Arguments:
- queries: bfloat16 [32, 2048, 2048], P('dp', 'seq'), may hold values from -6 to 6
- key_rows: bfloat16 [32, 2048, 2048], P('dp', 'seq'), may hold values from -6 to 6
- value_rows: bfloat16 [32, 2048, 2048], P('dp', 'seq'), may hold values from -6 to 6
- out_grad: bfloat16 [32, 2048, 2048], P('dp', 'seq'), may hold values from -6 to 6
- norm_gain: float32 [2048], P('dp'), may hold values from 0.25 to 1.75
- doc_starts: int32 [32, 8], P('dp'), may hold values from 0 to 2047, as said below
Outputs:
- attended: bfloat16 [32, 2048, 2048], P('dp', 'seq')
- query_grad: bfloat16 [32, 2048, 2048], P('dp', 'seq')
- key_grad: bfloat16 [32, 2048, 2048], P('dp', 'seq')
- value_grad: bfloat16 [32, 2048, 2048], P('dp', 'seq')
- gain_grad: float32 [2048], P('dp')
Inputs may be any that keep to these rules, and one draw needn't show every extreme that they name: `doc_starts`: each row begins with 0 and rises strictly.
All inputs are finite; a program needn't handle non-finite values.
Results may differ from a plain program's by a relative error of at most 0.011.
Values sent between devices are 32-bit elements; how exact they have to be, the bound alone decides.
No kernel may reach another device: no remote copies, remote signals or barrier semaphores. Data moves between devices by JAX's collectives and lax.ppermute only.
A program may use at most 128 MiB of HBM per device.

v0:
```python
import math

import jax
import jax.numpy as jnp
from jax import lax
from jax.sharding import PartitionSpec as P

HEADS = 16
FEAT = 128


EPS = 1e-06


def entering(value, axis, join, neutral, backward):
    count, mine = (lax.axis_size(axis), lax.axis_index(axis))
    pieces = jax.tree.map(lambda part: lax.all_gather(part, axis), value)
    if backward:
        pieces = jax.tree.map(lambda part: part[::-1], pieces)
        mine = count - 1 - mine
    subtotal = jax.tree.map(
        lambda part, zero: jnp.full_like(part, 0) + jnp.asarray(zero, part.dtype), value, neutral
    )

    def hop(position, subtotal):
        longer = join(subtotal, jax.tree.map(lambda part: part[position], pieces))
        return jax.tree.map(lambda new, old: jnp.where(position < mine, new, old), longer, subtotal)

    return lax.fori_loop(0, count - 1, hop, subtotal)


def features(x):
    return jnp.where(x > 0, x + 1.0, jnp.exp(jnp.minimum(x, 0.0)))


def slope(x):
    return jnp.where(x > 0, 1.0, jnp.exp(jnp.minimum(x, 0.0)))


def combine(earlier, later):
    return (later[0] + later[1] * earlier[0], earlier[1] * later[1])


def shards(queries, key_rows, value_rows, out_grad, norm_gain, doc_starts):
    batch, tok_rows, _ = queries.shape
    shape = (batch, tok_rows, HEADS, FEAT)
    seq_index = lax.axis_index("seq")
    seq_count = lax.axis_size("seq")
    first = seq_index * tok_rows
    pos = first + jnp.arange(tok_rows, dtype=jnp.int32)
    docs = jnp.sum((doc_starts[:, None, :] <= pos[None, :, None]).astype(jnp.int32), -1)
    before = jnp.sum((doc_starts <= first - 1).astype(jnp.int32), -1)
    last_doc = docs[:, -1]
    cin = (docs == before[:, None]).astype(jnp.float32)[..., None, None]
    eout = (docs == last_doc[:, None]).astype(jnp.float32)[..., None, None]
    passes = (last_doc == before).astype(jnp.float32)[:, None, None, None]
    tri = jnp.arange(tok_rows)[:, None] >= jnp.arange(tok_rows)[None, :]
    mask = (tri[None] & (docs[:, :, None] == docs[:, None, :])).astype(jnp.float32)[:, None]
    q32 = queries.astype(jnp.float32).reshape(shape)
    k32 = key_rows.astype(jnp.float32).reshape(shape)
    values = value_rows.reshape(shape)
    qb = features(q32).astype(jnp.bfloat16)
    kb = features(k32).astype(jnp.bfloat16)
    scores = (
        jnp.einsum("bthf,bshf->bhts", qb, kb, preferred_element_type=jnp.float32) * mask
    ).astype(jnp.bfloat16)
    intra = jnp.einsum("bhts,bshf->bthf", scores, values, preferred_element_type=jnp.float32)
    keep_keys = (kb * eout).astype(jnp.bfloat16)
    local = jnp.einsum("bthf,bthe->bhfe", keep_keys, values, preferred_element_type=jnp.float32)
    zero = jnp.zeros_like(local)
    incoming, _ = entering((local, passes), "seq", combine, (zero, jnp.ones_like(passes)), False)
    incoming = lax.optimization_barrier(incoming)
    inb = incoming.astype(jnp.bfloat16)
    num = intra + jnp.einsum("bthf,bhfe->bthe", qb, inb, preferred_element_type=jnp.float32) * cin
    recip = lax.rsqrt(jnp.mean(num * num, -1, keepdims=True) + EPS)
    normed = num * recip
    gains = lax.all_gather(norm_gain, "dp", axis=0, tiled=True).reshape(HEADS, FEAT)
    attended = (normed * gains).astype(jnp.bfloat16)
    dy = out_grad.astype(jnp.float32).reshape(shape)
    upper = dy * gains
    dn = (recip * upper - normed * recip * jnp.mean(upper * normed, -1, keepdims=True)).astype(
        jnp.bfloat16
    )
    gterm = jnp.sum(dy * normed, axis=(0, 1)).reshape(HEADS * FEAT)
    dscores = (
        jnp.einsum("bthf,bshf->bhts", dn, values, preferred_element_type=jnp.float32) * mask
    ).astype(jnp.bfloat16)
    masked_dn = (dn * cin).astype(jnp.bfloat16)
    state_grad = jnp.einsum("bthf,bthe->bhfe", qb, masked_dn, preferred_element_type=jnp.float32)
    outgoing, _ = entering(
        (state_grad, passes), "seq", combine, (zero, jnp.ones_like(passes)), True
    )
    outgoing = lax.optimization_barrier(outgoing)
    outb = outgoing.astype(jnp.bfloat16)
    dq = jnp.einsum("bhts,bshf->bthf", dscores, kb, preferred_element_type=jnp.float32)
    dq = dq + jnp.einsum("bthe,bhfe->bthf", dn, inb, preferred_element_type=jnp.float32) * cin
    dk = jnp.einsum("bhts,bthf->bshf", dscores, qb, preferred_element_type=jnp.float32)
    dk = dk + jnp.einsum("bthe,bhfe->bthf", values, outb, preferred_element_type=jnp.float32) * eout
    dv = jnp.einsum("bhts,bthf->bshf", scores, dn, preferred_element_type=jnp.float32)
    dv = dv + jnp.einsum("bthf,bhfe->bthe", kb, outb, preferred_element_type=jnp.float32) * eout
    dq = dq * slope(q32)
    dk = dk * slope(k32)
    total_rows = batch * tok_rows * lax.axis_size("dp") * seq_count
    summed = lax.psum(gterm, "seq")
    gain_part = lax.psum_scatter(summed, "dp", scatter_dimension=0, tiled=True)
    gain_grad = gain_part / math.sqrt(total_rows)
    flat = (batch, tok_rows, HEADS * FEAT)
    return (
        attended.reshape(flat),
        dq.astype(jnp.bfloat16).reshape(flat),
        dk.astype(jnp.bfloat16).reshape(flat),
        dv.astype(jnp.bfloat16).reshape(flat),
        gain_grad,
    )


def solution(mesh):
    return jax.shard_map(
        shards,
        mesh=mesh,
        in_specs=(
            P("dp", "seq", None),
            P("dp", "seq", None),
            P("dp", "seq", None),
            P("dp", "seq", None),
            P("dp"),
            P("dp", None),
        ),
        out_specs=(
            P("dp", "seq", None),
            P("dp", "seq", None),
            P("dp", "seq", None),
            P("dp", "seq", None),
            P("dp"),
        ),
        check_vma=False,
    )
```

profile of v0, /device:TPU:1, one launch (start us, length us, event | category | flops | bytes accessed | tf_op | source)
XLA Modules:
  0.0 383.4 jit_solution(5303857816454248715)
XLA Ops:
  28.0 32.1 %all-reduce = f32[16]{0:T(128)S(1)} all-reduce(f32[16]{0:T(128)S(1)} %fusion.55), channel_id=3, replica_groups=mesh['dp'=32,'seq'=16] {'seq'}, use_global_device_ids=true, to_apply=%add | all-reduce | flops 16 | bytes 128
  60.1 62.6 %all-reduce.1 = f32[2048]{0:T(1024)S(1)} all-reduce(f32[2048]{0:T(1024)S(1)} %dynamic-update-slice.1), channel_id=1, replica_groups=mesh['dp'=32,'seq'=16] {'dp'}, use_global_device_ids=true, to_apply=%add.1 | all-reduce | flops 2048 | bytes 16384
  125.1 50.8 %while.28 = (s32[]{:T(128)}, f32[1,16,128,128]{3,2,1,0:T(8,128)S(1)}, s32[]{:T(128)}, f32[16,1,16,128,128]{4,3,2,1,0:T(8,128)}, f32[16,1,1,1,1]{0,4,3,2,1:T(1,128)S(1)}, /*index=5*/s32[]{:T(128)}, s32[]{:T(128)}) while((s32[]{:T(128)}, f32[1,16,128,128]{3,2,1,0:T(8,128)S(1)}, s32[]{:T(128)}, f32[16,1,16,128,128]{4,3,2,1,0:T(8,128)}, ...), condition=%wide.region_3.4_spmd.clone, body=%wide.region_2.3_spmd.clone.sunk | while | flops 1048580 | bytes 3145853 | solution.py:29
  125.7 2.8 fusion.68
  129.1 2.8 fusion.68
  132.5 2.8 fusion.68
  135.9 2.8 fusion.68
  139.3 2.8 fusion.68
  142.6 2.8 fusion.68
  146.0 2.8 fusion.68
  149.4 2.8 fusion.68
  152.8 2.8 fusion.68
  156.2 2.8 fusion.68
  159.6 2.8 fusion.68
  163.0 2.8 fusion.68
  166.4 2.8 fusion.68
  169.7 2.8 fusion.68
  173.1 2.8 fusion.68
  196.1 58.5 %all-reduce.2 = f32[2048]{0:T(1024)S(1)} all-reduce(f32[2048]{0:T(1024)S(1)} %bitcast.171), channel_id=5, replica_groups=mesh['dp'=32,'seq'=16] {'dp'}, use_global_device_ids=true, to_apply=%region_10.11.clone | all-reduce | flops 2048 | bytes 16384
  254.7 52.5 %psum.8 = f32[64]{0:T(128)S(1)} all-reduce(f32[64]{0:T(128)S(1)} %dynamic-slice.3), channel_id=1, replica_groups=mesh['dp'=32,'seq'=16] {'seq'}, use_global_device_ids=true, to_apply=%region_9.10 | all-reduce | flops 64 | bytes 512 | tf_op jit(solution)/shard_map/psum | solution.py:104
  307.7 11.7 %rev.6 = f32[16,1,16,128,128]{4,3,2,1,0:T(8,128)} reverse(f32[16,1,16,128,128]{4,3,2,1,0:T(8,128)} %bitcast.148), dimensions={0} | reverse | bytes 33554432 | tf_op jit(solution)/shard_map/rev | solution.py:19
  319.4 51.1 %while.29 = (s32[]{:T(128)}, f32[1,16,128,128]{3,2,1,0:T(8,128)S(1)}, s32[]{:T(128)}, f32[16,1,16,128,128]{4,3,2,1,0:T(8,128)}, f32[16,1,1,1,1]{0,4,3,2,1:T(1,128)S(1)}, /*index=5*/s32[]{:T(128)}, s32[]{:T(128)}) while((s32[]{:T(128)}, f32[1,16,128,128]{3,2,1,0:T(8,128)S(1)}, s32[]{:T(128)}, f32[16,1,16,128,128]{4,3,2,1,0:T(8,128)}, ...), condition=%wide.region_7.8_spmd.clone, body=%wide.region_6.7_spmd.clone.sunk | while | flops 1048580 | bytes 3145853 | solution.py:29
  320.0 2.8 fusion.69
  323.4 2.8 fusion.69
  326.8 2.8 fusion.69
  330.3 2.8 fusion.69
  333.7 2.8 fusion.69
  337.1 2.8 fusion.69
  340.5 2.8 fusion.69
  343.9 2.8 fusion.69
  347.3 2.8 fusion.69
  357.5 2.8 fusion.69
  (99 shorter events, 80.4 us)
Async XLA Ops:
  7.2 118.0 %all-gather.6.cloned.1.call-start = ((), (), s32[]{:S(2)}) async-start(), calls=%async_computation | async-start | bytes 17825792 | tf_op jit(solution)/shard_map/all_gather | solution.py:17
  13.5 7.0 %copy-start.2 = (bf16[16,8,16,128]{3,2,1,0:T(8,128)(2,1)}, bf16[16,8,16,128]{3,2,1,0:T(8,128)(2,1)S(1)}, u32[]{:S(2)}) copy-start(bf16[16,8,16,128]{3,2,1,0:T(8,128)(2,1)S(1)} %copy.95) | copy-start | bytes 1572868
  13.9 2.7 copy-start.5
  16.6 291.1 %all-gather.8.cloned.1.call-start = ((), (), s32[]{:S(2)}) async-start(), calls=%async_computation.1 | async-start | bytes 17825792 | tf_op jit(solution)/shard_map/all_gather | solution.py:17
  179.8 0.8 copy-start
  191.6 1.5 copy-start.4
  307.7 62.8 %copy-start.3 = (bf16[16,8,16,128]{3,2,1,0:T(8,128)(2,1)S(1)}, bf16[16,8,16,128]{3,2,1,0:T(8,128)(2,1)}, u32[]{:S(2)}) copy-start(bf16[16,8,16,128]{3,2,1,0:T(8,128)(2,1)} %copy-done.2) | copy-start | bytes 1572868
  319.4 52.1 %copy-start.1 = (bf16[1,128,16,128]{1,3,2,0:T(8,128)(2,1)S(1)}, bf16[1,128,16,128]{1,3,2,0:T(8,128)(2,1)}, u32[]{:S(2)}) copy-start(bf16[1,128,16,128]{1,3,2,0:T(8,128)(2,1)} %copy-done) | copy-start | bytes 1572868
Sparse Core Ops, SparseCore 0:
  16.7 105.0 all-gather.5
  182.3 103.7 all-gather.7
where the time goes:
time: 386 us; the launch traced here: 383 us
  blocking collectives  206 us (53%)
  other arithmetic  96 us (25%)
  local copies, waits for them, and re-layouts  49.2 us (13%)
  matrix products  16.1 us (4%)
  between operations  15.6 us (4%)
    unnamed x3, blocking collectives  153 us
    select_n x30, other arithmetic, hop(): jnp.where(position < mine, new, old)  83.2 us
    psum x1, blocking collectives, shards(): summed = lax.psum(gterm, 'seq')  52.5 us
    dynamic_slice x30, local copies, waits for them, and re-layouts, hop(): longer = join(subtotal, jax.tree.map(lambda part: part[position], pieces))  18 us
    rev x1, local copies, waits for them, and re-layouts, entering(): pieces = jax.tree.map(lambda part: part[::-1], pieces)  11.7 us
    unnamed x25, local copies, waits for them, and re-layouts  10.8 us
  transfers between devices with their start and end apart: 2, of which 0 were waited for; matrix products, arithmetic and copies ran while one was open for 7% of the time, Pallas kernels for 0%

commit v1 on v0

v1 whole, which is shorter than its diff:
```python
import math

import jax
import jax.numpy as jnp
from jax import lax
from jax.experimental import pallas as pl
from jax.experimental.pallas import tpu as pltpu
from jax.sharding import PartitionSpec as P

HEADS = 16
FEAT = 128
TOK = 128
HALF = HEADS // 2
CHIPS = 8
DOCS = 8
EPS = 1e-06
F32 = jnp.float32
BF16 = jnp.bfloat16

VM = pl.BlockSpec(memory_space=pltpu.VMEM)
SM = pl.BlockSpec(memory_space=pltpu.SMEM)


def call(body, outs, n_in, flops=0, nbytes=0, trans=0):
    return pl.pallas_call(
        body,
        out_shape=[jax.ShapeDtypeStruct(s, d) for s, d in outs],
        in_specs=[SM] + [VM] * (n_in - 1),
        out_specs=[VM] * len(outs),
        compiler_params=pltpu.CompilerParams(vmem_limit_bytes=24 * 1024 * 1024),
        cost_estimate=pl.CostEstimate(
            flops=flops, bytes_accessed=nbytes, transcendentals=trans
        ),
    )


def doc_at(starts, p):
    total = jnp.int32(0)
    for j in range(DOCS):
        total = total + (starts[0, j] <= p).astype(jnp.int32)
    return total


def docs_of(starts, pos):
    total = jnp.zeros(pos.shape, jnp.int32)
    for j in range(DOCS):
        total = total + (starts[0, j] <= pos).astype(jnp.int32)
    return total


def place():
    idx = lax.axis_index("seq")
    return idx, lax.rem(idx, 2)


def row_pos(idx):
    return idx * TOK + lax.broadcasted_iota(jnp.int32, (TOK, FEAT), 0)


def enters(starts, idx):
    return docs_of(starts, row_pos(idx)) == doc_at(starts, idx * TOK - 1)


def leaves(starts, idx):
    return docs_of(starts, row_pos(idx)) == doc_at(starts, idx * TOK + TOK - 1)


def mask_of(starts, idx):
    rows = row_pos(idx)
    cols = idx * TOK + lax.broadcasted_iota(jnp.int32, (TOK, TOK), 1)
    return (rows >= cols) & (docs_of(starts, rows) == docs_of(starts, cols))


def carry_of(starts, idx):
    return (doc_at(starts, idx * TOK - 1) == doc_at(starts, idx * TOK + TOK - 1)).astype(F32)


def chip_carry(starts, z):
    first = z * 2 * TOK
    return (doc_at(starts, first - 1) == doc_at(starts, first + 2 * TOK - 1)).astype(F32)


def phi(x):
    return jnp.where(x > 0, x + 1.0, jnp.exp(jnp.minimum(x, 0.0)))


def slope(x):
    return jnp.where(x > 0, 1.0, jnp.exp(jnp.minimum(x, 0.0)))


def dot(a, b, ca, cb):
    return lax.dot_general(a, b, (((ca,), (cb,)), ((), ())), preferred_element_type=F32)


def cols(h):
    return pl.ds(pl.multiple_of(h * FEAT, FEAT), FEAT)


def state_body(starts, k, v, keep, give):
    idx, core = place()
    last = leaves(starts, idx)
    for j in range(HALF):
        for out, side in ((keep, core), (give, 1 - core)):
            at = cols(side * HALF + j)
            kf = jnp.where(last, phi(k[:, at].astype(F32)), 0.0).astype(BF16)
            out[j] = dot(kf, v[:, at], 0, 0)


def join_body(starts, keep, recv, out):
    idx, core = place()
    later = carry_of(starts, idx - core + 1)
    mine = jnp.where(core == 0, later, 1.0)
    theirs = jnp.where(core == 0, 1.0, later)
    for j in range(HALF):
        out[j] = mine * keep[j] + theirs * recv[j]


def join_back_body(starts, keep, recv, out):
    idx, core = place()
    earlier = carry_of(starts, idx - core)
    mine = jnp.where(core == 0, 1.0, earlier)
    theirs = jnp.where(core == 0, earlier, 1.0)
    for j in range(HALF):
        out[j] = mine * keep[j] + theirs * recv[j]


def scan_body(starts, parts, out):
    total = jnp.zeros((FEAT, FEAT), F32)
    for z in range(CHIPS):
        out[z] = total
        if z < CHIPS - 1:
            total = parts[z] + chip_carry(starts, z) * total


def scan_back_body(starts, parts, terms, out):
    total = jnp.zeros((FEAT, FEAT), F32)
    gsum = jnp.broadcast_to(jnp.sum(terms[...], axis=0, keepdims=True), (8, FEAT))
    for z in reversed(range(CHIPS)):
        out[z, :FEAT] = total
        out[z, FEAT:] = gsum
        if z > 0:
            total = parts[z] + chip_carry(starts, z) * total


def give_body(starts, keep, coming, out):
    idx, core = place()
    flag = carry_of(starts, idx - core)
    a = jnp.where(core == 0, 1.0, 0.0)
    b = jnp.where(core == 0, flag, 1.0)
    for j in range(HALF):
        out[j] = a * keep[j] + b * coming[j]


def give_back_body(starts, keep, coming, out):
    idx, core = place()
    flag = carry_of(starts, idx - core + 1)
    a = jnp.where(core == 0, 0.0, 1.0)
    b = jnp.where(core == 0, 1.0, flag)
    gsum = jnp.zeros((8, FEAT), F32)
    for j in range(HALF):
        out[j * FEAT : (j + 1) * FEAT] = a * keep[j] + b * coming[j, :FEAT]
        gsum = gsum + coming[j, FEAT:]
    out[HALF * FEAT :] = gsum


def local_body(starts, q, k, v, qf_out, kf_out, scores_out, intra_out):
    idx, _ = place()
    mask = mask_of(starts, idx)
    for h in range(HEADS):
        at = slice(h * FEAT, (h + 1) * FEAT)
        qf = phi(q[:, at].astype(F32)).astype(BF16)
        kf = phi(k[:, at].astype(F32)).astype(BF16)
        qf_out[:, at] = qf
        kf_out[:, at] = kf
        scores = jnp.where(mask, dot(qf, kf, 1, 1), 0.0).astype(BF16)
        scores_out[:, at] = scores
        intra_out[:, at] = dot(scores, v[:, at], 1, 0)


def norm_body(
    starts, qf, intra, dy, gains, coming, theirs, ready,
    att, dn_out, inb_out, keep, give, terms,
):
    idx, core = place()
    cin = enters(starts, idx)
    flag = carry_of(starts, idx - core)
    a = jnp.where(core == 0, 0.0, 1.0)
    b = jnp.where(core == 0, 1.0, flag)
    for j in range(HALF):
        for side, state in ((core, keep), (1 - core, give)):
            h = side * HALF + j
            at = cols(h)
            incoming = a * theirs[j] + b * coming[j] if state is keep else ready[j]
            inb = incoming.astype(BF16)
            inb_out[h] = inb
            qh = qf[:, at]
            num = intra[:, at] + jnp.where(cin, dot(qh, inb, 1, 0), 0.0)
            recip = lax.rsqrt(jnp.mean(num * num, -1, keepdims=True) + EPS)
            normed = num * recip
            gain = gains[pl.ds(2 * h, 1), :] + gains[pl.ds(2 * h + 1, 1), :]
            att[:, at] = (normed * gain).astype(BF16)
            grad = dy[:, at].astype(F32)
            upper = grad * gain
            mean = jnp.mean(upper * normed, -1, keepdims=True)
            dn = (recip * upper - normed * recip * mean).astype(BF16)
            dn_out[:, at] = dn
            term = jnp.sum(grad * normed, axis=0, keepdims=True)
            terms[pl.ds(2 * h, 1), :] = term
            terms[pl.ds(2 * h + 1, 1), :] = term
            masked = jnp.where(cin, dn, jnp.zeros_like(dn))
            state[j] = dot(qh, masked, 0, 0)


def grads_body(starts, q, v, qf, kf, scores, dn, inb, dq_out, dk_part, dv_part):
    idx, _ = place()
    mask = mask_of(starts, idx)
    cin = enters(starts, idx)
    for h in range(HEADS):
        at = slice(h * FEAT, (h + 1) * FEAT)
        dnh = dn[:, at]
        dscores = jnp.where(mask, dot(dnh, v[:, at], 1, 1), 0.0).astype(BF16)
        dq = dot(dscores, kf[:, at], 1, 0) + jnp.where(cin, dot(dnh, inb[h], 1, 1), 0.0)
        dq_out[:, at] = (dq * slope(q[:, at].astype(F32))).astype(BF16)
        dk_part[:, at] = dot(dscores, qf[:, at], 0, 0)
        dv_part[:, at] = dot(scores[:, at], dnh, 0, 0)


def last_body(
    starts, k, v, kf, dk_part, dv_part, theirs, coming, ready,
    dk_out, dv_out, gain_out,
):
    idx, core = place()
    last = leaves(starts, idx)
    flag = carry_of(starts, idx - core + 1)
    a = jnp.where(core == 0, 1.0, 0.0)
    b = jnp.where(core == 0, flag, 1.0)
    gsum = ready[HALF * FEAT :]
    for j in range(HALF):
        gsum = gsum + coming[j, FEAT:]
        for mine, side in ((True, core), (False, 1 - core)):
            at = cols(side * HALF + j)
            if mine:
                outgoing = a * theirs[j] + b * coming[j, :FEAT]
            else:
                outgoing = ready[j * FEAT : (j + 1) * FEAT]
            outb = outgoing.astype(BF16)
            dk = dk_part[:, at] + jnp.where(last, dot(v[:, at], outb, 1, 1), 0.0)
            dk_out[:, at] = (dk * slope(k[:, at].astype(F32))).astype(BF16)
            dv = dv_part[:, at] + jnp.where(last, dot(kf[:, at], outb, 1, 0), 0.0)
            dv_out[:, at] = dv.astype(BF16)
    half = lax.rem(lax.axis_index("dp"), 2)
    total = gsum[:1] * (1.0 / math.sqrt(32 * 2048))
    gain_out[...] = jnp.where(half == 0, total[:, :64], total[:, 64:])


def shards(queries, key_rows, value_rows, out_grad, norm_gain, doc_starts):
    q, k, v, dy = (a.reshape(TOK, HEADS * FEAT) for a in (queries, key_rows, value_rows, out_grad))
    starts = doc_starts
    swap = [(i, i ^ 1) for i in range(2 * CHIPS)]
    zgroups = [[2 * z + c for z in range(CHIPS)] for c in range(2)]
    wide = (TOK, HEADS * FEAT)
    half_states = (HALF, FEAT, FEAT)
    mm = 2 * TOK * FEAT * FEAT

    def other(x):
        return lax.ppermute(x, "seq", swap)

    def across(x):
        return lax.all_to_all(x, "seq", 0, 0, axis_index_groups=zgroups, tiled=True)

    parity = lax.rem(lax.axis_index("dp"), 2)
    row = jnp.where(
        jnp.arange(FEAT) // 64 == parity, jnp.concatenate([norm_gain, norm_gain]), 0.0
    )
    gains = lax.all_to_all(jnp.broadcast_to(row[None], (32, FEAT)), "dp", 0, 0, tiled=True)

    keep1, give1 = call(
        state_body, [(half_states, F32)] * 2, 3, 16 * mm, 2 << 20, 1 << 18
    )(starts, k, v)
    recv1 = other(give1)
    (chip,) = call(join_body, [(half_states, F32)], 3, 1 << 18, 3 << 19)(starts, keep1, recv1)
    parts = across(chip)
    qf, kf, scores, intra = call(
        local_body, [(wide, BF16)] * 3 + [(wide, F32)], 4, 32 * mm, 4 << 20, 1 << 19
    )(starts, q, k, v)
    (prefix,) = call(scan_body, [(half_states, F32)], 2, 1 << 18, 1 << 20)(starts, parts)
    coming = across(prefix)
    (send2,) = call(give_body, [(half_states, F32)], 3, 1 << 18, 3 << 19)(starts, keep1, coming)
    ready = other(send2)
    att, dn, inb, keep3, give3, terms = call(
        norm_body,
        [(wide, BF16), (wide, BF16), ((HEADS, FEAT, FEAT), BF16)]
        + [(half_states, F32)] * 2
        + [((32, FEAT), F32)],
        8, 32 * mm, 5 << 20, 1 << 15,
    )(starts, qf, intra, dy, gains, coming, recv1, ready)
    gathered = lax.all_to_all(terms, "dp", 0, 0, tiled=True)
    recv3 = other(give3)
    (chip3,) = call(join_back_body, [(half_states, F32)], 3, 1 << 18, 3 << 19)(starts, keep3, recv3)
    parts3 = across(chip3)
    dq, dk_part, dv_part = call(
        grads_body, [(wide, BF16), (wide, F32), (wide, F32)], 8, 80 * mm, 7 << 20, 1 << 18
    )(starts, q, v, qf, kf, scores, dn, inb)
    (suffix,) = call(
        scan_back_body, [((CHIPS, FEAT + 8, FEAT), F32)], 3, 1 << 18, 1 << 20
    )(starts, parts3, gathered)
    coming4 = across(suffix)
    (send4,) = call(
        give_back_body, [((HALF * FEAT + 8, FEAT), F32)], 3, 1 << 18, 3 << 19
    )(starts, keep3, coming4)
    ready4 = other(send4)
    dk, dv, gain_grad = call(
        last_body, [(wide, BF16)] * 2 + [((1, 64), F32)], 9, 32 * mm, 5 << 20, 1 << 18
    )(starts, k, v, kf, dk_part, dv_part, recv3, coming4, ready4)
    full = (1, TOK, HEADS * FEAT)
    return (
        att.reshape(full),
        dq.reshape(full),
        dk.reshape(full),
        dv.reshape(full),
        gain_grad.reshape(64),
    )


def solution(mesh):
    rows = P("dp", "seq", None)
    return jax.shard_map(
        shards,
        mesh=mesh,
        in_specs=(rows, rows, rows, rows, P("dp"), P("dp", None)),
        out_specs=(rows, rows, rows, rows, P("dp")),
        check_vma=False,
    )
```

time: 386 us -> 158 us (0.41)
  blocking collectives: 206 us -> 74.4 us
  other arithmetic: 96 us -> 0.08 us
  starting transfers between devices: 0.08 us -> 38.8 us
  local copies, waits for them, and re-layouts: 49.2 us -> 11.6 us
  Pallas kernels: 0 us -> 19.4 us
  matrix products: 16.1 us -> 0 us
  between operations: 15.6 us -> 0.85 us
  waiting for transfers between devices: 0.04 us -> 12.3 us
    unnamed x3 -> x0, blocking collectives: 153 us -> none
    select_n x32 -> x1, other arithmetic: 88.1 us -> 0.08 us  [shards(): jnp.where(jnp.arange(FEAT) // 64 == parity, jnp.concatenate([norm_gain, n...]
    all_to_all x0 -> x4, blocking collectives: none -> 74.4 us  [across(): return lax.all_to_all(x, 'seq', 0, 0, axis_index_groups=zgroups, tiled=True)]
    psum x1 -> x0, blocking collectives: 52.5 us -> none  [shards(): summed = lax.psum(gterm, 'seq')]
    ppermute x0 -> x4, starting transfers between devices: none -> 23.5 us  [other(): return lax.ppermute(x, 'seq', swap)]
    pallas_call x0 -> x11, Pallas kernels: none -> 19.4 us  [the longest x1 4.82 us: shards(): call(grads_body, [(wide, BF16), (wide, F32), (wide, F32)], 8, 80 * mm, 7...]
    dynamic_slice x30 -> x0, local copies, waits for them, and re-layouts: 18 us -> none  [hop(): longer = join(subtotal, jax.tree.map(lambda part: part[position], pieces))]
    dot_general x12 -> x0, matrix products: 16.1 us -> none  [the longest x1 2.36 us: shards(): jnp.einsum('bthf,bshf->bhts', qb, kb, preferred_element_type=jnp.float32)]
  transfers between devices with their start and end apart: 2 -> 6, of which waited for: 0 -> 3; matrix products, arithmetic and copies ran while one was open for 7% -> 0% of each run, Pallas kernels for 0% -> 5%
where the time goes in v1:
time: 158 us; the launch traced here: 157 us
  blocking collectives  74.4 us (47%)
  starting transfers between devices  38.8 us (25%)
  Pallas kernels  19.4 us (12%)
  waiting for transfers between devices  12.3 us (8%)
  local copies, waits for them, and re-layouts  11.6 us (7%)
    all_to_all x4, blocking collectives, across(): return lax.all_to_all(x, 'seq', 0, 0, axis_index_groups=zgroups, tiled=True)  74.4 us
    ppermute x4, starting transfers between devices, other(): return lax.ppermute(x, 'seq', swap)  23.5 us
    unnamed x40, local copies, waits for them, and re-layouts  10.9 us
    all_to_all x1, starting transfers between devices, shards(): lax.all_to_all(jnp.broadcast_to(row[None], (32, FEAT)), 'dp', 0, 0, tiled...  9.67 us
    all_to_all x1, waiting for transfers between devices, shards(): gathered = lax.all_to_all(terms, 'dp', 0, 0, tiled=True)  7.98 us
    all_to_all x1, starting transfers between devices, shards(): gathered = lax.all_to_all(terms, 'dp', 0, 0, tiled=True)  5.58 us
    pallas_call x1, Pallas kernels, shards(): call(grads_body, [(wide, BF16), (wide, F32), (wide, F32)], 8, 80 * mm, 7...  4.82 us
    pallas_call x1, Pallas kernels, shards(): call(norm_body, [(wide, BF16), (wide, BF16), ((HEADS, FEAT, FEAT), BF16)]...  3.26 us
  transfers between devices with their start and end apart: 6, of which 3 were waited for; matrix products, arithmetic and copies ran while one was open for 0% of the time, Pallas kernels for 5%

profile of v1, /device:TPU:1, one launch (start us, length us, event | category | flops | bytes accessed | tf_op | source)
XLA Modules:
  0.0 157.4 jit_solution(2892517302484209286)
XLA Ops:
  0.6 0.6 copy-done.18
  1.3 1.0 copy-done
  2.3 1.0 copy-done.2
  3.4 1.1 shard_map.102
  4.5 8.8 %collective-permute-start = (f32[8,128,128]{2,1,0:T(8,128)S(1)}, f32[8,128,128]{2,1,0:T(8,128)S(1)}, u32[]{:S(2)}, u32[]{:S(2)}) collective-permute-start(f32[8,128,128]{2,1,0:T(8,128)S(1)} %get-tuple-element.26), channel_id=1, source_target_pairs={{0,1},{1,0},{2,3},{3,2},{4,5},{5,4},{6,7},{7,6},{8,9},{9,8},{10,11... | collective-permute-start | bytes 1572872 | tf_op jit(solution)/shard_map/ppermute | solution.py:266
  13.3 1.5 collective-permute-done.recv.theirs
  15.5 21.1 %all_to_all.39.parts = f32[8,128,128]{2,1,0:T(8,128)S(1)} all-to-all(f32[8,128,128]{2,1,0:T(8,128)S(1)} %shard_map.103), channel_id=1, replica_groups={{0,2,4,6,8,10,12,14},{1,3,5,7,9,11,13,15},{16,18,20,22,24,26,28,30},{17..., dimensions={0} | all-to-all | bytes 1048576 | tf_op jit(solution)/shard_map/all_to_all | solution.py:269
  37.3 17.3 %all_to_all.40.coming = f32[8,128,128]{2,1,0:T(8,128)S(1)} all-to-all(f32[8,128,128]{2,1,0:T(8,128)S(1)} %shard_map.104), channel_id=1, replica_groups={{0,2,4,6,8,10,12,14},{1,3,5,7,9,11,13,15},{16,18,20,22,24,26,28,30},{17..., dimensions={0} | all-to-all | bytes 1048576 | tf_op jit(solution)/shard_map/all_to_all | solution.py:269
  54.5 1.4 shard_map.105
  56.0 5.5 %collective-permute-start.1 = (f32[8,128,128]{2,1,0:T(8,128)}, f32[8,128,128]{2,1,0:T(8,128)}, u32[]{:S(2)}, u32[]{:S(2)}) collective-permute-start(f32[8,128,128]{2,1,0:T(8,128)} %shard_map.105), channel_id=1, source_target_pairs={{0,1},{1,0},{2,3},{3,2},{4,5},{5,4},{6,7},{7,6},{8,9},{9,8},{10,11... | collective-permute-start | bytes 1572872 | tf_op jit(solution)/shard_map/ppermute | solution.py:266
  61.5 0.6 copy-done.19
  62.8 9.7 %all-to-all-start = ((f32[32,1,128]{2,1,0:T(1,128)}), f32[32,1,128]{2,1,0:T(1,128)S(1)}, u32[]{:S(2)}, u32[]{:S(2)}) async-start(f32[32,1,128]{2,1,0:T(1,128)} %broadcast_in_dim.11), calls=%async_computation | async-start | bytes 32768 | tf_op jit(solution)/shard_map/all_to_all | solution.py:275
  72.5 3.1 %shard_map.101 = (bf16[128,2048]{1,0:T(8,128)(2,1)S(1)}, bf16[128,2048]{1,0:T(8,128)(2,1)S(1)}, bf16[128,2048]{1,0:T(8,128)(2,1)S(1)}, f32[128,2048]{1,0:T(8,128)S(1)}) custom-call(s32[1,8]{1,0:T(1,128)S(1)} %copy-done.18, bf16[128,2048]{1,0:T(8,128)(2,1)S(1)} %bitcast.21, bf16[128,2048]{1,0:T(8,128)(2,1)S(1)} %bitcast.19, bf16[128,2048]{1,0:T(8,128)(2,1)S(1)} %bitcast.15), custom_call_target="tpu_custom_call" | custom-call | flops 134217728 | bytes 4194304 | tf_op jit(solution)/shard_map/pallas_call | solution.py:283
  75.7 0.8 copy-done.6
  76.4 1.0 copy-done.9
  77.5 0.8 copy-done.12
  78.3 2.8 %all-to-all-done = f32[32,1,128]{2,1,0:T(1,128)S(1)} async-done(((f32[32,1,128]{2,1,0:T(1,128)}), f32[32,1,128]{2,1,0:T(1,128)S(1)}, u32[]{:S(2)}, u32[]{:S(2)}) %all-to-all-start) | async-done | bytes 16416 | tf_op jit(solution)/shard_map/all_to_all | solution.py:275
  81.1 1.0 copy-done.7
  82.1 1.2 copy-done.10
  83.3 1.0 copy-done.11
  84.4 3.3 %shard_map.106 = (bf16[128,2048]{1,0:T(8,128)(2,1)}, bf16[128,2048]{1,0:T(8,128)(2,1)S(1)}, bf16[16,128,128]{2,1,0:T(8,128)(2,1)S(1)}, f32[8,128,128]{2,1,0:T(8,...) custom-call(s32[1,8]{1,0:T(1,128)S(1)} %copy-done.18, bf16[128,2048]{1,0:T(8,128)(2,1)S(1)} %copy-done.7, ...), custom_call_target="tpu_custom_call" | custom-call | flops 134217728 | bytes 5242880 | tf_op jit(solution)/shard_map/pallas_call | solution.py:290
  87.6 0.8 copy-done.14
  88.4 0.8 copy-done.16
  89.2 3.3 %collective-permute-start.2 = (f32[8,128,128]{2,1,0:T(8,128)}, f32[8,128,128]{2,1,0:T(8,128)S(1)}, u32[]{:S(2)}, u32[]{:S(2)}) collective-permute-start(f32[8,128,128]{2,1,0:T(8,128)} %get-tuple-element.35), channel_id=1, source_target_pairs={{0,1},{1,0},{2,3},{3,2},{4,5},{5,4},{6,7},{7,6},{8,9},{9,8},{10,11... | collective-permute-start | bytes 1572872 | tf_op jit(solution)/shard_map/ppermute | solution.py:266
  92.6 5.6 %all-to-all-start.4 = ((f32[32,1,128]{2,1,0:T(1,128)}), f32[32,1,128]{2,1,0:T(1,128)S(1)}, u32[]{:S(2)}, u32[]{:S(2)}) async-start(f32[32,1,128]{2,1,0:T(1,128)} %bitcast.8), calls=%async_computation.4 | async-start | bytes 32768 | tf_op jit(solution)/shard_map/all_to_all | solution.py:297
  98.8 8.0 %all-to-all-done.4 = f32[32,1,128]{2,1,0:T(1,128)S(1)} async-done(((f32[32,1,128]{2,1,0:T(1,128)}), f32[32,1,128]{2,1,0:T(1,128)S(1)}, u32[]{:S(2)}, u32[]{:S(2)}) %all-to-all-start.4) | async-done | bytes 16416 | tf_op jit(solution)/shard_map/all_to_all | solution.py:297
  106.8 17.8 %all_to_all.41.parts = f32[8,128,128]{2,1,0:T(8,128)S(1)} all-to-all(f32[8,128,128]{2,1,0:T(8,128)S(1)} %shard_map.108), channel_id=1, replica_groups={{0,2,4,6,8,10,12,14},{1,3,5,7,9,11,13,15},{16,18,20,22,24,26,28,30},{17..., dimensions={0} | all-to-all | bytes 1048576 | tf_op jit(solution)/shard_map/all_to_all | solution.py:269
  125.2 18.2 %all_to_all.42.coming = f32[8,136,128]{2,1,0:T(8,128)S(1)} all-to-all(f32[8,136,128]{2,1,0:T(8,128)S(1)} %shard_map.109), channel_id=1, replica_groups={{0,2,4,6,8,10,12,14},{1,3,5,7,9,11,13,15},{16,18,20,22,24,26,28,30},{17..., dimensions={0} | all-to-all | bytes 1114112 | tf_op jit(solution)/shard_map/all_to_all | solution.py:269
  143.5 0.6 shard_map.110
  144.1 5.9 %collective-permute-start.3 = (f32[1032,128]{1,0:T(8,128)S(1)}, f32[1032,128]{1,0:T(8,128)S(1)}, u32[]{:S(2)}, u32[]{:S(2)}) collective-permute-start(f32[1032,128]{1,0:T(8,128)S(1)} %shard_map.110), channel_id=1, source_target_pairs={{0,1},{1,0},{2,3},{3,2},{4,5},{5,4},{6,7},{7,6},{8,9},{9,8},{10,11... | collective-permute-start | bytes 1585160 | tf_op jit(solution)/shard_map/ppermute | solution.py:266
  150.1 4.8 %shard_map.107 = (bf16[128,2048]{1,0:T(8,128)(2,1)}, f32[128,2048]{1,0:T(8,128)S(1)}, f32[128,2048]{1,0:T(8,128)S(1)}) custom-call(s32[1,8]{1,0:T(1,128)S(1)} %copy-done.18, bf16[128,2048]{1,0:T(8,128)(2,1)S(1)} %bitcast.22, bf16[128,2048]{1,0:T(8,128)(2,1)S(1)} %bitcast.16, bf16[128,2048]{1,0:T(8,128)(2,1)S(1)} %copy-done.8, ...), custom_call_target="tpu_custom_call" | custom-call | flops 335544320 | bytes 7340032 | tf_op jit(solution)/shard_map/pallas_call | solution.py:301
  154.9 2.5 %shard_map.111 = (bf16[128,2048]{1,0:T(8,128)(2,1)}, bf16[128,2048]{1,0:T(8,128)(2,1)}, f32[1,64]{1,0:T(1,128)}) custom-call(s32[1,8]{1,0:T(1,128)S(1)} %copy-done.18, bf16[128,2048]{1,0:T(8,128)(2,1)S(1)} %bitcast.20, bf16[128,2048]{1,0:T(8,128)(2,1)S(1)} %bitcast.17, bf16[128,2048]{1,0:T(8,128)(2,1)S(1)} %get-tuple-element.28.kf, ...), custom_call_target="tpu_custom_call" | custom-call | flops 134217728 | bytes 5242880 | tf_op jit(solution)/shard_map/pallas_call | solution.py:312
  (37 shorter events, 3.3 us)
Async XLA Ops:
  0.6 0.7 copy-start.18
  1.3 1.0 copy-start
  2.3 1.0 copy-start.2
  4.5 10.3 %collective-permute-start = (f32[8,128,128]{2,1,0:T(8,128)S(1)}, f32[8,128,128]{2,1,0:T(8,128)S(1)}, u32[]{:S(2)}, u32[]{:S(2)}) collective-permute-start(f32[8,128,128]{2,1,0:T(8,128)S(1)} %get-tuple-element.26), channel_id=1, source_target_pairs={{0,1},{1,0},{2,3},{3,2},{4,5},{5,4},{6,7},{7,6},{8,9},{9,8},{10,11... | collective-permute-start | bytes 1572872 | tf_op jit(solution)/shard_map/ppermute | solution.py:266
  54.5 18.0 %copy-start.1 = (bf16[1,128,2048]{2,1,0:T(8,128)(2,1)S(1)}, bf16[1,128,2048]{2,1,0:T(8,128)(2,1)}, u32[]{:S(2)}) copy-start(bf16[1,128,2048]{2,1,0:T(8,128)(2,1)} %param.8) | copy-start | bytes 1572868
  54.5 18.0 %copy-start.3 = (bf16[1,128,2048]{2,1,0:T(8,128)(2,1)S(1)}, bf16[1,128,2048]{2,1,0:T(8,128)(2,1)}, u32[]{:S(2)}) copy-start(bf16[1,128,2048]{2,1,0:T(8,128)(2,1)} %param.7) | copy-start | bytes 1572868
  54.5 18.0 %copy-start.4 = (bf16[1,128,2048]{2,1,0:T(8,128)(2,1)S(1)}, bf16[1,128,2048]{2,1,0:T(8,128)(2,1)}, u32[]{:S(2)}) copy-start(bf16[1,128,2048]{2,1,0:T(8,128)(2,1)} %param.6) | copy-start | bytes 1572868
  56.0 25.1 %collective-permute-start.1 = (f32[8,128,128]{2,1,0:T(8,128)}, f32[8,128,128]{2,1,0:T(8,128)}, u32[]{:S(2)}, u32[]{:S(2)}) collective-permute-start(f32[8,128,128]{2,1,0:T(8,128)} %shard_map.105), channel_id=1, source_target_pairs={{0,1},{1,0},{2,3},{3,2},{4,5},{5,4},{6,7},{7,6},{8,9},{9,8},{10,11... | collective-permute-start | bytes 1572872 | tf_op jit(solution)/shard_map/ppermute | solution.py:266
  61.5 0.7 copy-start.19
  62.8 18.2 %all-to-all-start = ((f32[32,1,128]{2,1,0:T(1,128)}), f32[32,1,128]{2,1,0:T(1,128)S(1)}, u32[]{:S(2)}, u32[]{:S(2)}) async-start(f32[32,1,128]{2,1,0:T(1,128)} %broadcast_in_dim.11), calls=%async_computation | async-start | bytes 32768 | tf_op jit(solution)/shard_map/all_to_all | solution.py:275
  75.6 0.8 copy-start.6
  76.4 1.0 copy-start.9
  77.5 0.8 copy-start.12
  81.1 1.0 copy-start.7
  82.1 1.2 copy-start.10
  83.3 1.0 copy-start.11
  87.6 0.8 copy-start.14
  88.4 0.8 copy-start.16
  89.2 8.9 %collective-permute-start.2 = (f32[8,128,128]{2,1,0:T(8,128)}, f32[8,128,128]{2,1,0:T(8,128)S(1)}, u32[]{:S(2)}, u32[]{:S(2)}) collective-permute-start(f32[8,128,128]{2,1,0:T(8,128)} %get-tuple-element.35), channel_id=1, source_target_pairs={{0,1},{1,0},{2,3},{3,2},{4,5},{5,4},{6,7},{7,6},{8,9},{9,8},{10,11... | collective-permute-start | bytes 1572872 | tf_op jit(solution)/shard_map/ppermute | solution.py:266
  92.6 14.2 %all-to-all-start.4 = ((f32[32,1,128]{2,1,0:T(1,128)}), f32[32,1,128]{2,1,0:T(1,128)S(1)}, u32[]{:S(2)}, u32[]{:S(2)}) async-start(f32[32,1,128]{2,1,0:T(1,128)} %bitcast.8), calls=%async_computation.4 | async-start | bytes 32768 | tf_op jit(solution)/shard_map/all_to_all | solution.py:297
  125.2 24.8 %copy-start.15 = (bf16[128,2048]{1,0:T(8,128)(2,1)S(1)}, bf16[128,2048]{1,0:T(8,128)(2,1)}, u32[]{:S(2)}) copy-start(bf16[128,2048]{1,0:T(8,128)(2,1)} %copy-done.14) | copy-start | bytes 1572868
  125.2 24.8 %copy-start.17 = (bf16[16,128,128]{2,1,0:T(8,128)(2,1)S(1)}, bf16[16,128,128]{2,1,0:T(8,128)(2,1)}, u32[]{:S(2)}) copy-start(bf16[16,128,128]{2,1,0:T(8,128)(2,1)} %copy-done.16) | copy-start | bytes 1572868
  143.5 6.6 %copy-start.5 = (bf16[1,128,2048]{2,1,0:T(8,128)(2,1)S(1)}, bf16[1,128,2048]{2,1,0:T(8,128)(2,1)}, u32[]{:S(2)}) copy-start(bf16[1,128,2048]{2,1,0:T(8,128)(2,1)} %param.6) | copy-start | bytes 1572868
  143.5 6.6 %copy-start.8 = (bf16[128,2048]{1,0:T(8,128)(2,1)S(1)}, bf16[128,2048]{1,0:T(8,128)(2,1)}, u32[]{:S(2)}) copy-start(bf16[128,2048]{1,0:T(8,128)(2,1)} %copy-done.6) | copy-start | bytes 1572868
  143.5 6.6 %copy-start.13 = (bf16[128,2048]{1,0:T(8,128)(2,1)S(1)}, bf16[128,2048]{1,0:T(8,128)(2,1)}, u32[]{:S(2)}) copy-start(bf16[128,2048]{1,0:T(8,128)(2,1)} %copy-done.12) | copy-start | bytes 1572868
  144.1 10.8 %collective-permute-start.3 = (f32[1032,128]{1,0:T(8,128)S(1)}, f32[1032,128]{1,0:T(8,128)S(1)}, u32[]{:S(2)}, u32[]{:S(2)}) collective-permute-start(f32[1032,128]{1,0:T(8,128)S(1)} %shard_map.110), channel_id=1, source_target_pairs={{0,1},{1,0},{2,3},{3,2},{4,5},{5,4},{6,7},{7,6},{8,9},{9,8},{10,11... | collective-permute-start | bytes 1585160 | tf_op jit(solution)/shard_map/ppermute | solution.py:266

commit v2 on v1

--- a/solution.py
+++ b/solution.py
@@ -279,10 +279,12 @@
     )(starts, k, v)
     recv1 = other(give1)
     (chip,) = call(join_body, [(half_states, F32)], 3, 1 << 18, 3 << 19)(starts, keep1, recv1)
+    chip, gains, after = lax.optimization_barrier((chip, gains, starts))
     parts = across(chip)
     qf, kf, scores, intra = call(
         local_body, [(wide, BF16)] * 3 + [(wide, F32)], 4, 32 * mm, 4 << 20, 1 << 19
-    )(starts, q, k, v)
+    )(after, q, k, v)
+    parts, scores = lax.optimization_barrier((parts, scores))
     (prefix,) = call(scan_body, [(half_states, F32)], 2, 1 << 18, 1 << 20)(starts, parts)
     coming = across(prefix)
     (send2,) = call(give_body, [(half_states, F32)], 3, 1 << 18, 3 << 19)(starts, keep1, coming)
@@ -297,10 +299,12 @@
     gathered = lax.all_to_all(terms, "dp", 0, 0, tiled=True)
     recv3 = other(give3)
     (chip3,) = call(join_back_body, [(half_states, F32)], 3, 1 << 18, 3 << 19)(starts, keep3, recv3)
+    chip3, gathered, after3 = lax.optimization_barrier((chip3, gathered, starts))
     parts3 = across(chip3)
     dq, dk_part, dv_part = call(
         grads_body, [(wide, BF16), (wide, F32), (wide, F32)], 8, 80 * mm, 7 << 20, 1 << 18
-    )(starts, q, v, qf, kf, scores, dn, inb)
+    )(after3, q, v, qf, kf, scores, dn, inb)
+    parts3, dk_part = lax.optimization_barrier((parts3, dk_part))
     (suffix,) = call(
         scan_back_body, [((CHIPS, FEAT + 8, FEAT), F32)], 3, 1 << 18, 1 << 20
     )(starts, parts3, gathered)

time: 158 us -> 148 us (0.937)
  blocking collectives: 74.4 us -> 35 us
  waiting for transfers between devices: 12.3 us -> 32.2 us
  starting transfers between devices: 38.8 us -> 44.4 us
  local copies, waits for them, and re-layouts: 11.6 us -> 16.2 us
    all_to_all x4 -> x2, blocking collectives: 74.4 us -> 35 us  [across(): return lax.all_to_all(x, 'seq', 0, 0, axis_index_groups=zgroups, tiled=True)]
    all_to_all x0 -> x2, waiting for transfers between devices: none -> 14.9 us  [across(): return lax.all_to_all(x, 'seq', 0, 0, axis_index_groups=zgroups, tiled=True)]
    all_to_all x0 -> x2, starting transfers between devices: none -> 13.7 us  [across(): return lax.all_to_all(x, 'seq', 0, 0, axis_index_groups=zgroups, tiled=True)]
    all_to_all x1, starting transfers between devices: 9.67 us -> 4.3 us  [shards(): lax.all_to_all(jnp.broadcast_to(row[None], (32, FEAT)), 'dp', 0, 0, tiled...]
    unnamed x40 -> x54, local copies, waits for them, and re-layouts: 10.9 us -> 15.5 us
    all_to_all x1, waiting for transfers between devices: 2.79 us -> 7.1 us  [shards(): lax.all_to_all(jnp.broadcast_to(row[None], (32, FEAT)), 'dp', 0, 0, tiled...]
    all_to_all x1, starting transfers between devices: 5.58 us -> 3.85 us  [shards(): gathered = lax.all_to_all(terms, 'dp', 0, 0, tiled=True)]
  transfers between devices with their start and end apart: 6 -> 8, of which waited for: 3 -> 6; matrix products, arithmetic and copies ran while one was open for 0% -> 0% of each run, Pallas kernels for 5% -> 7%
where the time goes in v2:
time: 148 us; the launch traced here: 147 us
  starting transfers between devices  44.4 us (30%)
  blocking collectives  35 us (24%)
  waiting for transfers between devices  32.2 us (22%)
  Pallas kernels  18.6 us (13%)
  local copies, waits for them, and re-layouts  16.2 us (11%)
    all_to_all x2, blocking collectives, across(): return lax.all_to_all(x, 'seq', 0, 0, axis_index_groups=zgroups, tiled=True)  35 us
    ppermute x4, starting transfers between devices, other(): return lax.ppermute(x, 'seq', swap)  22.6 us
    unnamed x54, local copies, waits for them, and re-layouts  15.5 us
    all_to_all x2, waiting for transfers between devices, across(): return lax.all_to_all(x, 'seq', 0, 0, axis_index_groups=zgroups, tiled=True)  14.9 us
    all_to_all x2, starting transfers between devices, across(): return lax.all_to_all(x, 'seq', 0, 0, axis_index_groups=zgroups, tiled=True)  13.7 us
    all_to_all x1, waiting for transfers between devices, shards(): gathered = lax.all_to_all(terms, 'dp', 0, 0, tiled=True)  7.17 us
    all_to_all x1, waiting for transfers between devices, shards(): lax.all_to_all(jnp.broadcast_to(row[None], (32, FEAT)), 'dp', 0, 0, tiled...  7.1 us
    pallas_call x1, Pallas kernels, shards(): call(grads_body, [(wide, BF16), (wide, F32), (wide, F32)], 8, 80 * mm, 7...  4.78 us
  transfers between devices with their start and end apart: 8, of which 6 were waited for; matrix products, arithmetic and copies ran while one was open for 0% of the time, Pallas kernels for 7%

profile of v2, /device:TPU:1, one launch (start us, length us, event | category | flops | bytes accessed | tf_op | source)
XLA Modules:
  0.0 147.3 jit_solution(12928972871304818860)
XLA Ops:
  1.3 1.0 copy-done
  2.3 1.0 copy-done.2
  3.4 1.1 shard_map.101
  4.5 8.8 %collective-permute-start = (f32[8,128,128]{2,1,0:T(8,128)S(1)}, f32[8,128,128]{2,1,0:T(8,128)S(1)}, u32[]{:S(2)}, u32[]{:S(2)}) collective-permute-start(f32[8,128,128]{2,1,0:T(8,128)S(1)} %get-tuple-element.34), channel_id=1, source_target_pairs={{0,1},{1,0},{2,3},{3,2},{4,5},{5,4},{6,7},{7,6},{8,9},{9,8},{10,11... | collective-permute-start | bytes 1572872 | tf_op jit(solution)/shard_map/ppermute | solution.py:266
  14.7 4.3 %all-to-all-start = ((f32[32,1,128]{2,1,0:T(1,128)}), f32[32,1,128]{2,1,0:T(1,128)S(1)}, u32[]{:S(2)}, u32[]{:S(2)}) async-start(f32[32,1,128]{2,1,0:T(1,128)} %broadcast_in_dim.11), calls=%async_computation | async-start | bytes 32768 | tf_op jit(solution)/shard_map/all_to_all | solution.py:275
  19.0 1.4 shard_map.102
  20.4 7.1 %all-to-all-done = f32[32,1,128]{2,1,0:T(1,128)S(1)} async-done(((f32[32,1,128]{2,1,0:T(1,128)}), f32[32,1,128]{2,1,0:T(1,128)S(1)}, u32[]{:S(2)}, u32[]{:S(2)}) %all-to-all-start) | async-done | bytes 16416 | tf_op jit(solution)/shard_map/all_to_all | solution.py:275
  27.5 10.2 %all-to-all-start.1 = ((f32[8,128,128]{2,1,0:T(8,128)}), f32[8,128,128]{2,1,0:T(8,128)S(1)}, u32[]{:S(2)}, u32[]{:S(2)}) async-start(f32[8,128,128]{2,1,0:T(8,128)} %shard_map.102), calls=%async_computation.1 | async-start | bytes 1048576 | tf_op jit(solution)/shard_map/all_to_all | solution.py:269
  37.7 3.1 %shard_map.103 = (bf16[128,2048]{1,0:T(8,128)(2,1)S(1)}, bf16[128,2048]{1,0:T(8,128)(2,1)S(1)}, bf16[128,2048]{1,0:T(8,128)(2,1)S(1)}, f32[128,2048]{1,0:T(8,128)S(1)}) custom-call(s32[1,8]{1,0:T(1,128)S(1)} %copy-done.25, bf16[128,2048]{1,0:T(8,128)(2,1)S(1)} %bitcast.21, bf16[128,2048]{1,0:T(8,128)(2,1)S(1)} %bitcast.19, bf16[128,2048]{1,0:T(8,128)(2,1)S(1)} %bitcast.15), custom_call_target="tpu_custom_call" | custom-call | flops 134217728 | bytes 4194304 | tf_op jit(solution)/shard_map/pallas_call | solution.py:284
  41.7 1.0 copy-done.16
  43.4 10.2 %all-to-all-done.1.parts = f32[8,128,128]{2,1,0:T(8,128)S(1)} async-done(((f32[8,128,128]{2,1,0:T(8,128)}), f32[8,128,128]{2,1,0:T(8,128)S(1)}, u32[]{:S(2)}, u32[]{:S(2)}) %all-to-all-start.1) | async-done | bytes 524320 | tf_op jit(solution)/shard_map/all_to_all | solution.py:269
  54.3 17.0 %all_to_all.41.coming = f32[8,128,128]{2,1,0:T(8,128)S(1)} all-to-all(f32[8,128,128]{2,1,0:T(8,128)S(1)} %shard_map.104), channel_id=1, replica_groups={{0,2,4,6,8,10,12,14},{1,3,5,7,9,11,13,15},{16,18,20,22,24,26,28,30},{17..., dimensions={0} | all-to-all | bytes 1048576 | tf_op jit(solution)/shard_map/all_to_all | solution.py:269
  72.0 5.9 %collective-permute-start.1 = (f32[8,128,128]{2,1,0:T(8,128)S(1)}, f32[8,128,128]{2,1,0:T(8,128)S(1)}, u32[]{:S(2)}, u32[]{:S(2)}) collective-permute-start(f32[8,128,128]{2,1,0:T(8,128)S(1)} %shard_map.105), channel_id=1, source_target_pairs={{0,1},{1,0},{2,3},{3,2},{4,5},{5,4},{6,7},{7,6},{8,9},{9,8},{10,11... | collective-permute-start | bytes 1572872 | tf_op jit(solution)/shard_map/ppermute | solution.py:266
  77.9 1.5 %collective-permute-done.1.ready = f32[8,128,128]{2,1,0:T(8,128)S(1)} collective-permute-done((f32[8,128,128]{2,1,0:T(8,128)S(1)}, f32[8,128,128]{2,1,0:T(8,128)S(1)}, u32[]{:S(2)}, u32[]{:S(2)}) %collective-permute-start.1) | collective-permute-done | bytes 524320 | tf_op jit(solution)/shard_map/ppermute | solution.py:266
  79.4 2.6 %shard_map.106 = (bf16[128,2048]{1,0:T(8,128)(2,1)}, bf16[128,2048]{1,0:T(8,128)(2,1)S(1)}, bf16[16,128,128]{2,1,0:T(8,128)(2,1)S(1)}, f32[8,128,128]{2,1,0:T(8,...) custom-call(s32[1,8]{1,0:T(1,128)S(1)} %copy-done.25, bf16[128,2048]{1,0:T(8,128)(2,1)S(1)} %copy-done.10, ...), custom_call_target="tpu_custom_call" | custom-call | flops 134217728 | bytes 5242880 | tf_op jit(solution)/shard_map/pallas_call | solution.py:292
  83.5 2.3 %collective-permute-start.2 = (f32[8,128,128]{2,1,0:T(8,128)S(1)}, f32[8,128,128]{2,1,0:T(8,128)S(1)}, u32[]{:S(2)}, u32[]{:S(2)}) collective-permute-start(f32[8,128,128]{2,1,0:T(8,128)S(1)} %get-tuple-element.44), channel_id=1, source_target_pairs={{0,1},{1,0},{2,3},{3,2},{4,5},{5,4},{6,7},{7,6},{8,9},{9,8},{10,11... | collective-permute-start | bytes 1572872 | tf_op jit(solution)/shard_map/ppermute | solution.py:266
  85.8 3.8 %all-to-all-start.3 = ((f32[32,1,128]{2,1,0:T(1,128)}), f32[32,1,128]{2,1,0:T(1,128)S(1)}, u32[]{:S(2)}, u32[]{:S(2)}) async-start(f32[32,1,128]{2,1,0:T(1,128)} %bitcast.7), calls=%async_computation.3 | async-start | bytes 32768 | tf_op jit(solution)/shard_map/all_to_all | solution.py:299
  91.1 7.2 %all-to-all-done.3 = f32[32,1,128]{2,1,0:T(1,128)S(1)} async-done(((f32[32,1,128]{2,1,0:T(1,128)}), f32[32,1,128]{2,1,0:T(1,128)S(1)}, u32[]{:S(2)}, u32[]{:S(2)}) %all-to-all-start.3) | async-done | bytes 16416 | tf_op jit(solution)/shard_map/all_to_all | solution.py:299
  98.3 3.5 %all-to-all-start.4 = ((f32[8,128,128]{2,1,0:T(8,128)}), f32[8,128,128]{2,1,0:T(8,128)S(1)}, u32[]{:S(2)}, u32[]{:S(2)}) async-start(f32[8,128,128]{2,1,0:T(8,128)} %copy-done.4), calls=%async_computation.4 | async-start | bytes 1048576 | tf_op jit(solution)/shard_map/all_to_all | solution.py:269
  101.8 1.0 copy-done.6
  102.8 1.0 copy-done.11
  103.9 1.0 copy-done.20
  104.9 1.0 copy-done.22
  106.0 1.0 copy-done.24
  107.0 4.8 %shard_map.108 = (bf16[128,2048]{1,0:T(8,128)(2,1)}, f32[128,2048]{1,0:T(8,128)S(1)}, f32[128,2048]{1,0:T(8,128)S(1)}) custom-call(s32[1,8]{1,0:T(1,128)S(1)} %copy-done.25, bf16[128,2048]{1,0:T(8,128)(2,1)S(1)} %bitcast.22, bf16[128,2048]{1,0:T(8,128)(2,1)S(1)} %bitcast.16, bf16[128,2048]{1,0:T(8,128)(2,1)S(1)} %copy-done.11, ...), custom_call_target="tpu_custom_call" | custom-call | flops 335544320 | bytes 7340032 | tf_op jit(solution)/shard_map/pallas_call | solution.py:304
  111.8 1.0 copy-done.12
  112.8 1.0 copy-done.14
  113.8 4.7 %all-to-all-done.4.parts = f32[8,128,128]{2,1,0:T(8,128)S(1)} async-done(((f32[8,128,128]{2,1,0:T(8,128)}), f32[8,128,128]{2,1,0:T(8,128)S(1)}, u32[]{:S(2)}, u32[]{:S(2)}) %all-to-all-start.4) | async-done | bytes 524320 | tf_op jit(solution)/shard_map/all_to_all | solution.py:269
  119.1 18.0 %all_to_all.42.coming = f32[8,136,128]{2,1,0:T(8,128)S(1)} all-to-all(f32[8,136,128]{2,1,0:T(8,128)S(1)} %shard_map.109), channel_id=1, replica_groups={{0,2,4,6,8,10,12,14},{1,3,5,7,9,11,13,15},{16,18,20,22,24,26,28,30},{17..., dimensions={0} | all-to-all | bytes 1114112 | tf_op jit(solution)/shard_map/all_to_all | solution.py:269
  137.7 5.6 %collective-permute-start.3 = (f32[1032,128]{1,0:T(8,128)S(1)}, f32[1032,128]{1,0:T(8,128)S(1)}, u32[]{:S(2)}, u32[]{:S(2)}) collective-permute-start(f32[1032,128]{1,0:T(8,128)S(1)} %shard_map.110), channel_id=1, source_target_pairs={{0,1},{1,0},{2,3},{3,2},{4,5},{5,4},{6,7},{7,6},{8,9},{9,8},{10,11... | collective-permute-start | bytes 1585160 | tf_op jit(solution)/shard_map/ppermute | solution.py:266
  143.3 1.5 %collective-permute-done.3.ready = f32[1032,128]{1,0:T(8,128)S(1)} collective-permute-done((f32[1032,128]{1,0:T(8,128)S(1)}, f32[1032,128]{1,0:T(8,128)S(1)}, u32[]{:S(2)}, u32[]{:S(2)}) %collective-permute-start.3) | collective-permute-done | bytes 528416 | tf_op jit(solution)/shard_map/ppermute | solution.py:266
  144.8 2.5 %shard_map.111 = (bf16[128,2048]{1,0:T(8,128)(2,1)}, bf16[128,2048]{1,0:T(8,128)(2,1)}, f32[1,64]{1,0:T(1,128)}) custom-call(s32[1,8]{1,0:T(1,128)S(1)} %copy-done.25, bf16[128,2048]{1,0:T(8,128)(2,1)S(1)} %bitcast.20, bf16[128,2048]{1,0:T(8,128)(2,1)S(1)} %bitcast.17, bf16[128,2048]{1,0:T(8,128)(2,1)S(1)} %get-tuple-element.47.kf, ...), custom_call_target="tpu_custom_call" | custom-call | flops 134217728 | bytes 5242880 | tf_op jit(solution)/shard_map/pallas_call | solution.py:316
  (53 shorter events, 9.2 us)
Async XLA Ops:
  1.3 1.0 copy-start
  2.3 1.0 copy-start.2
  4.5 14.5 %collective-permute-start = (f32[8,128,128]{2,1,0:T(8,128)S(1)}, f32[8,128,128]{2,1,0:T(8,128)S(1)}, u32[]{:S(2)}, u32[]{:S(2)}) collective-permute-start(f32[8,128,128]{2,1,0:T(8,128)S(1)} %get-tuple-element.34), channel_id=1, source_target_pairs={{0,1},{1,0},{2,3},{3,2},{4,5},{5,4},{6,7},{7,6},{8,9},{9,8},{10,11... | collective-permute-start | bytes 1572872 | tf_op jit(solution)/shard_map/ppermute | solution.py:266
  14.7 12.9 %all-to-all-start = ((f32[32,1,128]{2,1,0:T(1,128)}), f32[32,1,128]{2,1,0:T(1,128)S(1)}, u32[]{:S(2)}, u32[]{:S(2)}) async-start(f32[32,1,128]{2,1,0:T(1,128)} %broadcast_in_dim.11), calls=%async_computation | async-start | bytes 32768 | tf_op jit(solution)/shard_map/all_to_all | solution.py:275
  19.0 1.4 copy-start.7
  19.0 18.7 %copy-start.5 = (bf16[1,128,2048]{2,1,0:T(8,128)(2,1)S(1)}, bf16[1,128,2048]{2,1,0:T(8,128)(2,1)}, u32[]{:S(2)}) copy-start(bf16[1,128,2048]{2,1,0:T(8,128)(2,1)} %param.6) | copy-start | bytes 1572868
  27.5 10.2 %copy-start.1 = (bf16[1,128,2048]{2,1,0:T(8,128)(2,1)S(1)}, bf16[1,128,2048]{2,1,0:T(8,128)(2,1)}, u32[]{:S(2)}) copy-start(bf16[1,128,2048]{2,1,0:T(8,128)(2,1)} %param.8) | copy-start | bytes 1572868
  27.5 10.2 %copy-start.3 = (bf16[1,128,2048]{2,1,0:T(8,128)(2,1)S(1)}, bf16[1,128,2048]{2,1,0:T(8,128)(2,1)}, u32[]{:S(2)}) copy-start(bf16[1,128,2048]{2,1,0:T(8,128)(2,1)} %param.7) | copy-start | bytes 1572868
  27.5 26.1 %all-to-all-start.1 = ((f32[8,128,128]{2,1,0:T(8,128)}), f32[8,128,128]{2,1,0:T(8,128)S(1)}, u32[]{:S(2)}, u32[]{:S(2)}) async-start(f32[8,128,128]{2,1,0:T(8,128)} %shard_map.102), calls=%async_computation.1 | async-start | bytes 1048576 | tf_op jit(solution)/shard_map/all_to_all | solution.py:269
  40.9 0.8 copy-start.9
  41.7 1.0 copy-start.16
  42.7 0.8 copy-start.19
  54.3 25.1 %copy-start.17 = (f32[128,2048]{1,0:T(8,128)S(1)}, f32[128,2048]{1,0:T(8,128)}, u32[]{:S(2)}) copy-start(f32[128,2048]{1,0:T(8,128)} %copy-done.16) | copy-start | bytes 3145732
  71.3 8.1 %copy-start.8 = (f32[8,128,128]{2,1,0:T(8,128)S(1)}, f32[8,128,128]{2,1,0:T(8,128)}, u32[]{:S(2)}) copy-start(f32[8,128,128]{2,1,0:T(8,128)} %copy-done.7) | copy-start | bytes 1572868
  71.3 8.1 %copy-start.10 = (bf16[128,2048]{1,0:T(8,128)(2,1)S(1)}, bf16[128,2048]{1,0:T(8,128)(2,1)}, u32[]{:S(2)}) copy-start(bf16[128,2048]{1,0:T(8,128)(2,1)} %copy-done.9) | copy-start | bytes 1572868
  71.3 8.1 %copy-start.18 = (bf16[1,128,2048]{2,1,0:T(8,128)(2,1)S(1)}, bf16[1,128,2048]{2,1,0:T(8,128)(2,1)}, u32[]{:S(2)}) copy-start(bf16[1,128,2048]{2,1,0:T(8,128)(2,1)} %param.9) | copy-start | bytes 1572868
  72.0 7.4 %collective-permute-start.1 = (f32[8,128,128]{2,1,0:T(8,128)S(1)}, f32[8,128,128]{2,1,0:T(8,128)S(1)}, u32[]{:S(2)}, u32[]{:S(2)}) collective-permute-start(f32[8,128,128]{2,1,0:T(8,128)S(1)} %shard_map.105), channel_id=1, source_target_pairs={{0,1},{1,0},{2,3},{3,2},{4,5},{5,4},{6,7},{7,6},{8,9},{9,8},{10,11... | collective-permute-start | bytes 1572872 | tf_op jit(solution)/shard_map/ppermute | solution.py:266
  82.0 0.8 copy-start.21
  83.5 6.1 %collective-permute-start.2 = (f32[8,128,128]{2,1,0:T(8,128)S(1)}, f32[8,128,128]{2,1,0:T(8,128)S(1)}, u32[]{:S(2)}, u32[]{:S(2)}) collective-permute-start(f32[8,128,128]{2,1,0:T(8,128)S(1)} %get-tuple-element.44), channel_id=1, source_target_pairs={{0,1},{1,0},{2,3},{3,2},{4,5},{5,4},{6,7},{7,6},{8,9},{9,8},{10,11... | collective-permute-start | bytes 1572872 | tf_op jit(solution)/shard_map/ppermute | solution.py:266
  85.8 12.5 %all-to-all-start.3 = ((f32[32,1,128]{2,1,0:T(1,128)}), f32[32,1,128]{2,1,0:T(1,128)S(1)}, u32[]{:S(2)}, u32[]{:S(2)}) async-start(f32[32,1,128]{2,1,0:T(1,128)} %bitcast.7), calls=%async_computation.3 | async-start | bytes 32768 | tf_op jit(solution)/shard_map/all_to_all | solution.py:299
  90.3 0.8 copy-start.4
  98.3 20.1 %all-to-all-start.4 = ((f32[8,128,128]{2,1,0:T(8,128)}), f32[8,128,128]{2,1,0:T(8,128)S(1)}, u32[]{:S(2)}, u32[]{:S(2)}) async-start(f32[8,128,128]{2,1,0:T(8,128)} %copy-done.4), calls=%async_computation.4 | async-start | bytes 1048576 | tf_op jit(solution)/shard_map/all_to_all | solution.py:269
  101.8 1.0 copy-start.6
  102.8 1.0 copy-start.11
  103.9 1.0 copy-start.20
  104.9 1.0 copy-start.22
  106.0 1.0 copy-start.24
  111.8 1.0 copy-start.12
  112.8 1.0 copy-start.14
  119.1 25.7 %copy-start.15 = (f32[128,2048]{1,0:T(8,128)S(1)}, f32[128,2048]{1,0:T(8,128)}, u32[]{:S(2)}) copy-start(f32[128,2048]{1,0:T(8,128)} %copy-done.14) | copy-start | bytes 3145732
  137.0 7.8 %copy-start.13 = (f32[128,2048]{1,0:T(8,128)S(1)}, f32[128,2048]{1,0:T(8,128)}, u32[]{:S(2)}) copy-start(f32[128,2048]{1,0:T(8,128)} %copy-done.12) | copy-start | bytes 3145732
  137.7 7.1 %collective-permute-start.3 = (f32[1032,128]{1,0:T(8,128)S(1)}, f32[1032,128]{1,0:T(8,128)S(1)}, u32[]{:S(2)}, u32[]{:S(2)}) collective-permute-start(f32[1032,128]{1,0:T(8,128)S(1)} %shard_map.110), channel_id=1, source_target_pairs={{0,1},{1,0},{2,3},{3,2},{4,5},{5,4},{6,7},{7,6},{8,9},{9,8},{10,11... | collective-permute-start | bytes 1585160 | tf_op jit(solution)/shard_map/ppermute | solution.py:266
  (3 other events, 2.1 us)

commit v3 on v2

--- a/solution.py
+++ b/solution.py
@@ -21,12 +21,13 @@
 SM = pl.BlockSpec(memory_space=pltpu.SMEM)
 
 
-def call(body, outs, n_in, flops=0, nbytes=0, trans=0):
+def call(body, outs, n_in, flops=0, nbytes=0, trans=0, scratch=()):
     return pl.pallas_call(
         body,
         out_shape=[jax.ShapeDtypeStruct(s, d) for s, d in outs],
         in_specs=[SM] + [VM] * (n_in - 1),
         out_specs=[VM] * len(outs),
+        scratch_shapes=scratch,
         compiler_params=pltpu.CompilerParams(vmem_limit_bytes=24 * 1024 * 1024),
         cost_estimate=pl.CostEstimate(
             flops=flops, bytes_accessed=nbytes, transcendentals=trans
@@ -124,10 +125,11 @@
         out[j] = mine * keep[j] + theirs * recv[j]
 
 
-def scan_body(starts, parts, out):
+def scan_body(starts, parts, gain_rows, out):
     total = jnp.zeros((FEAT, FEAT), F32)
     for z in range(CHIPS):
-        out[z] = total
+        out[z, :FEAT] = total
+        out[z, FEAT:] = gain_rows[...]
         if z < CHIPS - 1:
             total = parts[z] + chip_carry(starts, z) * total
 
@@ -148,7 +150,8 @@
     a = jnp.where(core == 0, 1.0, 0.0)
     b = jnp.where(core == 0, flag, 1.0)
     for j in range(HALF):
-        out[j] = a * keep[j] + b * coming[j]
+        out[j * FEAT : (j + 1) * FEAT] = a * keep[j] + b * coming[j, :FEAT]
+        out[HALF * FEAT + 8 * j : HALF * FEAT + 8 * j + 8] = coming[j, FEAT:]
 
 
 def give_back_body(starts, keep, coming, out):
@@ -178,10 +181,14 @@
 
 
 def norm_body(
-    starts, qf, intra, dy, gains, coming, theirs, ready,
-    att, dn_out, inb_out, keep, give, terms,
+    starts, qf, intra, dy, coming, theirs, ready,
+    att, dn_out, inb_out, keep, give, terms, gains,
 ):
     idx, core = place()
+    y = lax.rem(lax.axis_index("dp"), CHIPS)
+    for j in range(CHIPS):
+        at = HALF * FEAT + 8 * j
+        gains[8 * j : 8 * j + 8, :] = coming[j, FEAT:] + ready[at : at + 8]
     cin = enters(starts, idx)
     flag = carry_of(starts, idx - core)
     a = jnp.where(core == 0, 0.0, 1.0)
@@ -190,14 +197,19 @@
         for side, state in ((core, keep), (1 - core, give)):
             h = side * HALF + j
             at = cols(h)
-            incoming = a * theirs[j] + b * coming[j] if state is keep else ready[j]
+            if state is keep:
+                incoming = a * theirs[j] + b * coming[j, :FEAT]
+            else:
+                incoming = ready[j * FEAT : (j + 1) * FEAT]
             inb = incoming.astype(BF16)
             inb_out[h] = inb
             qh = qf[:, at]
             num = intra[:, at] + jnp.where(cin, dot(qh, inb, 1, 0), 0.0)
             recip = lax.rsqrt(jnp.mean(num * num, -1, keepdims=True) + EPS)
             normed = num * recip
-            gain = gains[pl.ds(2 * h, 1), :] + gains[pl.ds(2 * h + 1, 1), :]
+            even = lax.rem(2 * lax.rem(h, 4) - y + CHIPS, CHIPS)
+            odd = lax.rem(2 * lax.rem(h, 4) + 1 - y + CHIPS, CHIPS)
+            gain = gains[pl.ds(8 * even + h // 4, 1), :] + gains[pl.ds(8 * odd + h // 4, 1), :]
             att[:, at] = (normed * gain).astype(BF16)
             grad = dy[:, at].astype(F32)
             upper = grad * gain
@@ -268,34 +280,45 @@
     def across(x):
         return lax.all_to_all(x, "seq", 0, 0, axis_index_groups=zgroups, tiled=True)
 
-    parity = lax.rem(lax.axis_index("dp"), 2)
+    part = lax.axis_index("dp")
     row = jnp.where(
-        jnp.arange(FEAT) // 64 == parity, jnp.concatenate([norm_gain, norm_gain]), 0.0
+        (jnp.arange(8)[:, None] == part // CHIPS) & (jnp.arange(FEAT)[None] // 64 == part % 2),
+        jnp.concatenate([norm_gain, norm_gain])[None],
+        0.0,
     )
-    gains = lax.all_to_all(jnp.broadcast_to(row[None], (32, FEAT)), "dp", 0, 0, tiled=True)
+    row = row + lax.ppermute(row, "dp", [(i, i ^ CHIPS) for i in range(4 * CHIPS)])
+    shifted = [
+        ((((x ^ (2 * c)) * CHIPS + (y + z) % CHIPS) * CHIPS + z) * 2 + c, ((x * CHIPS + y) * CHIPS + z) * 2 + c)
+        for x in range(4) for y in range(CHIPS) for z in range(CHIPS) for c in range(2)
+    ]
+    gain_rows = lax.ppermute(row, ("dp", "seq"), shifted)
 
     keep1, give1 = call(
         state_body, [(half_states, F32)] * 2, 3, 16 * mm, 2 << 20, 1 << 18
     )(starts, k, v)
     recv1 = other(give1)
     (chip,) = call(join_body, [(half_states, F32)], 3, 1 << 18, 3 << 19)(starts, keep1, recv1)
-    chip, gains, after = lax.optimization_barrier((chip, gains, starts))
     parts = across(chip)
+    (prefix,) = call(
+        scan_body, [((CHIPS, FEAT + 8, FEAT), F32)], 3, 1 << 18, 1 << 20
+    )(starts, parts, gain_rows)
+    prefix, after = lax.optimization_barrier((prefix, starts))
+    coming = across(prefix)
     qf, kf, scores, intra = call(
         local_body, [(wide, BF16)] * 3 + [(wide, F32)], 4, 32 * mm, 4 << 20, 1 << 19
     )(after, q, k, v)
-    parts, scores = lax.optimization_barrier((parts, scores))
-    (prefix,) = call(scan_body, [(half_states, F32)], 2, 1 << 18, 1 << 20)(starts, parts)
-    coming = across(prefix)
-    (send2,) = call(give_body, [(half_states, F32)], 3, 1 << 18, 3 << 19)(starts, keep1, coming)
+    coming, scores = lax.optimization_barrier((coming, scores))
+    (send2,) = call(
+        give_body, [((HALF * FEAT + 64, FEAT), F32)], 3, 1 << 18, 3 << 19
+    )(starts, keep1, coming)
     ready = other(send2)
     att, dn, inb, keep3, give3, terms = call(
         norm_body,
         [(wide, BF16), (wide, BF16), ((HEADS, FEAT, FEAT), BF16)]
         + [(half_states, F32)] * 2
         + [((32, FEAT), F32)],
-        8, 32 * mm, 5 << 20, 1 << 15,
-    )(starts, qf, intra, dy, gains, coming, recv1, ready)
+        7, 32 * mm, 5 << 20, 1 << 15, scratch=[pltpu.VMEM((64, FEAT), F32)],
+    )(starts, qf, intra, dy, coming, recv1, ready)
     gathered = lax.all_to_all(terms, "dp", 0, 0, tiled=True)
     recv3 = other(give3)
     (chip3,) = call(join_back_body, [(half_states, F32)], 3, 1 << 18, 3 << 19)(starts, keep3, recv3)

time: 148 us -> 147 us (level)
  blocking collectives: 35 us -> 17.8 us
  waiting for transfers between devices: 32.2 us -> 38 us
  starting transfers between devices: 44.4 us -> 49.8 us
  local copies, waits for them, and re-layouts: 16.2 us -> 19.4 us
    all_to_all x2 -> x1, blocking collectives: 35 us -> 17.8 us  [across(): return lax.all_to_all(x, 'seq', 0, 0, axis_index_groups=zgroups, tiled=True)]
    all_to_all x2 -> x3, waiting for transfers between devices: 14.9 us -> 23.2 us  [across(): return lax.all_to_all(x, 'seq', 0, 0, axis_index_groups=zgroups, tiled=True)]
    ppermute x0 -> x2, starting transfers between devices: none -> 7.75 us  [the longest x1 4.64 us: shards(): gain_rows = lax.ppermute(row, ('dp', 'seq'), shifted)]
    all_to_all x1 -> x0, waiting for transfers between devices: 7.1 us -> none  [shards(): lax.all_to_all(jnp.broadcast_to(row[None], (32, FEAT)), 'dp', 0, 0, tiled...]
    all_to_all x1, starting transfers between devices: 3.85 us -> 9.41 us  [shards(): gathered = lax.all_to_all(terms, 'dp', 0, 0, tiled=True)]
    all_to_all x1 -> x0, starting transfers between devices: 4.3 us -> none  [shards(): lax.all_to_all(jnp.broadcast_to(row[None], (32, FEAT)), 'dp', 0, 0, tiled...]
    unnamed x54 -> x58, local copies, waits for them, and re-layouts: 15.5 us -> 19.4 us
    ppermute x4, starting transfers between devices: 22.6 us -> 19.2 us  [other(): return lax.ppermute(x, 'seq', swap)]
  transfers between devices with their start and end apart: 8 -> 10, of which waited for: 6 -> 9; matrix products, arithmetic and copies ran while one was open for 0% -> 0% of each run, Pallas kernels for 7% -> 6%
where the time goes in v3:
time: 147 us; the launch traced here: 146 us
  starting transfers between devices  49.8 us (34%)
  waiting for transfers between devices  38 us (26%)
  Pallas kernels  19.7 us (13%)
  local copies, waits for them, and re-layouts  19.4 us (13%)
  blocking collectives  17.8 us (12%)
    all_to_all x3, waiting for transfers between devices, across(): return lax.all_to_all(x, 'seq', 0, 0, axis_index_groups=zgroups, tiled=True)  23.2 us
    unnamed x58, local copies, waits for them, and re-layouts  19.4 us
    ppermute x4, starting transfers between devices, other(): return lax.ppermute(x, 'seq', swap)  19.2 us
    all_to_all x1, blocking collectives, across(): return lax.all_to_all(x, 'seq', 0, 0, axis_index_groups=zgroups, tiled=True)  17.8 us
    all_to_all x3, starting transfers between devices, across(): return lax.all_to_all(x, 'seq', 0, 0, axis_index_groups=zgroups, tiled=True)  13.4 us
    all_to_all x1, starting transfers between devices, shards(): gathered = lax.all_to_all(terms, 'dp', 0, 0, tiled=True)  9.41 us
    all_to_all x1, waiting for transfers between devices, shards(): gathered = lax.all_to_all(terms, 'dp', 0, 0, tiled=True)  7.2 us
    pallas_call x1, Pallas kernels, shards(): call(grads_body, [(wide, BF16), (wide, F32), (wide, F32)], 8, 80 * mm, 7...  4.78 us
  transfers between devices with their start and end apart: 10, of which 9 were waited for; matrix products, arithmetic and copies ran while one was open for 0% of the time, Pallas kernels for 6%

profile of v3, /device:TPU:1, one launch (start us, length us, event | category | flops | bytes accessed | tf_op | source)
XLA Modules:
  0.0 145.9 jit_solution(7620474720387914446)
XLA Ops:
  1.3 1.0 copy-done
  2.3 1.0 copy-done.2
  3.4 1.1 shard_map.101
  4.5 8.8 %collective-permute-start = (f32[8,128,128]{2,1,0:T(8,128)S(1)}, f32[8,128,128]{2,1,0:T(8,128)S(1)}, u32[]{:S(2)}, u32[]{:S(2)}) collective-permute-start(f32[8,128,128]{2,1,0:T(8,128)S(1)} %get-tuple-element.33), channel_id=1, source_target_pairs={{0,1},{1,0},{2,3},{3,2},{4,5},{5,4},{6,7},{7,6},{8,9},{9,8},{10,11... | collective-permute-start | bytes 1572872 | tf_op jit(solution)/shard_map/ppermute | solution.py:278
  13.3 1.5 %collective-permute-done.recv.theirs = f32[8,128,128]{2,1,0:T(8,128)S(1)} collective-permute-done((f32[8,128,128]{2,1,0:T(8,128)S(1)}, f32[8,128,128]{2,1,0:T(8,128)S(1)}, u32[]{:S(2)}, u32[]{:S(2)}) %collective-permute-start) | collective-permute-done | bytes 524320 | tf_op jit(solution)/shard_map/ppermute | solution.py:278
  14.8 1.5 %shard_map.102 = f32[8,128,128]{2,1,0:T(8,128)} custom-call(s32[1,8]{1,0:T(1,128)S(1)} %copy-done.27, f32[8,128,128]{2,1,0:T(8,128)S(1)} %get-tuple-element.32.keep, f32[8,128,128]{2,1,0:T(8,128)S(1)} %collective-permute-done.recv.theirs), custom_call_target="tpu_custom_call" | custom-call | flops 262144 | bytes 1572864 | tf_op jit(solution)/shard_map/pallas_call | solution.py:300
  17.1 4.7 %all-to-all-start = ((f32[8,128,128]{2,1,0:T(8,128)}), f32[8,128,128]{2,1,0:T(8,128)S(1)}, u32[]{:S(2)}, u32[]{:S(2)}) async-start(f32[8,128,128]{2,1,0:T(8,128)} %shard_map.102), calls=%async_computation | async-start | bytes 1048576 | tf_op jit(solution)/shard_map/all_to_all | solution.py:281
  22.6 3.1 %collective-permute-start.1 = (f32[8,128]{1,0:T(8,128)S(1)}, f32[8,128]{1,0:T(8,128)S(1)}, u32[]{:S(2)}, u32[]{:S(2)}) collective-permute-start(f32[8,128]{1,0:T(8,128)S(1)} %and_select_fusion), channel_id=1, source_target_pairs={{0,128},{16,144},{32,160},{48,176},{64,192},{80,208},{96,224},{112... | collective-permute-start | bytes 12296 | tf_op jit(solution)/shard_map/ppermute | solution.py:289
  25.7 1.5 %collective-permute-done.1 = f32[8,128]{1,0:T(8,128)S(1)} collective-permute-done((f32[8,128]{1,0:T(8,128)S(1)}, f32[8,128]{1,0:T(8,128)S(1)}, u32[]{:S(2)}, u32[]{:S(2)}) %collective-permute-start.1) | collective-permute-done | bytes 4128 | tf_op jit(solution)/shard_map/ppermute | solution.py:289
  27.3 4.6 %collective-permute-start.2 = (f32[8,128]{1,0:T(8,128)S(1)}, f32[8,128]{1,0:T(8,128)S(1)}, u32[]{:S(2)}, u32[]{:S(2)}) collective-permute-start(f32[8,128]{1,0:T(8,128)S(1)} %fusion.1), channel_id=1, source_target_pairs={{0,0},{257,1},{18,2},{275,3},{36,4},{293,5},{54,6},{311,7},{72,8},... | collective-permute-start | bytes 12296 | tf_op jit(solution)/shard_map/ppermute | solution.py:294
  31.9 1.5 %collective-permute-done.2.gain_rows = f32[8,128]{1,0:T(8,128)S(1)} collective-permute-done((f32[8,128]{1,0:T(8,128)S(1)}, f32[8,128]{1,0:T(8,128)S(1)}, u32[]{:S(2)}, u32[]{:S(2)}) %collective-permute-start.2) | collective-permute-done | bytes 4128 | tf_op jit(solution)/shard_map/ppermute | solution.py:294
  33.4 6.3 %all-to-all-done.parts = f32[8,128,128]{2,1,0:T(8,128)S(1)} async-done(((f32[8,128,128]{2,1,0:T(8,128)}), f32[8,128,128]{2,1,0:T(8,128)S(1)}, u32[]{:S(2)}, u32[]{:S(2)}) %all-to-all-start) | async-done | bytes 524320 | tf_op jit(solution)/shard_map/all_to_all | solution.py:281
  39.7 1.5 %shard_map.103 = f32[8,136,128]{2,1,0:T(8,128)} custom-call(s32[1,8]{1,0:T(1,128)S(1)} %copy-done.27, f32[8,128,128]{2,1,0:T(8,128)S(1)} %all-to-all-done.parts, f32[8,128]{1,0:T(8,128)S(1)} %collective-permute-done.2.gain_rows), custom_call_target="tpu_custom_call" | custom-call | flops 262144 | bytes 1048576 | tf_op jit(solution)/shard_map/pallas_call | solution.py:302
  41.2 5.3 %all-to-all-start.1 = ((f32[8,136,128]{2,1,0:T(8,128)}), f32[8,136,128]{2,1,0:T(8,128)S(1)}, u32[]{:S(2)}, u32[]{:S(2)}) async-start(f32[8,136,128]{2,1,0:T(8,128)} %shard_map.103), calls=%async_computation.1 | async-start | bytes 1114112 | tf_op jit(solution)/shard_map/all_to_all | solution.py:281
  46.5 3.1 %shard_map.104 = (bf16[128,2048]{1,0:T(8,128)(2,1)S(1)}, bf16[128,2048]{1,0:T(8,128)(2,1)S(1)}, bf16[128,2048]{1,0:T(8,128)(2,1)S(1)}, f32[128,2048]{1,0:T(8,128)S(1)}) custom-call(s32[1,8]{1,0:T(1,128)S(1)} %copy-done.27, bf16[128,2048]{1,0:T(8,128)(2,1)S(1)} %bitcast.20, bf16[128,2048]{1,0:T(8,128)(2,1)S(1)} %bitcast.18, bf16[128,2048]{1,0:T(8,128)(2,1)S(1)} %bitcast.14), custom_call_target="tpu_custom_call" | custom-call | flops 134217728 | bytes 4194304 | tf_op jit(solution)/shard_map/pallas_call | solution.py:307
  52.2 12.9 %all-to-all-done.1.coming = f32[8,136,128]{2,1,0:T(8,128)S(1)} async-done(((f32[8,136,128]{2,1,0:T(8,128)}), f32[8,136,128]{2,1,0:T(8,128)S(1)}, u32[]{:S(2)}, u32[]{:S(2)}) %all-to-all-start.1) | async-done | bytes 557088 | tf_op jit(solution)/shard_map/all_to_all | solution.py:281
  65.8 2.4 %collective-permute-start.3 = (f32[1088,128]{1,0:T(8,128)S(1)}, f32[1088,128]{1,0:T(8,128)S(1)}, u32[]{:S(2)}, u32[]{:S(2)}) collective-permute-start(f32[1088,128]{1,0:T(8,128)S(1)} %shard_map.105), channel_id=1, source_target_pairs={{0,1},{1,0},{2,3},{3,2},{4,5},{5,4},{6,7},{7,6},{8,9},{9,8},{10,11... | collective-permute-start | bytes 1671176 | tf_op jit(solution)/shard_map/ppermute | solution.py:278
  68.2 1.6 %collective-permute-done.3.ready = f32[1088,128]{1,0:T(8,128)S(1)} collective-permute-done((f32[1088,128]{1,0:T(8,128)S(1)}, f32[1088,128]{1,0:T(8,128)S(1)}, u32[]{:S(2)}, u32[]{:S(2)}) %collective-permute-start.3) | collective-permute-done | bytes 557088 | tf_op jit(solution)/shard_map/ppermute | solution.py:278
  69.7 1.2 copy-done.19
  71.0 2.8 %shard_map.106 = (bf16[128,2048]{1,0:T(8,128)(2,1)}, bf16[128,2048]{1,0:T(8,128)(2,1)S(1)}, bf16[16,128,128]{2,1,0:T(8,128)(2,1)S(1)}, f32[8,128,128]{2,1,0:T(8,...) custom-call(s32[1,8]{1,0:T(1,128)S(1)} %copy-done.27, bf16[128,2048]{1,0:T(8,128)(2,1)S(1)} %copy-done.12, ...), custom_call_target="tpu_custom_call" | custom-call | flops 134217728 | bytes 5242880 | tf_op jit(solution)/shard_map/pallas_call | solution.py:315
  75.4 2.3 %collective-permute-start.4 = (f32[8,128,128]{2,1,0:T(8,128)}, f32[8,128,128]{2,1,0:T(8,128)S(1)}, u32[]{:S(2)}, u32[]{:S(2)}) collective-permute-start(f32[8,128,128]{2,1,0:T(8,128)} %get-tuple-element.42), channel_id=1, source_target_pairs={{0,1},{1,0},{2,3},{3,2},{4,5},{5,4},{6,7},{7,6},{8,9},{9,8},{10,11... | collective-permute-start | bytes 1572872 | tf_op jit(solution)/shard_map/ppermute | solution.py:278
  77.6 9.4 %all-to-all-start.2 = ((f32[32,1,128]{2,1,0:T(1,128)}), f32[32,1,128]{2,1,0:T(1,128)S(1)}, u32[]{:S(2)}, u32[]{:S(2)}) async-start(f32[32,1,128]{2,1,0:T(1,128)} %bitcast.6), calls=%async_computation.2 | async-start | bytes 32768 | tf_op jit(solution)/shard_map/all_to_all | solution.py:322
  88.5 7.2 %all-to-all-done.2 = f32[32,1,128]{2,1,0:T(1,128)S(1)} async-done(((f32[32,1,128]{2,1,0:T(1,128)}), f32[32,1,128]{2,1,0:T(1,128)S(1)}, u32[]{:S(2)}, u32[]{:S(2)}) %all-to-all-start.2) | async-done | bytes 16416 | tf_op jit(solution)/shard_map/all_to_all | solution.py:322
  95.7 3.5 %all-to-all-start.3 = ((f32[8,128,128]{2,1,0:T(8,128)}), f32[8,128,128]{2,1,0:T(8,128)S(1)}, u32[]{:S(2)}, u32[]{:S(2)}) async-start(f32[8,128,128]{2,1,0:T(8,128)} %copy-done.6), calls=%async_computation.3 | async-start | bytes 1048576 | tf_op jit(solution)/shard_map/all_to_all | solution.py:281
  100.3 1.0 copy-done.13
  101.3 1.0 copy-done.22
  104.4 4.8 %shard_map.108 = (bf16[128,2048]{1,0:T(8,128)(2,1)}, f32[128,2048]{1,0:T(8,128)S(1)}, f32[128,2048]{1,0:T(8,128)S(1)}) custom-call(s32[1,8]{1,0:T(1,128)S(1)} %copy-done.27, bf16[128,2048]{1,0:T(8,128)(2,1)S(1)} %bitcast.21, bf16[128,2048]{1,0:T(8,128)(2,1)S(1)} %bitcast.15, bf16[128,2048]{1,0:T(8,128)(2,1)S(1)} %copy-done.13, ...), custom_call_target="tpu_custom_call" | custom-call | flops 335544320 | bytes 7340032 | tf_op jit(solution)/shard_map/pallas_call | solution.py:327
  111.2 4.0 %all-to-all-done.3.parts = f32[8,128,128]{2,1,0:T(8,128)S(1)} async-done(((f32[8,128,128]{2,1,0:T(8,128)}), f32[8,128,128]{2,1,0:T(8,128)S(1)}, u32[]{:S(2)}, u32[]{:S(2)}) %all-to-all-start.3) | async-done | bytes 524320 | tf_op jit(solution)/shard_map/all_to_all | solution.py:281
  117.7 17.8 %all_to_all.32.coming = f32[8,136,128]{2,1,0:T(8,128)S(1)} all-to-all(f32[8,136,128]{2,1,0:T(8,128)S(1)} %shard_map.109), channel_id=1, replica_groups={{0,2,4,6,8,10,12,14},{1,3,5,7,9,11,13,15},{16,18,20,22,24,26,28,30},{17..., dimensions={0} | all-to-all | bytes 1114112 | tf_op jit(solution)/shard_map/all_to_all | solution.py:281
  136.1 5.8 %collective-permute-start.5 = (f32[1032,128]{1,0:T(8,128)S(1)}, f32[1032,128]{1,0:T(8,128)S(1)}, u32[]{:S(2)}, u32[]{:S(2)}) collective-permute-start(f32[1032,128]{1,0:T(8,128)S(1)} %shard_map.110), channel_id=1, source_target_pairs={{0,1},{1,0},{2,3},{3,2},{4,5},{5,4},{6,7},{7,6},{8,9},{9,8},{10,11... | collective-permute-start | bytes 1585160 | tf_op jit(solution)/shard_map/ppermute | solution.py:278
  141.9 1.5 %collective-permute-done.5.ready = f32[1032,128]{1,0:T(8,128)S(1)} collective-permute-done((f32[1032,128]{1,0:T(8,128)S(1)}, f32[1032,128]{1,0:T(8,128)S(1)}, u32[]{:S(2)}, u32[]{:S(2)}) %collective-permute-start.5) | collective-permute-done | bytes 528416 | tf_op jit(solution)/shard_map/ppermute | solution.py:278
  143.4 2.5 %shard_map.111 = (bf16[128,2048]{1,0:T(8,128)(2,1)}, bf16[128,2048]{1,0:T(8,128)(2,1)}, f32[1,64]{1,0:T(1,128)}) custom-call(s32[1,8]{1,0:T(1,128)S(1)} %copy-done.27, bf16[128,2048]{1,0:T(8,128)(2,1)S(1)} %bitcast.19, bf16[128,2048]{1,0:T(8,128)(2,1)S(1)} %bitcast.16, bf16[128,2048]{1,0:T(8,128)(2,1)S(1)} %get-tuple-element.45.kf, ...), custom_call_target="tpu_custom_call" | custom-call | flops 134217728 | bytes 5242880 | tf_op jit(solution)/shard_map/pallas_call | solution.py:339
  (63 shorter events, 16.8 us)
Async XLA Ops:
  1.3 1.0 copy-start
  2.3 1.0 copy-start.2
  4.5 10.3 %collective-permute-start = (f32[8,128,128]{2,1,0:T(8,128)S(1)}, f32[8,128,128]{2,1,0:T(8,128)S(1)}, u32[]{:S(2)}, u32[]{:S(2)}) collective-permute-start(f32[8,128,128]{2,1,0:T(8,128)S(1)} %get-tuple-element.33), channel_id=1, source_target_pairs={{0,1},{1,0},{2,3},{3,2},{4,5},{5,4},{6,7},{7,6},{8,9},{9,8},{10,11... | collective-permute-start | bytes 1572872 | tf_op jit(solution)/shard_map/ppermute | solution.py:278
  17.1 22.6 %all-to-all-start = ((f32[8,128,128]{2,1,0:T(8,128)}), f32[8,128,128]{2,1,0:T(8,128)S(1)}, u32[]{:S(2)}, u32[]{:S(2)}) async-start(f32[8,128,128]{2,1,0:T(8,128)} %shard_map.102), calls=%async_computation | async-start | bytes 1048576 | tf_op jit(solution)/shard_map/all_to_all | solution.py:281
  22.6 4.6 %collective-permute-start.1 = (f32[8,128]{1,0:T(8,128)S(1)}, f32[8,128]{1,0:T(8,128)S(1)}, u32[]{:S(2)}, u32[]{:S(2)}) collective-permute-start(f32[8,128]{1,0:T(8,128)S(1)} %and_select_fusion), channel_id=1, source_target_pairs={{0,128},{16,144},{32,160},{48,176},{64,192},{80,208},{96,224},{112... | collective-permute-start | bytes 12296 | tf_op jit(solution)/shard_map/ppermute | solution.py:289
  27.3 6.1 %collective-permute-start.2 = (f32[8,128]{1,0:T(8,128)S(1)}, f32[8,128]{1,0:T(8,128)S(1)}, u32[]{:S(2)}, u32[]{:S(2)}) collective-permute-start(f32[8,128]{1,0:T(8,128)S(1)} %fusion.1), channel_id=1, source_target_pairs={{0,0},{257,1},{18,2},{275,3},{36,4},{293,5},{54,6},{311,7},{72,8},... | collective-permute-start | bytes 12296 | tf_op jit(solution)/shard_map/ppermute | solution.py:294
  39.7 6.7 %copy-start.7 = (bf16[1,128,2048]{2,1,0:T(8,128)(2,1)S(1)}, bf16[1,128,2048]{2,1,0:T(8,128)(2,1)}, u32[]{:S(2)}) copy-start(bf16[1,128,2048]{2,1,0:T(8,128)(2,1)} %param.6) | copy-start | bytes 1572868
  41.2 5.3 %copy-start.1 = (bf16[1,128,2048]{2,1,0:T(8,128)(2,1)S(1)}, bf16[1,128,2048]{2,1,0:T(8,128)(2,1)}, u32[]{:S(2)}) copy-start(bf16[1,128,2048]{2,1,0:T(8,128)(2,1)} %param.8) | copy-start | bytes 1572868
  41.2 5.3 %copy-start.3 = (bf16[1,128,2048]{2,1,0:T(8,128)(2,1)S(1)}, bf16[1,128,2048]{2,1,0:T(8,128)(2,1)}, u32[]{:S(2)}) copy-start(bf16[1,128,2048]{2,1,0:T(8,128)(2,1)} %param.7) | copy-start | bytes 1572868
  41.2 23.9 %all-to-all-start.1 = ((f32[8,136,128]{2,1,0:T(8,128)}), f32[8,136,128]{2,1,0:T(8,128)S(1)}, u32[]{:S(2)}, u32[]{:S(2)}) async-start(f32[8,136,128]{2,1,0:T(8,128)} %shard_map.103), calls=%async_computation.1 | async-start | bytes 1114112 | tf_op jit(solution)/shard_map/all_to_all | solution.py:281
  50.4 1.0 copy-start.18
  65.1 4.6 %copy-start.10 = (f32[8,128,128]{2,1,0:T(8,128)S(1)}, f32[8,128,128]{2,1,0:T(8,128)}, u32[]{:S(2)}) copy-start(f32[8,128,128]{2,1,0:T(8,128)} %copy-done.9) | copy-start | bytes 1572868
  65.1 4.6 %copy-start.12 = (bf16[128,2048]{1,0:T(8,128)(2,1)S(1)}, bf16[128,2048]{1,0:T(8,128)(2,1)}, u32[]{:S(2)}) copy-start(bf16[128,2048]{1,0:T(8,128)(2,1)} %copy-done.11) | copy-start | bytes 1572868
  65.1 4.6 %copy-start.20 = (bf16[1,128,2048]{2,1,0:T(8,128)(2,1)S(1)}, bf16[1,128,2048]{2,1,0:T(8,128)(2,1)}, u32[]{:S(2)}) copy-start(bf16[1,128,2048]{2,1,0:T(8,128)(2,1)} %param.9) | copy-start | bytes 1572868
  65.8 4.0 %collective-permute-start.3 = (f32[1088,128]{1,0:T(8,128)S(1)}, f32[1088,128]{1,0:T(8,128)S(1)}, u32[]{:S(2)}, u32[]{:S(2)}) collective-permute-start(f32[1088,128]{1,0:T(8,128)S(1)} %shard_map.105), channel_id=1, source_target_pairs={{0,1},{1,0},{2,3},{3,2},{4,5},{5,4},{6,7},{7,6},{8,9},{9,8},{10,11... | collective-permute-start | bytes 1671176 | tf_op jit(solution)/shard_map/ppermute | solution.py:278
  69.7 1.2 copy-start.19
  73.7 0.8 copy-start.23
  74.5 0.8 copy-start.25
  75.4 11.7 %collective-permute-start.4 = (f32[8,128,128]{2,1,0:T(8,128)}, f32[8,128,128]{2,1,0:T(8,128)S(1)}, u32[]{:S(2)}, u32[]{:S(2)}) collective-permute-start(f32[8,128,128]{2,1,0:T(8,128)} %get-tuple-element.42), channel_id=1, source_target_pairs={{0,1},{1,0},{2,3},{3,2},{4,5},{5,4},{6,7},{7,6},{8,9},{9,8},{10,11... | collective-permute-start | bytes 1572872 | tf_op jit(solution)/shard_map/ppermute | solution.py:278
  77.6 18.1 %all-to-all-start.2 = ((f32[32,1,128]{2,1,0:T(1,128)}), f32[32,1,128]{2,1,0:T(1,128)S(1)}, u32[]{:S(2)}, u32[]{:S(2)}) async-start(f32[32,1,128]{2,1,0:T(1,128)} %bitcast.6), calls=%async_computation.2 | async-start | bytes 32768 | tf_op jit(solution)/shard_map/all_to_all | solution.py:322
  95.7 19.5 %all-to-all-start.3 = ((f32[8,128,128]{2,1,0:T(8,128)}), f32[8,128,128]{2,1,0:T(8,128)S(1)}, u32[]{:S(2)}, u32[]{:S(2)}) async-start(f32[8,128,128]{2,1,0:T(8,128)} %copy-done.6), calls=%async_computation.3 | async-start | bytes 1048576 | tf_op jit(solution)/shard_map/all_to_all | solution.py:281
  99.2 1.0 copy-start.8
  100.3 1.0 copy-start.13
  101.3 1.0 copy-start.22
  102.3 1.0 copy-start.24
  103.4 1.0 copy-start.26
  109.2 1.0 copy-start.14
  110.2 1.0 copy-start.16
  116.0 1.0 copy-start.5
  117.7 25.8 %copy-start.17 = (f32[128,2048]{1,0:T(8,128)S(1)}, f32[128,2048]{1,0:T(8,128)}, u32[]{:S(2)}) copy-start(f32[128,2048]{1,0:T(8,128)} %copy-done.16) | copy-start | bytes 3145732
  135.5 7.9 %copy-start.15 = (f32[128,2048]{1,0:T(8,128)S(1)}, f32[128,2048]{1,0:T(8,128)}, u32[]{:S(2)}) copy-start(f32[128,2048]{1,0:T(8,128)} %copy-done.14) | copy-start | bytes 3145732
  136.1 7.3 %collective-permute-start.5 = (f32[1032,128]{1,0:T(8,128)S(1)}, f32[1032,128]{1,0:T(8,128)S(1)}, u32[]{:S(2)}, u32[]{:S(2)}) collective-permute-start(f32[1032,128]{1,0:T(8,128)S(1)} %shard_map.110), channel_id=1, source_target_pairs={{0,1},{1,0},{2,3},{3,2},{4,5},{5,4},{6,7},{7,6},{8,9},{9,8},{10,11... | collective-permute-start | bytes 1585160 | tf_op jit(solution)/shard_map/ppermute | solution.py:278
  (7 other events, 5.3 us)

commit v4 on v3

--- a/solution.py
+++ b/solution.py
@@ -19,14 +19,15 @@
 
 VM = pl.BlockSpec(memory_space=pltpu.VMEM)
 SM = pl.BlockSpec(memory_space=pltpu.SMEM)
-
-
-def call(body, outs, n_in, flops=0, nbytes=0, trans=0, scratch=()):
+HB = pl.BlockSpec(memory_space=pltpu.HBM)
+
+
+def call(body, outs, n_in, flops=0, nbytes=0, trans=0, far=False, scratch=()):
     return pl.pallas_call(
         body,
-        out_shape=[jax.ShapeDtypeStruct(s, d) for s, d in outs],
+        out_shape=[pltpu.HBM(s, d) if far else jax.ShapeDtypeStruct(s, d) for s, d in outs],
         in_specs=[SM] + [VM] * (n_in - 1),
-        out_specs=[VM] * len(outs),
+        out_specs=[HB if far else VM] * len(outs),
         scratch_shapes=scratch,
         compiler_params=pltpu.CompilerParams(vmem_limit_bytes=24 * 1024 * 1024),
         cost_estimate=pl.CostEstimate(
@@ -166,18 +167,33 @@
     out[HALF * FEAT :] = gsum
 
 
-def local_body(starts, q, k, v, qf_out, kf_out, scores_out, intra_out):
+def local_body(
+    starts, q, k, v, qf_out, kf_out, scores_out, intra_out,
+    qf_buf, kf_buf, scores_buf, intra_buf, sems,
+):
     idx, _ = place()
     mask = mask_of(starts, idx)
+    pairs = (
+        (qf_buf, qf_out), (kf_buf, kf_out), (scores_buf, scores_out), (intra_buf, intra_out),
+    )
+    copies = []
     for h in range(HEADS):
         at = slice(h * FEAT, (h + 1) * FEAT)
         qf = phi(q[:, at].astype(F32)).astype(BF16)
         kf = phi(k[:, at].astype(F32)).astype(BF16)
-        qf_out[:, at] = qf
-        kf_out[:, at] = kf
+        qf_buf[:, at] = qf
+        kf_buf[:, at] = kf
         scores = jnp.where(mask, dot(qf, kf, 1, 1), 0.0).astype(BF16)
-        scores_out[:, at] = scores
-        intra_out[:, at] = dot(scores, v[:, at], 1, 0)
+        scores_buf[:, at] = scores
+        intra_buf[:, at] = dot(scores, v[:, at], 1, 0)
+        if h % 4 == 3:
+            group = pl.ds((h - 3) * FEAT, 4 * FEAT)
+            for n, (buf, out) in enumerate(pairs):
+                c = pltpu.make_async_copy(buf.at[:, group], out.at[:, group], sems.at[h - 3 + n])
+                c.start()
+                copies.append(c)
+    for c in copies:
+        c.wait()
 
 
 def norm_body(
@@ -287,27 +303,27 @@
         0.0,
     )
     row = row + lax.ppermute(row, "dp", [(i, i ^ CHIPS) for i in range(4 * CHIPS)])
+    keep1, give1 = call(
+        state_body, [(half_states, F32)] * 2, 3, 16 * mm, 2 << 20, 1 << 18
+    )(starts, k, v)
+    recv1 = other(give1)
+    (chip,) = call(join_body, [(half_states, F32)], 3, 1 << 18, 3 << 19)(starts, keep1, recv1)
+    chip, row, after = lax.optimization_barrier((chip, row, starts))
+    parts = across(chip)
     shifted = [
         ((((x ^ (2 * c)) * CHIPS + (y + z) % CHIPS) * CHIPS + z) * 2 + c, ((x * CHIPS + y) * CHIPS + z) * 2 + c)
         for x in range(4) for y in range(CHIPS) for z in range(CHIPS) for c in range(2)
     ]
     gain_rows = lax.ppermute(row, ("dp", "seq"), shifted)
-
-    keep1, give1 = call(
-        state_body, [(half_states, F32)] * 2, 3, 16 * mm, 2 << 20, 1 << 18
-    )(starts, k, v)
-    recv1 = other(give1)
-    (chip,) = call(join_body, [(half_states, F32)], 3, 1 << 18, 3 << 19)(starts, keep1, recv1)
-    parts = across(chip)
+    qf, kf, scores, intra = call(
+        local_body, [(wide, BF16)] * 3 + [(wide, F32)], 4, 32 * mm, 4 << 20, 1 << 19, far=True,
+        scratch=[pltpu.VMEM(wide, BF16)] * 3 + [pltpu.VMEM(wide, F32), pltpu.SemaphoreType.DMA((16,))],
+    )(after, q, k, v)
+    parts, scores = lax.optimization_barrier((parts, scores))
     (prefix,) = call(
         scan_body, [((CHIPS, FEAT + 8, FEAT), F32)], 3, 1 << 18, 1 << 20
     )(starts, parts, gain_rows)
-    prefix, after = lax.optimization_barrier((prefix, starts))
     coming = across(prefix)
-    qf, kf, scores, intra = call(
-        local_body, [(wide, BF16)] * 3 + [(wide, F32)], 4, 32 * mm, 4 << 20, 1 << 19
-    )(after, q, k, v)
-    coming, scores = lax.optimization_barrier((coming, scores))
     (send2,) = call(
         give_body, [((HALF * FEAT + 64, FEAT), F32)], 3, 1 << 18, 3 << 19
     )(starts, keep1, coming)

time: 147 us -> 142 us (0.966)
  blocking collectives: 17.8 us -> 40 us
  waiting for transfers between devices: 38 us -> 24.8 us
  local copies, waits for them, and re-layouts: 19.4 us -> 12.2 us
  starting transfers between devices: 49.8 us -> 42.9 us
    all_to_all x1 -> x2, blocking collectives: 17.8 us -> 40 us  [across(): return lax.all_to_all(x, 'seq', 0, 0, axis_index_groups=zgroups, tiled=True)]
    all_to_all x3 -> x2, waiting for transfers between devices: 23.2 us -> 12.1 us  [across(): return lax.all_to_all(x, 'seq', 0, 0, axis_index_groups=zgroups, tiled=True)]
    unnamed x58 -> x46, local copies, waits for them, and re-layouts: 19.4 us -> 12.2 us
    all_to_all x3 -> x2, starting transfers between devices: 13.4 us -> 8.42 us  [across(): return lax.all_to_all(x, 'seq', 0, 0, axis_index_groups=zgroups, tiled=True)]
    ppermute x4, waiting for transfers between devices: 4.6 us -> 3.09 us  [other(): return lax.ppermute(x, 'seq', swap)]
    ppermute x1, waiting for transfers between devices: 1.49 us -> 0.01 us  [shards(): gain_rows = lax.ppermute(row, ('dp', 'seq'), shifted)]
  transfers between devices with their start and end apart: 10 -> 9, of which waited for: 9 -> 6; matrix products, arithmetic and copies ran while one was open for 0% -> 0% of each run, Pallas kernels for 6% -> 7%
where the time goes in v4:
time: 142 us; the launch traced here: 141 us
  starting transfers between devices  42.9 us (30%)
  blocking collectives  40 us (28%)
  waiting for transfers between devices  24.8 us (17%)
  Pallas kernels  19.8 us (14%)
  local copies, waits for them, and re-layouts  12.2 us (9%)
    all_to_all x2, blocking collectives, across(): return lax.all_to_all(x, 'seq', 0, 0, axis_index_groups=zgroups, tiled=True)  40 us
    ppermute x4, starting transfers between devices, other(): return lax.ppermute(x, 'seq', swap)  19.8 us
    unnamed x46, local copies, waits for them, and re-layouts  12.2 us
    all_to_all x2, waiting for transfers between devices, across(): return lax.all_to_all(x, 'seq', 0, 0, axis_index_groups=zgroups, tiled=True)  12.1 us
    all_to_all x2, starting transfers between devices, across(): return lax.all_to_all(x, 'seq', 0, 0, axis_index_groups=zgroups, tiled=True)  8.42 us
    all_to_all x1, starting transfers between devices, shards(): gathered = lax.all_to_all(terms, 'dp', 0, 0, tiled=True)  8.14 us
    all_to_all x1, waiting for transfers between devices, shards(): gathered = lax.all_to_all(terms, 'dp', 0, 0, tiled=True)  7.18 us
    pallas_call x1, Pallas kernels, shards(): call(grads_body, [(wide, BF16), (wide, F32), (wide, F32)], 8, 80 * mm, 7...  4.78 us
  transfers between devices with their start and end apart: 9, of which 6 were waited for; matrix products, arithmetic and copies ran while one was open for 0% of the time, Pallas kernels for 7%

profile of v4, /device:TPU:1, one launch (start us, length us, event | category | flops | bytes accessed | tf_op | source)
XLA Modules:
  0.0 140.7 jit_solution(16652884208194145025)
XLA Ops:
  1.3 1.0 copy-done
  2.3 1.0 copy-done.2
  3.4 1.1 shard_map.101
  4.5 8.8 %collective-permute-start = (f32[8,128,128]{2,1,0:T(8,128)S(1)}, f32[8,128,128]{2,1,0:T(8,128)S(1)}, u32[]{:S(2)}, u32[]{:S(2)}) collective-permute-start(f32[8,128,128]{2,1,0:T(8,128)S(1)} %get-tuple-element.34), channel_id=1, source_target_pairs={{0,1},{1,0},{2,3},{3,2},{4,5},{5,4},{6,7},{7,6},{8,9},{9,8},{10,11... | collective-permute-start | bytes 1572872 | tf_op jit(solution)/shard_map/ppermute | solution.py:294
  14.2 1.9 %collective-permute-start.1 = (f32[8,128]{1,0:T(8,128)S(1)}, f32[8,128]{1,0:T(8,128)S(1)}, u32[]{:S(2)}, u32[]{:S(2)}) collective-permute-start(f32[8,128]{1,0:T(8,128)S(1)} %and_select_fusion), channel_id=1, source_target_pairs={{0,128},{16,144},{32,160},{48,176},{64,192},{80,208},{96,224},{112... | collective-permute-start | bytes 12296 | tf_op jit(solution)/shard_map/ppermute | solution.py:305
  16.1 2.4 %collective-permute-done.1 = f32[8,128]{1,0:T(8,128)S(1)} collective-permute-done((f32[8,128]{1,0:T(8,128)S(1)}, f32[8,128]{1,0:T(8,128)S(1)}, u32[]{:S(2)}, u32[]{:S(2)}) %collective-permute-start.1) | collective-permute-done | bytes 4128 | tf_op jit(solution)/shard_map/ppermute | solution.py:305
  18.6 1.4 %shard_map.102 = f32[8,128,128]{2,1,0:T(8,128)} custom-call(s32[1,8]{1,0:T(1,128)S(1)} %copy-done.21, f32[8,128,128]{2,1,0:T(8,128)S(1)} %get-tuple-element.33.keep, f32[8,128,128]{2,1,0:T(8,128)S(1)} %collective-permute-done.recv.theirs), custom_call_target="tpu_custom_call" | custom-call | flops 262144 | bytes 1572864 | tf_op jit(solution)/shard_map/pallas_call | solution.py:310
  20.0 4.8 %all-to-all-start = ((f32[8,128,128]{2,1,0:T(8,128)}), f32[8,128,128]{2,1,0:T(8,128)S(1)}, u32[]{:S(2)}, u32[]{:S(2)}) async-start(f32[8,128,128]{2,1,0:T(8,128)} %shard_map.102), calls=%async_computation | async-start | bytes 1048576 | tf_op jit(solution)/shard_map/all_to_all | solution.py:297
  24.8 4.6 %collective-permute-start.2 = (f32[8,128]{1,0:T(8,128)S(1)}, f32[8,128]{1,0:T(8,128)S(1)}, u32[]{:S(2)}, u32[]{:S(2)}) collective-permute-start(f32[8,128]{1,0:T(8,128)S(1)} %fusion.1), channel_id=1, source_target_pairs={{0,0},{257,1},{18,2},{275,3},{36,4},{293,5},{54,6},{311,7},{72,8},... | collective-permute-start | bytes 12296 | tf_op jit(solution)/shard_map/ppermute | solution.py:317
  29.5 4.0 %shard_map.103 = (bf16[128,2048]{1,0:T(8,128)(2,1)}, bf16[128,2048]{1,0:T(8,128)(2,1)}, bf16[128,2048]{1,0:T(8,128)(2,1)}, f32[128,2048]{1,0:T(8,128)}) custom-call(s32[1,8]{1,0:T(1,128)S(1)} %copy-done.21, bf16[128,2048]{1,0:T(8,128)(2,1)S(1)} %bitcast.20, bf16[128,2048]{1,0:T(8,128)(2,1)S(1)} %bitcast.18, bf16[128,2048]{1,0:T(8,128)(2,1)S(1)} %bitcast.14), custom_call_target="tpu_custom_call" | custom-call | flops 134217728 | bytes 4194304 | tf_op jit(solution)/shard_map/pallas_call | solution.py:318
  33.5 7.8 %all-to-all-done.parts = f32[8,128,128]{2,1,0:T(8,128)S(1)} async-done(((f32[8,128,128]{2,1,0:T(8,128)}), f32[8,128,128]{2,1,0:T(8,128)S(1)}, u32[]{:S(2)}, u32[]{:S(2)}) %all-to-all-start) | async-done | bytes 524320 | tf_op jit(solution)/shard_map/all_to_all | solution.py:297
  42.0 22.5 %all_to_all.32.coming = f32[8,136,128]{2,1,0:T(8,128)S(1)} all-to-all(f32[8,136,128]{2,1,0:T(8,128)S(1)} %shard_map.104), channel_id=1, replica_groups={{0,2,4,6,8,10,12,14},{1,3,5,7,9,11,13,15},{16,18,20,22,24,26,28,30},{17..., dimensions={0} | all-to-all | bytes 1114112 | tf_op jit(solution)/shard_map/all_to_all | solution.py:297
  65.1 2.6 %collective-permute-start.3 = (f32[1088,128]{1,0:T(8,128)S(1)}, f32[1088,128]{1,0:T(8,128)S(1)}, u32[]{:S(2)}, u32[]{:S(2)}) collective-permute-start(f32[1088,128]{1,0:T(8,128)S(1)} %shard_map.105), channel_id=1, source_target_pairs={{0,1},{1,0},{2,3},{3,2},{4,5},{5,4},{6,7},{7,6},{8,9},{9,8},{10,11... | collective-permute-start | bytes 1671176 | tf_op jit(solution)/shard_map/ppermute | solution.py:294
  67.7 1.6 %collective-permute-done.3.ready = f32[1088,128]{1,0:T(8,128)S(1)} collective-permute-done((f32[1088,128]{1,0:T(8,128)S(1)}, f32[1088,128]{1,0:T(8,128)S(1)}, u32[]{:S(2)}, u32[]{:S(2)}) %collective-permute-start.3) | collective-permute-done | bytes 557088 | tf_op jit(solution)/shard_map/ppermute | solution.py:294
  69.3 2.8 %shard_map.106 = (bf16[128,2048]{1,0:T(8,128)(2,1)}, bf16[128,2048]{1,0:T(8,128)(2,1)S(1)}, bf16[16,128,128]{2,1,0:T(8,128)(2,1)S(1)}, f32[8,128,128]{2,1,0:T(8,...) custom-call(s32[1,8]{1,0:T(1,128)S(1)} %copy-done.21, bf16[128,2048]{1,0:T(8,128)(2,1)S(1)} %copy-done.8, ...), custom_call_target="tpu_custom_call" | custom-call | flops 134217728 | bytes 5242880 | tf_op jit(solution)/shard_map/pallas_call | solution.py:331
  72.9 2.3 %collective-permute-start.4 = (f32[8,128,128]{2,1,0:T(8,128)}, f32[8,128,128]{2,1,0:T(8,128)S(1)}, u32[]{:S(2)}, u32[]{:S(2)}) collective-permute-start(f32[8,128,128]{2,1,0:T(8,128)} %get-tuple-element.44), channel_id=1, source_target_pairs={{0,1},{1,0},{2,3},{3,2},{4,5},{5,4},{6,7},{7,6},{8,9},{9,8},{10,11... | collective-permute-start | bytes 1572872 | tf_op jit(solution)/shard_map/ppermute | solution.py:294
  75.2 8.1 %all-to-all-start.2 = ((f32[32,1,128]{2,1,0:T(1,128)}), f32[32,1,128]{2,1,0:T(1,128)S(1)}, u32[]{:S(2)}, u32[]{:S(2)}) async-start(f32[32,1,128]{2,1,0:T(1,128)} %bitcast.6), calls=%async_computation.2 | async-start | bytes 32768 | tf_op jit(solution)/shard_map/all_to_all | solution.py:338
  84.8 7.2 %all-to-all-done.2 = f32[32,1,128]{2,1,0:T(1,128)S(1)} async-done(((f32[32,1,128]{2,1,0:T(1,128)}), f32[32,1,128]{2,1,0:T(1,128)S(1)}, u32[]{:S(2)}, u32[]{:S(2)}) %all-to-all-start.2) | async-done | bytes 16416 | tf_op jit(solution)/shard_map/all_to_all | solution.py:338
  92.0 3.6 %all-to-all-start.3 = ((f32[8,128,128]{2,1,0:T(8,128)}), f32[8,128,128]{2,1,0:T(8,128)S(1)}, u32[]{:S(2)}, u32[]{:S(2)}) async-start(f32[8,128,128]{2,1,0:T(8,128)} %copy-done.5), calls=%async_computation.3 | async-start | bytes 1048576 | tf_op jit(solution)/shard_map/all_to_all | solution.py:297
  95.6 1.0 copy-done.7
  96.6 1.0 copy-done.9
  97.7 1.0 copy-done.16
  98.7 1.0 copy-done.18
  99.8 1.0 copy-done.20
  100.8 4.8 %shard_map.108 = (bf16[128,2048]{1,0:T(8,128)(2,1)}, f32[128,2048]{1,0:T(8,128)S(1)}, f32[128,2048]{1,0:T(8,128)S(1)}) custom-call(s32[1,8]{1,0:T(1,128)S(1)} %copy-done.21, bf16[128,2048]{1,0:T(8,128)(2,1)S(1)} %bitcast.21, bf16[128,2048]{1,0:T(8,128)(2,1)S(1)} %bitcast.15, bf16[128,2048]{1,0:T(8,128)(2,1)S(1)} %copy-done.9, ...), custom_call_target="tpu_custom_call" | custom-call | flops 335544320 | bytes 7340032 | tf_op jit(solution)/shard_map/pallas_call | solution.py:343
  105.6 1.0 copy-done.11
  106.6 1.0 copy-done.13
  107.5 4.3 %all-to-all-done.3.parts = f32[8,128,128]{2,1,0:T(8,128)S(1)} async-done(((f32[8,128,128]{2,1,0:T(8,128)}), f32[8,128,128]{2,1,0:T(8,128)S(1)}, u32[]{:S(2)}, u32[]{:S(2)}) %all-to-all-start.3) | async-done | bytes 524320 | tf_op jit(solution)/shard_map/all_to_all | solution.py:297
  112.5 17.5 %all_to_all.33.coming = f32[8,136,128]{2,1,0:T(8,128)S(1)} all-to-all(f32[8,136,128]{2,1,0:T(8,128)S(1)} %shard_map.109), channel_id=1, replica_groups={{0,2,4,6,8,10,12,14},{1,3,5,7,9,11,13,15},{16,18,20,22,24,26,28,30},{17..., dimensions={0} | all-to-all | bytes 1114112 | tf_op jit(solution)/shard_map/all_to_all | solution.py:297
  130.6 6.1 %collective-permute-start.5 = (f32[1032,128]{1,0:T(8,128)S(1)}, f32[1032,128]{1,0:T(8,128)S(1)}, u32[]{:S(2)}, u32[]{:S(2)}) collective-permute-start(f32[1032,128]{1,0:T(8,128)S(1)} %shard_map.110), channel_id=1, source_target_pairs={{0,1},{1,0},{2,3},{3,2},{4,5},{5,4},{6,7},{7,6},{8,9},{9,8},{10,11... | collective-permute-start | bytes 1585160 | tf_op jit(solution)/shard_map/ppermute | solution.py:294
  136.7 1.5 %collective-permute-done.5.ready = f32[1032,128]{1,0:T(8,128)S(1)} collective-permute-done((f32[1032,128]{1,0:T(8,128)S(1)}, f32[1032,128]{1,0:T(8,128)S(1)}, u32[]{:S(2)}, u32[]{:S(2)}) %collective-permute-start.5) | collective-permute-done | bytes 528416 | tf_op jit(solution)/shard_map/ppermute | solution.py:294
  138.3 2.5 %shard_map.111 = (bf16[128,2048]{1,0:T(8,128)(2,1)}, bf16[128,2048]{1,0:T(8,128)(2,1)}, f32[1,64]{1,0:T(1,128)}) custom-call(s32[1,8]{1,0:T(1,128)S(1)} %copy-done.21, bf16[128,2048]{1,0:T(8,128)(2,1)S(1)} %bitcast.19, bf16[128,2048]{1,0:T(8,128)(2,1)S(1)} %bitcast.16, bf16[128,2048]{1,0:T(8,128)(2,1)S(1)} %copy-done.4, f32[128,2048]{1,0:T(8,128)S(1)} %copy-done.12, ...), custom_call_target="tpu_custom_call" | custom-call | flops 134217728 | bytes 5242880 | tf_op jit(solution)/shard_map/pallas_call | solution.py:355
  (50 shorter events, 6.3 us)
Async XLA Ops:
  0.6 0.7 copy-start.21
  1.3 1.0 copy-start
  2.3 1.0 copy-start.2
  4.5 14.1 %collective-permute-start = (f32[8,128,128]{2,1,0:T(8,128)S(1)}, f32[8,128,128]{2,1,0:T(8,128)S(1)}, u32[]{:S(2)}, u32[]{:S(2)}) collective-permute-start(f32[8,128,128]{2,1,0:T(8,128)S(1)} %get-tuple-element.34), channel_id=1, source_target_pairs={{0,1},{1,0},{2,3},{3,2},{4,5},{5,4},{6,7},{7,6},{8,9},{9,8},{10,11... | collective-permute-start | bytes 1572872 | tf_op jit(solution)/shard_map/ppermute | solution.py:294
  13.4 0.7 copy-start.22
  14.2 4.3 %collective-permute-start.1 = (f32[8,128]{1,0:T(8,128)S(1)}, f32[8,128]{1,0:T(8,128)S(1)}, u32[]{:S(2)}, u32[]{:S(2)}) collective-permute-start(f32[8,128]{1,0:T(8,128)S(1)} %and_select_fusion), channel_id=1, source_target_pairs={{0,128},{16,144},{32,160},{48,176},{64,192},{80,208},{96,224},{112... | collective-permute-start | bytes 12296 | tf_op jit(solution)/shard_map/ppermute | solution.py:305
  18.6 10.9 %copy-start.6 = (bf16[1,128,2048]{2,1,0:T(8,128)(2,1)S(1)}, bf16[1,128,2048]{2,1,0:T(8,128)(2,1)}, u32[]{:S(2)}) copy-start(bf16[1,128,2048]{2,1,0:T(8,128)(2,1)} %param.6) | copy-start | bytes 1572868
  20.0 9.5 %copy-start.1 = (bf16[1,128,2048]{2,1,0:T(8,128)(2,1)S(1)}, bf16[1,128,2048]{2,1,0:T(8,128)(2,1)}, u32[]{:S(2)}) copy-start(bf16[1,128,2048]{2,1,0:T(8,128)(2,1)} %param.8) | copy-start | bytes 1572868
  20.0 9.5 %copy-start.3 = (bf16[1,128,2048]{2,1,0:T(8,128)(2,1)S(1)}, bf16[1,128,2048]{2,1,0:T(8,128)(2,1)}, u32[]{:S(2)}) copy-start(bf16[1,128,2048]{2,1,0:T(8,128)(2,1)} %param.7) | copy-start | bytes 1572868
  20.0 21.3 %all-to-all-start = ((f32[8,128,128]{2,1,0:T(8,128)}), f32[8,128,128]{2,1,0:T(8,128)S(1)}, u32[]{:S(2)}, u32[]{:S(2)}) async-start(f32[8,128,128]{2,1,0:T(8,128)} %shard_map.102), calls=%async_computation | async-start | bytes 1048576 | tf_op jit(solution)/shard_map/all_to_all | solution.py:297
  24.8 16.5 %collective-permute-start.2 = (f32[8,128]{1,0:T(8,128)S(1)}, f32[8,128]{1,0:T(8,128)S(1)}, u32[]{:S(2)}, u32[]{:S(2)}) collective-permute-start(f32[8,128]{1,0:T(8,128)S(1)} %fusion.1), channel_id=1, source_target_pairs={{0,0},{257,1},{18,2},{275,3},{36,4},{293,5},{54,6},{311,7},{72,8},... | collective-permute-start | bytes 12296 | tf_op jit(solution)/shard_map/ppermute | solution.py:317
  42.0 27.3 %copy-start.15 = (bf16[1,128,2048]{2,1,0:T(8,128)(2,1)S(1)}, bf16[1,128,2048]{2,1,0:T(8,128)(2,1)}, u32[]{:S(2)}) copy-start(bf16[1,128,2048]{2,1,0:T(8,128)(2,1)} %param.9) | copy-start | bytes 1572868
  64.4 4.9 %copy-start.8 = (bf16[128,2048]{1,0:T(8,128)(2,1)S(1)}, bf16[128,2048]{1,0:T(8,128)(2,1)}, u32[]{:S(2)}) copy-start(bf16[128,2048]{1,0:T(8,128)(2,1)} %get-tuple-element.36.qf) | copy-start | bytes 1572868
  64.4 4.9 %copy-start.10 = (f32[128,2048]{1,0:T(8,128)S(1)}, f32[128,2048]{1,0:T(8,128)}, u32[]{:S(2)}) copy-start(f32[128,2048]{1,0:T(8,128)} %get-tuple-element.37.intra) | copy-start | bytes 3145732
  65.1 4.2 %collective-permute-start.3 = (f32[1088,128]{1,0:T(8,128)S(1)}, f32[1088,128]{1,0:T(8,128)S(1)}, u32[]{:S(2)}, u32[]{:S(2)}) collective-permute-start(f32[1088,128]{1,0:T(8,128)S(1)} %shard_map.105), channel_id=1, source_target_pairs={{0,1},{1,0},{2,3},{3,2},{4,5},{5,4},{6,7},{7,6},{8,9},{9,8},{10,11... | collective-permute-start | bytes 1671176 | tf_op jit(solution)/shard_map/ppermute | solution.py:294
  72.1 0.8 copy-start.17
  72.9 11.1 %copy-start.19 = (bf16[16,128,128]{2,1,0:T(8,128)(2,1)}, bf16[16,128,128]{2,1,0:T(8,128)(2,1)S(1)}, u32[]{:S(2)}) copy-start(bf16[16,128,128]{2,1,0:T(8,128)(2,1)S(1)} %get-tuple-element.50.inb) | copy-start | bytes 1572868
  72.9 10.4 %collective-permute-start.4 = (f32[8,128,128]{2,1,0:T(8,128)}, f32[8,128,128]{2,1,0:T(8,128)S(1)}, u32[]{:S(2)}, u32[]{:S(2)}) collective-permute-start(f32[8,128,128]{2,1,0:T(8,128)} %get-tuple-element.44), channel_id=1, source_target_pairs={{0,1},{1,0},{2,3},{3,2},{4,5},{5,4},{6,7},{7,6},{8,9},{9,8},{10,11... | collective-permute-start | bytes 1572872 | tf_op jit(solution)/shard_map/ppermute | solution.py:294
  75.2 16.8 %all-to-all-start.2 = ((f32[32,1,128]{2,1,0:T(1,128)}), f32[32,1,128]{2,1,0:T(1,128)S(1)}, u32[]{:S(2)}, u32[]{:S(2)}) async-start(f32[32,1,128]{2,1,0:T(1,128)} %bitcast.6), calls=%async_computation.2 | async-start | bytes 32768 | tf_op jit(solution)/shard_map/all_to_all | solution.py:338
  84.0 0.8 copy-start.5
  92.0 3.6 %copy-start.4 = (bf16[128,2048]{1,0:T(8,128)(2,1)S(1)}, bf16[128,2048]{1,0:T(8,128)(2,1)}, u32[]{:S(2)}) copy-start(bf16[128,2048]{1,0:T(8,128)(2,1)} %get-tuple-element.47.kf) | copy-start | bytes 1572868
  92.0 19.9 %all-to-all-start.3 = ((f32[8,128,128]{2,1,0:T(8,128)}), f32[8,128,128]{2,1,0:T(8,128)S(1)}, u32[]{:S(2)}, u32[]{:S(2)}) async-start(f32[8,128,128]{2,1,0:T(8,128)} %copy-done.5), calls=%async_computation.3 | async-start | bytes 1048576 | tf_op jit(solution)/shard_map/all_to_all | solution.py:297
  95.6 1.0 copy-start.7
  96.6 1.0 copy-start.9
  97.7 1.0 copy-start.16
  98.7 1.0 copy-start.18
  99.8 1.0 copy-start.20
  105.6 1.0 copy-start.11
  106.6 1.0 copy-start.13
  112.5 25.7 %copy-start.14 = (f32[128,2048]{1,0:T(8,128)S(1)}, f32[128,2048]{1,0:T(8,128)}, u32[]{:S(2)}) copy-start(f32[128,2048]{1,0:T(8,128)} %copy-done.13) | copy-start | bytes 3145732
  130.0 8.3 %copy-start.12 = (f32[128,2048]{1,0:T(8,128)S(1)}, f32[128,2048]{1,0:T(8,128)}, u32[]{:S(2)}) copy-start(f32[128,2048]{1,0:T(8,128)} %copy-done.11) | copy-start | bytes 3145732
  130.6 7.6 %collective-permute-start.5 = (f32[1032,128]{1,0:T(8,128)S(1)}, f32[1032,128]{1,0:T(8,128)S(1)}, u32[]{:S(2)}, u32[]{:S(2)}) collective-permute-start(f32[1032,128]{1,0:T(8,128)S(1)} %shard_map.110), channel_id=1, source_target_pairs={{0,1},{1,0},{2,3},{3,2},{4,5},{5,4},{6,7},{7,6},{8,9},{9,8},{10,11... | collective-permute-start | bytes 1585160 | tf_op jit(solution)/shard_map/ppermute | solution.py:294

commit v5 on v4

--- a/solution.py
+++ b/solution.py
@@ -22,11 +22,11 @@
 HB = pl.BlockSpec(memory_space=pltpu.HBM)
 
 
-def call(body, outs, n_in, flops=0, nbytes=0, trans=0, far=False, scratch=()):
+def call(body, outs, n_in, flops=0, nbytes=0, trans=0, far=False, far_in=(), scratch=()):
     return pl.pallas_call(
         body,
         out_shape=[pltpu.HBM(s, d) if far else jax.ShapeDtypeStruct(s, d) for s, d in outs],
-        in_specs=[SM] + [VM] * (n_in - 1),
+        in_specs=[SM] + [HB if i in far_in else VM for i in range(1, n_in)],
         out_specs=[HB if far else VM] * len(outs),
         scratch_shapes=scratch,
         compiler_params=pltpu.CompilerParams(vmem_limit_bytes=24 * 1024 * 1024),
@@ -137,7 +137,8 @@
 
 def scan_back_body(starts, parts, terms, out):
     total = jnp.zeros((FEAT, FEAT), F32)
-    gsum = jnp.broadcast_to(jnp.sum(terms[...], axis=0, keepdims=True), (8, FEAT))
+    x = lax.axis_index("dp") // CHIPS
+    gsum = jnp.broadcast_to(terms[pl.ds(x, 1), :], (8, FEAT))
     for z in reversed(range(CHIPS)):
         out[z, :FEAT] = total
         out[z, FEAT:] = gsum
@@ -202,6 +203,7 @@
 ):
     idx, core = place()
     y = lax.rem(lax.axis_index("dp"), CHIPS)
+    terms[...] = jnp.zeros_like(terms)
     for j in range(CHIPS):
         at = HALF * FEAT + 8 * j
         gains[8 * j : 8 * j + 8, :] = coming[j, FEAT:] + ready[at : at + 8]
@@ -233,24 +235,54 @@
             dn = (recip * upper - normed * recip * mean).astype(BF16)
             dn_out[:, at] = dn
             term = jnp.sum(grad * normed, axis=0, keepdims=True)
-            terms[pl.ds(2 * h, 1), :] = term
-            terms[pl.ds(2 * h + 1, 1), :] = term
+            to = 16 * lax.rem(h, 4) + h // 4
+            terms[pl.ds(to, 1), :] = term
+            terms[pl.ds(to + 8, 1), :] = term
             masked = jnp.where(cin, dn, jnp.zeros_like(dn))
             state[j] = dot(qh, masked, 0, 0)
 
 
-def grads_body(starts, q, v, qf, kf, scores, dn, inb, dq_out, dk_part, dv_part):
+def grads_body(starts, *refs):
+    ins, outs, in_bufs, out_bufs, sems = refs[:7], refs[7:10], refs[10:17], refs[17:20], refs[20]
+    q, v, qf, kf, scores, dn, inb = in_bufs
+    dq_buf, dk_buf, dv_buf = out_bufs
+    groups = [pl.ds(4 * g * FEAT, 4 * FEAT) for g in range(4)]
+    coming, going = [], []
+    for g in range(4):
+        these = []
+        for n in range(7):
+            if n < 6:
+                src, dst = ins[n].at[:, groups[g]], in_bufs[n].at[:, groups[g]]
+            else:
+                src, dst = ins[n].at[pl.ds(4 * g, 4)], in_bufs[n].at[pl.ds(4 * g, 4)]
+            these.append(pltpu.make_async_copy(src, dst, sems.at[10 * g + n]))
+        for c in these:
+            c.start()
+        coming.append(these)
     idx, _ = place()
     mask = mask_of(starts, idx)
     cin = enters(starts, idx)
     for h in range(HEADS):
+        g = h // 4
+        if h % 4 == 0:
+            for c in coming[g]:
+                c.wait()
         at = slice(h * FEAT, (h + 1) * FEAT)
         dnh = dn[:, at]
         dscores = jnp.where(mask, dot(dnh, v[:, at], 1, 1), 0.0).astype(BF16)
         dq = dot(dscores, kf[:, at], 1, 0) + jnp.where(cin, dot(dnh, inb[h], 1, 1), 0.0)
-        dq_out[:, at] = (dq * slope(q[:, at].astype(F32))).astype(BF16)
-        dk_part[:, at] = dot(dscores, qf[:, at], 0, 0)
-        dv_part[:, at] = dot(scores[:, at], dnh, 0, 0)
+        dq_buf[:, at] = (dq * slope(q[:, at].astype(F32))).astype(BF16)
+        dk_buf[:, at] = dot(dscores, qf[:, at], 0, 0)
+        dv_buf[:, at] = dot(scores[:, at], dnh, 0, 0)
+        if h % 4 == 3:
+            for n in range(3):
+                c = pltpu.make_async_copy(
+                    out_bufs[n].at[:, groups[g]], outs[n].at[:, groups[g]], sems.at[10 * g + 7 + n]
+                )
+                c.start()
+                going.append(c)
+    for c in going:
+        c.wait()
 
 
 def last_body(
@@ -332,21 +364,33 @@
         norm_body,
         [(wide, BF16), (wide, BF16), ((HEADS, FEAT, FEAT), BF16)]
         + [(half_states, F32)] * 2
-        + [((32, FEAT), F32)],
+        + [((64, FEAT), F32)],
         7, 32 * mm, 5 << 20, 1 << 15, scratch=[pltpu.VMEM((64, FEAT), F32)],
     )(starts, qf, intra, dy, coming, recv1, ready)
-    gathered = lax.all_to_all(terms, "dp", 0, 0, tiled=True)
+    lines = [[x * CHIPS + y for y in range(CHIPS)] for x in range(4)]
+    gathered = lax.all_to_all(terms, "dp", 0, 0, axis_index_groups=lines, tiled=True)
     recv3 = other(give3)
     (chip3,) = call(join_back_body, [(half_states, F32)], 3, 1 << 18, 3 << 19)(starts, keep3, recv3)
     chip3, gathered, after3 = lax.optimization_barrier((chip3, gathered, starts))
     parts3 = across(chip3)
+    total = jnp.sum(gathered.reshape(CHIPS, 8, FEAT), axis=0)
+    for step in (2 * CHIPS, CHIPS):
+        total = total + lax.ppermute(total, "dp", [(i, i ^ step) for i in range(4 * CHIPS)])
     dq, dk_part, dv_part = call(
-        grads_body, [(wide, BF16), (wide, F32), (wide, F32)], 8, 80 * mm, 7 << 20, 1 << 18
-    )(after3, q, v, qf, kf, scores, dn, inb)
+        grads_body, [(wide, BF16), (wide, F32), (wide, F32)], 8, 80 * mm, 7 << 20, 1 << 18,
+        far=True, far_in=range(1, 8),
+        scratch=[pltpu.VMEM(wide, BF16)] * 6
+        + [pltpu.VMEM((HEADS, FEAT, FEAT), BF16), pltpu.VMEM(wide, BF16)]
+        + [pltpu.VMEM(wide, F32)] * 2
+        + [pltpu.SemaphoreType.DMA((40,))],
+    )(
+        after3,
+        *(pltpu.with_memory_space_constraint(x, pltpu.HBM) for x in (q, v, qf, kf, scores, dn, inb)),
+    )
     parts3, dk_part = lax.optimization_barrier((parts3, dk_part))
     (suffix,) = call(
         scan_back_body, [((CHIPS, FEAT + 8, FEAT), F32)], 3, 1 << 18, 1 << 20
-    )(starts, parts3, gathered)
+    )(starts, parts3, total)
     coming4 = across(suffix)
     (send4,) = call(
         give_back_body, [((HALF * FEAT + 8, FEAT), F32)], 3, 1 << 18, 3 << 19

time: 142 us -> 141 us (level)
  local copies, waits for them, and re-layouts: 12.2 us -> 4.22 us
  starting transfers between devices: 42.9 us -> 48.8 us
  waiting for transfers between devices: 24.8 us -> 20 us
  blocking collectives: 40 us -> 43.1 us
  Pallas kernels: 19.8 us -> 22.8 us
    unnamed x46 -> x32, local copies, waits for them, and re-layouts: 12.2 us -> 4.22 us
    ppermute x0 -> x2, starting transfers between devices: none -> 7.75 us  [shards(): lax.ppermute(total, 'dp', [(i, i ^ step) for i in range(4 * CHIPS)])]
    all_to_all x2, waiting for transfers between devices: 12.1 us -> 7.82 us  [across(): return lax.all_to_all(x, 'seq', 0, 0, axis_index_groups=zgroups, tiled=True)]
    all_to_all x2, blocking collectives: 40 us -> 43.1 us  [across(): return lax.all_to_all(x, 'seq', 0, 0, axis_index_groups=zgroups, tiled=True)]
    all_to_all x1, starting transfers between devices: 8.14 us -> 5.3 us  [shards(): lax.all_to_all(terms, 'dp', 0, 0, axis_index_groups=lines, tiled=True)]
    pallas_call x1, Pallas kernels: 4.78 us -> 7 us  [shards(): call(grads_body, [(wide, BF16), (wide, F32), (wide, F32)], 8, 80 * mm, 7...]
    all_to_all x1, waiting for transfers between devices: 7.18 us -> 5.45 us  [shards(): lax.all_to_all(terms, 'dp', 0, 0, axis_index_groups=lines, tiled=True)]
  transfers between devices with their start and end apart: 9 -> 11, of which waited for: 6 -> 6; matrix products, arithmetic and copies ran while one was open for 0% -> 0% of each run, Pallas kernels for 7% -> 9%
where the time goes in v5:
time: 141 us; the launch traced here: 140 us
  starting transfers between devices  48.8 us (35%)
  blocking collectives  43.1 us (31%)
  Pallas kernels  22.8 us (16%)
  waiting for transfers between devices  20 us (14%)
  local copies, waits for them, and re-layouts  4.22 us (3%)
    all_to_all x2, blocking collectives, across(): return lax.all_to_all(x, 'seq', 0, 0, axis_index_groups=zgroups, tiled=True)  43.1 us
    ppermute x4, starting transfers between devices, other(): return lax.ppermute(x, 'seq', swap)  20.9 us
    all_to_all x2, starting transfers between devices, across(): return lax.all_to_all(x, 'seq', 0, 0, axis_index_groups=zgroups, tiled=True)  8.29 us
    all_to_all x2, waiting for transfers between devices, across(): return lax.all_to_all(x, 'seq', 0, 0, axis_index_groups=zgroups, tiled=True)  7.82 us
    ppermute x2, starting transfers between devices, shards(): lax.ppermute(total, 'dp', [(i, i ^ step) for i in range(4 * CHIPS)])  7.75 us
    pallas_call x1, Pallas kernels, shards(): call(grads_body, [(wide, BF16), (wide, F32), (wide, F32)], 8, 80 * mm, 7...  7 us
    all_to_all x1, waiting for transfers between devices, shards(): lax.all_to_all(terms, 'dp', 0, 0, axis_index_groups=lines, tiled=True)  5.45 us
    all_to_all x1, starting transfers between devices, shards(): lax.all_to_all(terms, 'dp', 0, 0, axis_index_groups=lines, tiled=True)  5.3 us
  transfers between devices with their start and end apart: 11, of which 6 were waited for; matrix products, arithmetic and copies ran while one was open for 0% of the time, Pallas kernels for 9%

profile of v5, /device:TPU:1, one launch (start us, length us, event | category | flops | bytes accessed | tf_op | source)
XLA Modules:
  0.0 140.1 jit_solution(9844478465343478684)
XLA Ops:
  0.6 0.6 copy-done.14
  1.3 1.0 copy-done
  2.3 1.0 copy-done.3
  3.4 1.1 shard_map.101
  4.5 8.8 %collective-permute-start = (f32[8,128,128]{2,1,0:T(8,128)S(1)}, f32[8,128,128]{2,1,0:T(8,128)S(1)}, u32[]{:S(2)}, u32[]{:S(2)}) collective-permute-start(f32[8,128,128]{2,1,0:T(8,128)S(1)} %get-tuple-element.34), channel_id=1, source_target_pairs={{0,1},{1,0},{2,3},{3,2},{4,5},{5,4},{6,7},{7,6},{8,9},{9,8},{10,11... | collective-permute-start | bytes 1572872 | tf_op jit(solution)/shard_map/ppermute | solution.py:326
  14.2 1.9 %collective-permute-start.1 = (f32[8,128]{1,0:T(8,128)S(1)}, f32[8,128]{1,0:T(8,128)S(1)}, u32[]{:S(2)}, u32[]{:S(2)}) collective-permute-start(f32[8,128]{1,0:T(8,128)S(1)} %and_select_fusion), channel_id=1, source_target_pairs={{0,128},{16,144},{32,160},{48,176},{64,192},{80,208},{96,224},{112... | collective-permute-start | bytes 12296 | tf_op jit(solution)/shard_map/ppermute | solution.py:337
  16.1 2.4 %collective-permute-done.1 = f32[8,128]{1,0:T(8,128)S(1)} collective-permute-done((f32[8,128]{1,0:T(8,128)S(1)}, f32[8,128]{1,0:T(8,128)S(1)}, u32[]{:S(2)}, u32[]{:S(2)}) %collective-permute-start.1) | collective-permute-done | bytes 4128 | tf_op jit(solution)/shard_map/ppermute | solution.py:337
  18.6 1.4 %shard_map.102 = f32[8,128,128]{2,1,0:T(8,128)} custom-call(s32[1,8]{1,0:T(1,128)S(1)} %copy-done.14, f32[8,128,128]{2,1,0:T(8,128)S(1)} %get-tuple-element.33.keep, f32[8,128,128]{2,1,0:T(8,128)S(1)} %collective-permute-done.recv.theirs), custom_call_target="tpu_custom_call" | custom-call | flops 262144 | bytes 1572864 | tf_op jit(solution)/shard_map/pallas_call | solution.py:342
  20.0 4.8 %all-to-all-start = ((f32[8,128,128]{2,1,0:T(8,128)}), f32[8,128,128]{2,1,0:T(8,128)S(1)}, u32[]{:S(2)}, u32[]{:S(2)}) async-start(f32[8,128,128]{2,1,0:T(8,128)} %shard_map.102), calls=%async_computation | async-start | bytes 1048576 | tf_op jit(solution)/shard_map/all_to_all | solution.py:329
  24.8 4.6 %collective-permute-start.2 = (f32[8,128]{1,0:T(8,128)S(1)}, f32[8,128]{1,0:T(8,128)S(1)}, u32[]{:S(2)}, u32[]{:S(2)}) collective-permute-start(f32[8,128]{1,0:T(8,128)S(1)} %fusion.1), channel_id=1, source_target_pairs={{0,0},{257,1},{18,2},{275,3},{36,4},{293,5},{54,6},{311,7},{72,8},... | collective-permute-start | bytes 12296 | tf_op jit(solution)/shard_map/ppermute | solution.py:349
  29.5 4.0 %shard_map.103 = (bf16[128,2048]{1,0:T(8,128)(2,1)}, bf16[128,2048]{1,0:T(8,128)(2,1)}, bf16[128,2048]{1,0:T(8,128)(2,1)}, f32[128,2048]{1,0:T(8,128)}) custom-call(s32[1,8]{1,0:T(1,128)S(1)} %copy-done.14, bf16[128,2048]{1,0:T(8,128)(2,1)S(1)} %bitcast.21, bf16[128,2048]{1,0:T(8,128)(2,1)S(1)} %bitcast.18, bf16[128,2048]{1,0:T(8,128)(2,1)S(1)} %bitcast.15), custom_call_target="tpu_custom_call" | custom-call | flops 134217728 | bytes 4194304 | tf_op jit(solution)/shard_map/pallas_call | solution.py:350
  33.5 7.8 %all-to-all-done.parts = f32[8,128,128]{2,1,0:T(8,128)S(1)} async-done(((f32[8,128,128]{2,1,0:T(8,128)}), f32[8,128,128]{2,1,0:T(8,128)S(1)}, u32[]{:S(2)}, u32[]{:S(2)}) %all-to-all-start) | async-done | bytes 524320 | tf_op jit(solution)/shard_map/all_to_all | solution.py:329
  42.0 22.5 %all_to_all.32.coming = f32[8,136,128]{2,1,0:T(8,128)S(1)} all-to-all(f32[8,136,128]{2,1,0:T(8,128)S(1)} %shard_map.104), channel_id=1, replica_groups={{0,2,4,6,8,10,12,14},{1,3,5,7,9,11,13,15},{16,18,20,22,24,26,28,30},{17..., dimensions={0} | all-to-all | bytes 1114112 | tf_op jit(solution)/shard_map/all_to_all | solution.py:329
  65.1 2.6 %collective-permute-start.3 = (f32[1088,128]{1,0:T(8,128)S(1)}, f32[1088,128]{1,0:T(8,128)S(1)}, u32[]{:S(2)}, u32[]{:S(2)}) collective-permute-start(f32[1088,128]{1,0:T(8,128)S(1)} %shard_map.105), channel_id=1, source_target_pairs={{0,1},{1,0},{2,3},{3,2},{4,5},{5,4},{6,7},{7,6},{8,9},{9,8},{10,11... | collective-permute-start | bytes 1671176 | tf_op jit(solution)/shard_map/ppermute | solution.py:326
  67.7 1.6 %collective-permute-done.3.ready = f32[1088,128]{1,0:T(8,128)S(1)} collective-permute-done((f32[1088,128]{1,0:T(8,128)S(1)}, f32[1088,128]{1,0:T(8,128)S(1)}, u32[]{:S(2)}, u32[]{:S(2)}) %collective-permute-start.3) | collective-permute-done | bytes 557088 | tf_op jit(solution)/shard_map/ppermute | solution.py:326
  69.3 2.8 %shard_map.106 = (bf16[128,2048]{1,0:T(8,128)(2,1)}, bf16[128,2048]{1,0:T(8,128)(2,1)S(1)}, bf16[16,128,128]{2,1,0:T(8,128)(2,1)S(1)}, f32[8,128,128]{2,1,0:T(8,...) custom-call(s32[1,8]{1,0:T(1,128)S(1)} %copy-done.14, bf16[128,2048]{1,0:T(8,128)(2,1)S(1)} %copy-done.7, ...), custom_call_target="tpu_custom_call" | custom-call | flops 134217728 | bytes 5242880 | tf_op jit(solution)/shard_map/pallas_call | solution.py:363
  72.1 0.8 copy-done.13
  72.9 2.3 %collective-permute-start.4 = (f32[8,128,128]{2,1,0:T(8,128)}, f32[8,128,128]{2,1,0:T(8,128)S(1)}, u32[]{:S(2)}, u32[]{:S(2)}) collective-permute-start(f32[8,128,128]{2,1,0:T(8,128)} %get-tuple-element.44), channel_id=1, source_target_pairs={{0,1},{1,0},{2,3},{3,2},{4,5},{5,4},{6,7},{7,6},{8,9},{9,8},{10,11... | collective-permute-start | bytes 1572872 | tf_op jit(solution)/shard_map/ppermute | solution.py:326
  75.2 5.3 %all-to-all-start.2 = ((f32[8,8,128]{2,1,0:T(8,128)}), f32[8,8,128]{2,1,0:T(8,128)S(1)}, u32[]{:S(2)}, u32[]{:S(2)}) async-start(f32[8,8,128]{2,1,0:T(8,128)} %bitcast.5), calls=%async_computation.2 | async-start | bytes 65536 | tf_op jit(solution)/shard_map/all_to_all | solution.py:371
  80.5 1.4 %shard_map.107 = f32[8,128,128]{2,1,0:T(8,128)} custom-call(s32[1,8]{1,0:T(1,128)S(1)} %copy-done.14, f32[8,128,128]{2,1,0:T(8,128)S(1)} %get-tuple-element.43.keep, f32[8,128,128]{2,1,0:T(8,128)S(1)} %collective-permute-done.4.recv.theirs), custom_call_target="tpu_custom_call" | custom-call | flops 262144 | bytes 1572864 | tf_op jit(solution)/shard_map/pallas_call | solution.py:373
  81.9 5.4 %all-to-all-done.2 = f32[8,8,128]{2,1,0:T(8,128)S(1)} async-done(((f32[8,8,128]{2,1,0:T(8,128)}), f32[8,8,128]{2,1,0:T(8,128)S(1)}, u32[]{:S(2)}, u32[]{:S(2)}) %all-to-all-start.2) | async-done | bytes 32800 | tf_op jit(solution)/shard_map/all_to_all | solution.py:371
  87.4 3.5 %all-to-all-start.3 = ((f32[8,128,128]{2,1,0:T(8,128)}), f32[8,128,128]{2,1,0:T(8,128)S(1)}, u32[]{:S(2)}, u32[]{:S(2)}) async-start(f32[8,128,128]{2,1,0:T(8,128)} %shard_map.107), calls=%async_computation.3 | async-start | bytes 1048576 | tf_op jit(solution)/shard_map/all_to_all | solution.py:329
  90.9 4.7 %collective-permute-start.5 = (f32[8,128]{1,0:T(8,128)S(1)}, f32[8,128]{1,0:T(8,128)S(1)}, u32[]{:S(2)}, u32[]{:S(2)}) collective-permute-start(f32[8,128]{1,0:T(8,128)S(1)} %bitcast_reduce_fusion), channel_id=1, source_target_pairs={{0,256},{16,272},{32,288},{48,304},{64,320},{80,336},{96,352},{112... | collective-permute-start | bytes 12296 | tf_op jit(solution)/shard_map/ppermute | solution.py:378
  95.5 1.2 collective-permute-done.5
  96.7 3.1 %collective-permute-start.6 = (f32[8,128]{1,0:T(8,128)S(1)}, f32[8,128]{1,0:T(8,128)S(1)}, u32[]{:S(2)}, u32[]{:S(2)}) collective-permute-start(f32[8,128]{1,0:T(8,128)S(1)} %add.22), channel_id=1, source_target_pairs={{0,128},{16,144},{32,160},{48,176},{64,192},{80,208},{96,224},{112... | collective-permute-start | bytes 12296 | tf_op jit(solution)/shard_map/ppermute | solution.py:378
  99.8 7.0 %shard_map.108 = (bf16[128,2048]{1,0:T(8,128)(2,1)}, f32[128,2048]{1,0:T(8,128)}, f32[128,2048]{1,0:T(8,128)}) custom-call(s32[1,8]{1,0:T(1,128)S(1)} %copy-done.14, bf16[128,2048]{1,0:T(8,128)(2,1)} %bitcast.20, bf16[128,2048]{1,0:T(8,128)(2,1)} %bitcast.13, bf16[128,2048]{1,0:T(8,128)(2,1)} %get-tuple-element.36.qf.refs_2_, ...), custom_call_target="tpu_custom_call" | custom-call | flops 335544320 | bytes 7340032 | tf_op jit(solution)/shard_map/pallas_call | solution.py:379
  106.9 0.6 shard_map.109
  107.6 20.6 %all_to_all.33.coming = f32[8,136,128]{2,1,0:T(8,128)S(1)} all-to-all(f32[8,136,128]{2,1,0:T(8,128)S(1)} %shard_map.109), channel_id=1, replica_groups={{0,2,4,6,8,10,12,14},{1,3,5,7,9,11,13,15},{16,18,20,22,24,26,28,30},{17..., dimensions={0} | all-to-all | bytes 1114112 | tf_op jit(solution)/shard_map/all_to_all | solution.py:329
  128.2 0.7 shard_map.110
  128.8 7.2 %collective-permute-start.7 = (f32[1032,128]{1,0:T(8,128)S(1)}, f32[1032,128]{1,0:T(8,128)S(1)}, u32[]{:S(2)}, u32[]{:S(2)}) collective-permute-start(f32[1032,128]{1,0:T(8,128)S(1)} %shard_map.110), channel_id=1, source_target_pairs={{0,1},{1,0},{2,3},{3,2},{4,5},{5,4},{6,7},{7,6},{8,9},{9,8},{10,11... | collective-permute-start | bytes 1585160 | tf_op jit(solution)/shard_map/ppermute | solution.py:326
  136.1 1.5 %collective-permute-done.7.ready = f32[1032,128]{1,0:T(8,128)S(1)} collective-permute-done((f32[1032,128]{1,0:T(8,128)S(1)}, f32[1032,128]{1,0:T(8,128)S(1)}, u32[]{:S(2)}, u32[]{:S(2)}) %collective-permute-start.7) | collective-permute-done | bytes 528416 | tf_op jit(solution)/shard_map/ppermute | solution.py:326
  137.6 2.5 %shard_map.111 = (bf16[128,2048]{1,0:T(8,128)(2,1)}, bf16[128,2048]{1,0:T(8,128)(2,1)}, f32[1,64]{1,0:T(1,128)}) custom-call(s32[1,8]{1,0:T(1,128)S(1)} %copy-done.14, bf16[128,2048]{1,0:T(8,128)(2,1)S(1)} %bitcast.19, bf16[128,2048]{1,0:T(8,128)(2,1)S(1)} %bitcast.16, bf16[128,2048]{1,0:T(8,128)(2,1)S(1)} %copy-done.5, f32[128,2048]{1,0:T(8,128)S(1)} %copy-done.8, ...), custom_call_target="tpu_custom_call" | custom-call | flops 134217728 | bytes 5242880 | tf_op jit(solution)/shard_map/pallas_call | solution.py:399
  (43 shorter events, 2.2 us)
Async XLA Ops:
  0.6 0.7 copy-start.14
  1.3 1.0 copy-start
  2.3 1.0 copy-start.3
  4.5 14.1 %collective-permute-start = (f32[8,128,128]{2,1,0:T(8,128)S(1)}, f32[8,128,128]{2,1,0:T(8,128)S(1)}, u32[]{:S(2)}, u32[]{:S(2)}) collective-permute-start(f32[8,128,128]{2,1,0:T(8,128)S(1)} %get-tuple-element.34), channel_id=1, source_target_pairs={{0,1},{1,0},{2,3},{3,2},{4,5},{5,4},{6,7},{7,6},{8,9},{9,8},{10,11... | collective-permute-start | bytes 1572872 | tf_op jit(solution)/shard_map/ppermute | solution.py:326
  13.4 0.7 copy-start.15
  14.2 4.3 %collective-permute-start.1 = (f32[8,128]{1,0:T(8,128)S(1)}, f32[8,128]{1,0:T(8,128)S(1)}, u32[]{:S(2)}, u32[]{:S(2)}) collective-permute-start(f32[8,128]{1,0:T(8,128)S(1)} %and_select_fusion), channel_id=1, source_target_pairs={{0,128},{16,144},{32,160},{48,176},{64,192},{80,208},{96,224},{112... | collective-permute-start | bytes 12296 | tf_op jit(solution)/shard_map/ppermute | solution.py:337
  18.6 10.9 %copy-start.6 = (bf16[1,128,2048]{2,1,0:T(8,128)(2,1)S(1)}, bf16[1,128,2048]{2,1,0:T(8,128)(2,1)}, u32[]{:S(2)}) copy-start(bf16[1,128,2048]{2,1,0:T(8,128)(2,1)} %param.6) | copy-start | bytes 1572868
  20.0 9.5 %copy-start.1 = (bf16[1,128,2048]{2,1,0:T(8,128)(2,1)S(1)}, bf16[1,128,2048]{2,1,0:T(8,128)(2,1)}, u32[]{:S(2)}) copy-start(bf16[1,128,2048]{2,1,0:T(8,128)(2,1)} %param.8) | copy-start | bytes 1572868
  20.0 9.5 %copy-start.4 = (bf16[1,128,2048]{2,1,0:T(8,128)(2,1)S(1)}, bf16[1,128,2048]{2,1,0:T(8,128)(2,1)}, u32[]{:S(2)}) copy-start(bf16[1,128,2048]{2,1,0:T(8,128)(2,1)} %param.7) | copy-start | bytes 1572868
  20.0 21.3 %all-to-all-start = ((f32[8,128,128]{2,1,0:T(8,128)}), f32[8,128,128]{2,1,0:T(8,128)S(1)}, u32[]{:S(2)}, u32[]{:S(2)}) async-start(f32[8,128,128]{2,1,0:T(8,128)} %shard_map.102), calls=%async_computation | async-start | bytes 1048576 | tf_op jit(solution)/shard_map/all_to_all | solution.py:329
  24.8 16.5 %collective-permute-start.2 = (f32[8,128]{1,0:T(8,128)S(1)}, f32[8,128]{1,0:T(8,128)S(1)}, u32[]{:S(2)}, u32[]{:S(2)}) collective-permute-start(f32[8,128]{1,0:T(8,128)S(1)} %fusion.1), channel_id=1, source_target_pairs={{0,0},{257,1},{18,2},{275,3},{36,4},{293,5},{54,6},{311,7},{72,8},... | collective-permute-start | bytes 12296 | tf_op jit(solution)/shard_map/ppermute | solution.py:349
  42.0 27.3 %copy-start.11 = (bf16[1,128,2048]{2,1,0:T(8,128)(2,1)S(1)}, bf16[1,128,2048]{2,1,0:T(8,128)(2,1)}, u32[]{:S(2)}) copy-start(bf16[1,128,2048]{2,1,0:T(8,128)(2,1)} %param.9) | copy-start | bytes 1572868
  64.4 4.8 %copy-start.7 = (bf16[128,2048]{1,0:T(8,128)(2,1)S(1)}, bf16[128,2048]{1,0:T(8,128)(2,1)}, u32[]{:S(2)}) copy-start(bf16[128,2048]{1,0:T(8,128)(2,1)} %get-tuple-element.36.qf.refs_2_) | copy-start | bytes 1572868
  64.4 4.8 %copy-start.10 = (f32[128,2048]{1,0:T(8,128)S(1)}, f32[128,2048]{1,0:T(8,128)}, u32[]{:S(2)}) copy-start(f32[128,2048]{1,0:T(8,128)} %get-tuple-element.37.intra) | copy-start | bytes 3145732
  65.1 4.2 %collective-permute-start.3 = (f32[1088,128]{1,0:T(8,128)S(1)}, f32[1088,128]{1,0:T(8,128)S(1)}, u32[]{:S(2)}, u32[]{:S(2)}) collective-permute-start(f32[1088,128]{1,0:T(8,128)S(1)} %shard_map.105), channel_id=1, source_target_pairs={{0,1},{1,0},{2,3},{3,2},{4,5},{5,4},{6,7},{7,6},{8,9},{9,8},{10,11... | collective-permute-start | bytes 1671176 | tf_op jit(solution)/shard_map/ppermute | solution.py:326
  72.1 0.8 copy-start.13
  72.9 9.0 %copy-start.12 = (bf16[128,2048]{1,0:T(8,128)(2,1)}, bf16[128,2048]{1,0:T(8,128)(2,1)S(1)}, u32[]{:S(2)}) copy-start(bf16[128,2048]{1,0:T(8,128)(2,1)S(1)} %get-tuple-element.49.refs_5_) | copy-start | bytes 1572868
  72.9 7.6 %collective-permute-start.4 = (f32[8,128,128]{2,1,0:T(8,128)}, f32[8,128,128]{2,1,0:T(8,128)S(1)}, u32[]{:S(2)}, u32[]{:S(2)}) collective-permute-start(f32[8,128,128]{2,1,0:T(8,128)} %get-tuple-element.44), channel_id=1, source_target_pairs={{0,1},{1,0},{2,3},{3,2},{4,5},{5,4},{6,7},{7,6},{8,9},{9,8},{10,11... | collective-permute-start | bytes 1572872 | tf_op jit(solution)/shard_map/ppermute | solution.py:326
  75.2 12.2 %all-to-all-start.2 = ((f32[8,8,128]{2,1,0:T(8,128)}), f32[8,8,128]{2,1,0:T(8,128)S(1)}, u32[]{:S(2)}, u32[]{:S(2)}) async-start(f32[8,8,128]{2,1,0:T(8,128)} %bitcast.5), calls=%async_computation.2 | async-start | bytes 65536 | tf_op jit(solution)/shard_map/all_to_all | solution.py:371
  87.4 19.5 %all-to-all-start.3 = ((f32[8,128,128]{2,1,0:T(8,128)}), f32[8,128,128]{2,1,0:T(8,128)S(1)}, u32[]{:S(2)}, u32[]{:S(2)}) async-start(f32[8,128,128]{2,1,0:T(8,128)} %shard_map.107), calls=%async_computation.3 | async-start | bytes 1048576 | tf_op jit(solution)/shard_map/all_to_all | solution.py:329
  90.9 5.9 %collective-permute-start.5 = (f32[8,128]{1,0:T(8,128)S(1)}, f32[8,128]{1,0:T(8,128)S(1)}, u32[]{:S(2)}, u32[]{:S(2)}) collective-permute-start(f32[8,128]{1,0:T(8,128)S(1)} %bitcast_reduce_fusion), channel_id=1, source_target_pairs={{0,256},{16,272},{32,288},{48,304},{64,320},{80,336},{96,352},{112... | collective-permute-start | bytes 12296 | tf_op jit(solution)/shard_map/ppermute | solution.py:378
  96.7 10.1 %collective-permute-start.6 = (f32[8,128]{1,0:T(8,128)S(1)}, f32[8,128]{1,0:T(8,128)S(1)}, u32[]{:S(2)}, u32[]{:S(2)}) collective-permute-start(f32[8,128]{1,0:T(8,128)S(1)} %add.22), channel_id=1, source_target_pairs={{0,128},{16,144},{32,160},{48,176},{64,192},{80,208},{96,224},{112... | collective-permute-start | bytes 12296 | tf_op jit(solution)/shard_map/ppermute | solution.py:378
  106.9 30.7 %copy-start.9 = (f32[128,2048]{1,0:T(8,128)S(1)}, f32[128,2048]{1,0:T(8,128)}, u32[]{:S(2)}) copy-start(f32[128,2048]{1,0:T(8,128)} %get-tuple-element.55.dv_part) | copy-start | bytes 3145732
  107.5 30.1 %copy-start.8 = (f32[128,2048]{1,0:T(8,128)S(1)}, f32[128,2048]{1,0:T(8,128)}, u32[]{:S(2)}) copy-start(f32[128,2048]{1,0:T(8,128)} %get-tuple-element.54.dk_part) | copy-start | bytes 3145732
  128.2 9.4 %copy-start.2 = (bf16[1,128,2048]{2,1,0:T(8,128)(2,1)S(1)}, bf16[1,128,2048]{2,1,0:T(8,128)(2,1)}, u32[]{:S(2)}) copy-start(bf16[1,128,2048]{2,1,0:T(8,128)(2,1)} %param.8) | copy-start | bytes 1572868
  128.2 9.4 %copy-start.5 = (bf16[128,2048]{1,0:T(8,128)(2,1)S(1)}, bf16[128,2048]{1,0:T(8,128)(2,1)}, u32[]{:S(2)}) copy-start(bf16[128,2048]{1,0:T(8,128)(2,1)} %get-tuple-element.47.refs_3_.kf) | copy-start | bytes 1572868
  128.8 8.7 %collective-permute-start.7 = (f32[1032,128]{1,0:T(8,128)S(1)}, f32[1032,128]{1,0:T(8,128)S(1)}, u32[]{:S(2)}, u32[]{:S(2)}) collective-permute-start(f32[1032,128]{1,0:T(8,128)S(1)} %shard_map.110), channel_id=1, source_target_pairs={{0,1},{1,0},{2,3},{3,2},{4,5},{5,4},{6,7},{7,6},{8,9},{9,8},{10,11... | collective-permute-start | bytes 1585160 | tf_op jit(solution)/shard_map/ppermute | solution.py:326

commit v6 on v5

--- a/solution.py
+++ b/solution.py
@@ -371,11 +371,16 @@
     gathered = lax.all_to_all(terms, "dp", 0, 0, axis_index_groups=lines, tiled=True)
     recv3 = other(give3)
     (chip3,) = call(join_back_body, [(half_states, F32)], 3, 1 << 18, 3 << 19)(starts, keep3, recv3)
-    chip3, gathered, after3 = lax.optimization_barrier((chip3, gathered, starts))
+    chip3, gathered = lax.optimization_barrier((chip3, gathered))
     parts3 = across(chip3)
     total = jnp.sum(gathered.reshape(CHIPS, 8, FEAT), axis=0)
     for step in (2 * CHIPS, CHIPS):
         total = total + lax.ppermute(total, "dp", [(i, i ^ step) for i in range(4 * CHIPS)])
+    (suffix,) = call(
+        scan_back_body, [((CHIPS, FEAT + 8, FEAT), F32)], 3, 1 << 18, 1 << 20
+    )(starts, parts3, total)
+    suffix, after4 = lax.optimization_barrier((suffix, starts))
+    coming4 = across(suffix)
     dq, dk_part, dv_part = call(
         grads_body, [(wide, BF16), (wide, F32), (wide, F32)], 8, 80 * mm, 7 << 20, 1 << 18,
         far=True, far_in=range(1, 8),
@@ -384,14 +389,10 @@
         + [pltpu.VMEM(wide, F32)] * 2
         + [pltpu.SemaphoreType.DMA((40,))],
     )(
-        after3,
+        after4,
         *(pltpu.with_memory_space_constraint(x, pltpu.HBM) for x in (q, v, qf, kf, scores, dn, inb)),
     )
-    parts3, dk_part = lax.optimization_barrier((parts3, dk_part))
-    (suffix,) = call(
-        scan_back_body, [((CHIPS, FEAT + 8, FEAT), F32)], 3, 1 << 18, 1 << 20
-    )(starts, parts3, total)
-    coming4 = across(suffix)
+    coming4, dk_part = lax.optimization_barrier((coming4, dk_part))
     (send4,) = call(
         give_back_body, [((HALF * FEAT + 8, FEAT), F32)], 3, 1 << 18, 3 << 19
     )(starts, keep3, coming4)

time: 141 us -> 141 us (level)
  blocking collectives: 43.1 us -> 22.5 us
  waiting for transfers between devices: 20 us -> 36 us
  local copies, waits for them, and re-layouts: 4.22 us -> 7.46 us
    all_to_all x2 -> x1, blocking collectives: 43.1 us -> 22.5 us  [across(): return lax.all_to_all(x, 'seq', 0, 0, axis_index_groups=zgroups, tiled=True)]
    all_to_all x2 -> x3, waiting for transfers between devices: 7.82 us -> 22.3 us  [across(): return lax.all_to_all(x, 'seq', 0, 0, axis_index_groups=zgroups, tiled=True)]
    all_to_all x2 -> x3, starting transfers between devices: 8.29 us -> 11.8 us  [across(): return lax.all_to_all(x, 'seq', 0, 0, axis_index_groups=zgroups, tiled=True)]
    unnamed x32, local copies, waits for them, and re-layouts: 4.22 us -> 7.46 us
    ppermute x4, starting transfers between devices: 20.9 us -> 18.6 us  [other(): return lax.ppermute(x, 'seq', swap)]
    ppermute x2, waiting for transfers between devices: 1.2 us -> 2.72 us  [shards(): lax.ppermute(total, 'dp', [(i, i ^ step) for i in range(4 * CHIPS)])]
  transfers between devices with their start and end apart: 11 -> 12, of which waited for: 6 -> 9; matrix products, arithmetic and copies ran while one was open for 0% -> 0% of each run, Pallas kernels for 9% -> 9%
where the time goes in v6:
time: 141 us; the launch traced here: 140 us
  starting transfers between devices  50.1 us (36%)
  waiting for transfers between devices  36 us (26%)
  Pallas kernels  23.4 us (17%)
  blocking collectives  22.5 us (16%)
  local copies, waits for them, and re-layouts  7.46 us (5%)
    all_to_all x1, blocking collectives, across(): return lax.all_to_all(x, 'seq', 0, 0, axis_index_groups=zgroups, tiled=True)  22.5 us
    all_to_all x3, waiting for transfers between devices, across(): return lax.all_to_all(x, 'seq', 0, 0, axis_index_groups=zgroups, tiled=True)  22.3 us
    ppermute x4, starting transfers between devices, other(): return lax.ppermute(x, 'seq', swap)  18.6 us
    all_to_all x3, starting transfers between devices, across(): return lax.all_to_all(x, 'seq', 0, 0, axis_index_groups=zgroups, tiled=True)  11.8 us
    ppermute x2, starting transfers between devices, shards(): lax.ppermute(total, 'dp', [(i, i ^ step) for i in range(4 * CHIPS)])  7.76 us
    unnamed x32, local copies, waits for them, and re-layouts  7.46 us
    pallas_call x1, Pallas kernels, shards(): call(grads_body, [(wide, BF16), (wide, F32), (wide, F32)], 8, 80 * mm, 7...  7.01 us
    all_to_all x1, waiting for transfers between devices, shards(): lax.all_to_all(terms, 'dp', 0, 0, axis_index_groups=lines, tiled=True)  5.45 us
  transfers between devices with their start and end apart: 12, of which 9 were waited for; matrix products, arithmetic and copies ran while one was open for 0% of the time, Pallas kernels for 9%

profile of v6, /device:TPU:1, one launch (start us, length us, event | category | flops | bytes accessed | tf_op | source)
XLA Modules:
  0.0 140.5 jit_solution(4714776021505724604)
XLA Ops:
  3.4 1.1 shard_map.101
  4.5 8.8 %collective-permute-start = (f32[8,128,128]{2,1,0:T(8,128)S(1)}, f32[8,128,128]{2,1,0:T(8,128)S(1)}, u32[]{:S(2)}, u32[]{:S(2)}) collective-permute-start(f32[8,128,128]{2,1,0:T(8,128)S(1)} %get-tuple-element.35), channel_id=1, source_target_pairs={{0,1},{1,0},{2,3},{3,2},{4,5},{5,4},{6,7},{7,6},{8,9},{9,8},{10,11... | collective-permute-start | bytes 1572872 | tf_op jit(solution)/shard_map/ppermute | solution.py:326
  14.2 1.9 %collective-permute-start.1 = (f32[8,128]{1,0:T(8,128)S(1)}, f32[8,128]{1,0:T(8,128)S(1)}, u32[]{:S(2)}, u32[]{:S(2)}) collective-permute-start(f32[8,128]{1,0:T(8,128)S(1)} %and_select_fusion), channel_id=1, source_target_pairs={{0,128},{16,144},{32,160},{48,176},{64,192},{80,208},{96,224},{112... | collective-permute-start | bytes 12296 | tf_op jit(solution)/shard_map/ppermute | solution.py:337
  16.1 2.4 %collective-permute-done.1 = f32[8,128]{1,0:T(8,128)S(1)} collective-permute-done((f32[8,128]{1,0:T(8,128)S(1)}, f32[8,128]{1,0:T(8,128)S(1)}, u32[]{:S(2)}, u32[]{:S(2)}) %collective-permute-start.1) | collective-permute-done | bytes 4128 | tf_op jit(solution)/shard_map/ppermute | solution.py:337
  18.6 1.4 %shard_map.102 = f32[8,128,128]{2,1,0:T(8,128)} custom-call(s32[1,8]{1,0:T(1,128)S(1)} %copy-done.14, f32[8,128,128]{2,1,0:T(8,128)S(1)} %get-tuple-element.34.keep, f32[8,128,128]{2,1,0:T(8,128)S(1)} %collective-permute-done.recv.theirs), custom_call_target="tpu_custom_call" | custom-call | flops 262144 | bytes 1572864 | tf_op jit(solution)/shard_map/pallas_call | solution.py:342
  20.0 4.8 %all-to-all-start = ((f32[8,128,128]{2,1,0:T(8,128)}), f32[8,128,128]{2,1,0:T(8,128)S(1)}, u32[]{:S(2)}, u32[]{:S(2)}) async-start(f32[8,128,128]{2,1,0:T(8,128)} %shard_map.102), calls=%async_computation | async-start | bytes 1048576 | tf_op jit(solution)/shard_map/all_to_all | solution.py:329
  24.8 4.6 %collective-permute-start.2 = (f32[8,128]{1,0:T(8,128)S(1)}, f32[8,128]{1,0:T(8,128)S(1)}, u32[]{:S(2)}, u32[]{:S(2)}) collective-permute-start(f32[8,128]{1,0:T(8,128)S(1)} %fusion.1), channel_id=1, source_target_pairs={{0,0},{257,1},{18,2},{275,3},{36,4},{293,5},{54,6},{311,7},{72,8},... | collective-permute-start | bytes 12296 | tf_op jit(solution)/shard_map/ppermute | solution.py:349
  29.5 4.0 %shard_map.103 = (bf16[128,2048]{1,0:T(8,128)(2,1)}, bf16[128,2048]{1,0:T(8,128)(2,1)}, bf16[128,2048]{1,0:T(8,128)(2,1)}, f32[128,2048]{1,0:T(8,128)}) custom-call(s32[1,8]{1,0:T(1,128)S(1)} %copy-done.14, bf16[128,2048]{1,0:T(8,128)(2,1)S(1)} %bitcast.21, bf16[128,2048]{1,0:T(8,128)(2,1)S(1)} %bitcast.18, bf16[128,2048]{1,0:T(8,128)(2,1)S(1)} %bitcast.15), custom_call_target="tpu_custom_call" | custom-call | flops 134217728 | bytes 4194304 | tf_op jit(solution)/shard_map/pallas_call | solution.py:350
  33.5 7.8 %all-to-all-done.parts = f32[8,128,128]{2,1,0:T(8,128)S(1)} async-done(((f32[8,128,128]{2,1,0:T(8,128)}), f32[8,128,128]{2,1,0:T(8,128)S(1)}, u32[]{:S(2)}, u32[]{:S(2)}) %all-to-all-start) | async-done | bytes 524320 | tf_op jit(solution)/shard_map/all_to_all | solution.py:329
  42.0 22.5 %all_to_all.32.coming = f32[8,136,128]{2,1,0:T(8,128)S(1)} all-to-all(f32[8,136,128]{2,1,0:T(8,128)S(1)} %shard_map.104), channel_id=1, replica_groups={{0,2,4,6,8,10,12,14},{1,3,5,7,9,11,13,15},{16,18,20,22,24,26,28,30},{17..., dimensions={0} | all-to-all | bytes 1114112 | tf_op jit(solution)/shard_map/all_to_all | solution.py:329
  65.1 2.6 %collective-permute-start.3 = (f32[1088,128]{1,0:T(8,128)S(1)}, f32[1088,128]{1,0:T(8,128)S(1)}, u32[]{:S(2)}, u32[]{:S(2)}) collective-permute-start(f32[1088,128]{1,0:T(8,128)S(1)} %shard_map.105), channel_id=1, source_target_pairs={{0,1},{1,0},{2,3},{3,2},{4,5},{5,4},{6,7},{7,6},{8,9},{9,8},{10,11... | collective-permute-start | bytes 1671176 | tf_op jit(solution)/shard_map/ppermute | solution.py:326
  67.7 1.6 %collective-permute-done.3.ready = f32[1088,128]{1,0:T(8,128)S(1)} collective-permute-done((f32[1088,128]{1,0:T(8,128)S(1)}, f32[1088,128]{1,0:T(8,128)S(1)}, u32[]{:S(2)}, u32[]{:S(2)}) %collective-permute-start.3) | collective-permute-done | bytes 557088 | tf_op jit(solution)/shard_map/ppermute | solution.py:326
  69.3 2.6 %shard_map.106 = (bf16[128,2048]{1,0:T(8,128)(2,1)}, bf16[128,2048]{1,0:T(8,128)(2,1)S(1)}, bf16[16,128,128]{2,1,0:T(8,128)(2,1)S(1)}, f32[8,128,128]{2,1,0:T(8,...) custom-call(s32[1,8]{1,0:T(1,128)S(1)} %copy-done.14, bf16[128,2048]{1,0:T(8,128)(2,1)S(1)} %copy-done.7, ...), custom_call_target="tpu_custom_call" | custom-call | flops 134217728 | bytes 5242880 | tf_op jit(solution)/shard_map/pallas_call | solution.py:363
  73.4 2.3 %collective-permute-start.4 = (f32[8,128,128]{2,1,0:T(8,128)S(1)}, f32[8,128,128]{2,1,0:T(8,128)S(1)}, u32[]{:S(2)}, u32[]{:S(2)}) collective-permute-start(f32[8,128,128]{2,1,0:T(8,128)S(1)} %get-tuple-element.45), channel_id=1, source_target_pairs={{0,1},{1,0},{2,3},{3,2},{4,5},{5,4},{6,7},{7,6},{8,9},{9,8},{10,11... | collective-permute-start | bytes 1572872 | tf_op jit(solution)/shard_map/ppermute | solution.py:326
  75.7 5.3 %all-to-all-start.2 = ((f32[8,8,128]{2,1,0:T(8,128)}), f32[8,8,128]{2,1,0:T(8,128)S(1)}, u32[]{:S(2)}, u32[]{:S(2)}) async-start(f32[8,8,128]{2,1,0:T(8,128)} %bitcast.5), calls=%async_computation.2 | async-start | bytes 65536 | tf_op jit(solution)/shard_map/all_to_all | solution.py:371
  81.1 1.4 %shard_map.107 = f32[8,128,128]{2,1,0:T(8,128)} custom-call(s32[1,8]{1,0:T(1,128)S(1)} %copy-done.14, f32[8,128,128]{2,1,0:T(8,128)S(1)} %get-tuple-element.44.keep, f32[8,128,128]{2,1,0:T(8,128)S(1)} %collective-permute-done.4.recv.theirs), custom_call_target="tpu_custom_call" | custom-call | flops 262144 | bytes 1572864 | tf_op jit(solution)/shard_map/pallas_call | solution.py:373
  82.5 5.4 %all-to-all-done.2 = f32[8,8,128]{2,1,0:T(8,128)S(1)} async-done(((f32[8,8,128]{2,1,0:T(8,128)}), f32[8,8,128]{2,1,0:T(8,128)S(1)}, u32[]{:S(2)}, u32[]{:S(2)}) %all-to-all-start.2) | async-done | bytes 32800 | tf_op jit(solution)/shard_map/all_to_all | solution.py:371
  87.9 3.5 %all-to-all-start.3 = ((f32[8,128,128]{2,1,0:T(8,128)}), f32[8,128,128]{2,1,0:T(8,128)S(1)}, u32[]{:S(2)}, u32[]{:S(2)}) async-start(f32[8,128,128]{2,1,0:T(8,128)} %shard_map.107), calls=%async_computation.3 | async-start | bytes 1048576 | tf_op jit(solution)/shard_map/all_to_all | solution.py:329
  91.4 4.7 %collective-permute-start.5 = (f32[8,128]{1,0:T(8,128)S(1)}, f32[8,128]{1,0:T(8,128)S(1)}, u32[]{:S(2)}, u32[]{:S(2)}) collective-permute-start(f32[8,128]{1,0:T(8,128)S(1)} %bitcast_reduce_fusion), channel_id=1, source_target_pairs={{0,256},{16,272},{32,288},{48,304},{64,320},{80,336},{96,352},{112... | collective-permute-start | bytes 12296 | tf_op jit(solution)/shard_map/ppermute | solution.py:378
  96.1 1.2 collective-permute-done.5
  97.3 3.1 %collective-permute-start.6 = (f32[8,128]{1,0:T(8,128)S(1)}, f32[8,128]{1,0:T(8,128)S(1)}, u32[]{:S(2)}, u32[]{:S(2)}) collective-permute-start(f32[8,128]{1,0:T(8,128)S(1)} %add.22), channel_id=1, source_target_pairs={{0,128},{16,144},{32,160},{48,176},{64,192},{80,208},{96,224},{112... | collective-permute-start | bytes 12296 | tf_op jit(solution)/shard_map/ppermute | solution.py:378
  100.4 1.5 %collective-permute-done.6 = f32[8,128]{1,0:T(8,128)S(1)} collective-permute-done((f32[8,128]{1,0:T(8,128)S(1)}, f32[8,128]{1,0:T(8,128)S(1)}, u32[]{:S(2)}, u32[]{:S(2)}) %collective-permute-start.6) | collective-permute-done | bytes 4128 | tf_op jit(solution)/shard_map/ppermute | solution.py:378
  101.9 5.5 %all-to-all-done.3.parts = f32[8,128,128]{2,1,0:T(8,128)S(1)} async-done(((f32[8,128,128]{2,1,0:T(8,128)}), f32[8,128,128]{2,1,0:T(8,128)S(1)}, u32[]{:S(2)}, u32[]{:S(2)}) %all-to-all-start.3) | async-done | bytes 524320 | tf_op jit(solution)/shard_map/all_to_all | solution.py:329
  107.4 1.5 %shard_map.108 = f32[8,136,128]{2,1,0:T(8,128)} custom-call(s32[1,8]{1,0:T(1,128)S(1)} %copy-done.14, f32[8,128,128]{2,1,0:T(8,128)S(1)} %all-to-all-done.3.parts, f32[8,128]{1,0:T(8,128)S(1)} %add.23.terms), custom_call_target="tpu_custom_call" | custom-call | flops 262144 | bytes 1048576 | tf_op jit(solution)/shard_map/pallas_call | solution.py:379
  108.9 3.5 %all-to-all-start.4 = ((f32[8,136,128]{2,1,0:T(8,128)}), f32[8,136,128]{2,1,0:T(8,128)S(1)}, u32[]{:S(2)}, u32[]{:S(2)}) async-start(f32[8,136,128]{2,1,0:T(8,128)} %shard_map.108), calls=%async_computation.4 | async-start | bytes 1114112 | tf_op jit(solution)/shard_map/all_to_all | solution.py:329
  112.4 7.0 %shard_map.109 = (bf16[128,2048]{1,0:T(8,128)(2,1)}, f32[128,2048]{1,0:T(8,128)}, f32[128,2048]{1,0:T(8,128)}) custom-call(s32[1,8]{1,0:T(1,128)S(1)} %copy-done.14, bf16[128,2048]{1,0:T(8,128)(2,1)} %bitcast.20, bf16[128,2048]{1,0:T(8,128)(2,1)} %bitcast.13, bf16[128,2048]{1,0:T(8,128)(2,1)} %get-tuple-element.37.qf.refs_2_, ...), custom_call_target="tpu_custom_call" | custom-call | flops 335544320 | bytes 7340032 | tf_op jit(solution)/shard_map/pallas_call | solution.py:384
  119.4 9.0 %all-to-all-done.4.coming = f32[8,136,128]{2,1,0:T(8,128)S(1)} async-done(((f32[8,136,128]{2,1,0:T(8,128)}), f32[8,136,128]{2,1,0:T(8,128)S(1)}, u32[]{:S(2)}, u32[]{:S(2)}) %all-to-all-start.4) | async-done | bytes 557088 | tf_op jit(solution)/shard_map/all_to_all | solution.py:329
  129.1 4.9 %collective-permute-start.7 = (f32[1032,128]{1,0:T(8,128)S(1)}, f32[1032,128]{1,0:T(8,128)S(1)}, u32[]{:S(2)}, u32[]{:S(2)}) collective-permute-start(f32[1032,128]{1,0:T(8,128)S(1)} %shard_map.110), channel_id=1, source_target_pairs={{0,1},{1,0},{2,3},{3,2},{4,5},{5,4},{6,7},{7,6},{8,9},{9,8},{10,11... | collective-permute-start | bytes 1585160 | tf_op jit(solution)/shard_map/ppermute | solution.py:326
  134.0 1.5 %collective-permute-done.7.ready = f32[1032,128]{1,0:T(8,128)S(1)} collective-permute-done((f32[1032,128]{1,0:T(8,128)S(1)}, f32[1032,128]{1,0:T(8,128)S(1)}, u32[]{:S(2)}, u32[]{:S(2)}) %collective-permute-start.7) | collective-permute-done | bytes 528416 | tf_op jit(solution)/shard_map/ppermute | solution.py:326
  135.6 1.2 copy-done.9
  136.8 1.2 copy-done.10
  138.0 2.5 %shard_map.111 = (bf16[128,2048]{1,0:T(8,128)(2,1)}, bf16[128,2048]{1,0:T(8,128)(2,1)}, f32[1,64]{1,0:T(1,128)}) custom-call(s32[1,8]{1,0:T(1,128)S(1)} %copy-done.14, bf16[128,2048]{1,0:T(8,128)(2,1)S(1)} %bitcast.19, bf16[128,2048]{1,0:T(8,128)(2,1)S(1)} %bitcast.16, bf16[128,2048]{1,0:T(8,128)(2,1)S(1)} %copy-done.5, f32[128,2048]{1,0:T(8,128)S(1)} %copy-done.9, ...), custom_call_target="tpu_custom_call" | custom-call | flops 134217728 | bytes 5242880 | tf_op jit(solution)/shard_map/pallas_call | solution.py:400
  (44 shorter events, 7.2 us)
Async XLA Ops:
  0.6 0.7 copy-start.14
  1.3 1.0 copy-start
  2.3 1.0 copy-start.3
  4.5 14.1 %collective-permute-start = (f32[8,128,128]{2,1,0:T(8,128)S(1)}, f32[8,128,128]{2,1,0:T(8,128)S(1)}, u32[]{:S(2)}, u32[]{:S(2)}) collective-permute-start(f32[8,128,128]{2,1,0:T(8,128)S(1)} %get-tuple-element.35), channel_id=1, source_target_pairs={{0,1},{1,0},{2,3},{3,2},{4,5},{5,4},{6,7},{7,6},{8,9},{9,8},{10,11... | collective-permute-start | bytes 1572872 | tf_op jit(solution)/shard_map/ppermute | solution.py:326
  13.4 0.7 copy-start.15
  14.2 4.3 %collective-permute-start.1 = (f32[8,128]{1,0:T(8,128)S(1)}, f32[8,128]{1,0:T(8,128)S(1)}, u32[]{:S(2)}, u32[]{:S(2)}) collective-permute-start(f32[8,128]{1,0:T(8,128)S(1)} %and_select_fusion), channel_id=1, source_target_pairs={{0,128},{16,144},{32,160},{48,176},{64,192},{80,208},{96,224},{112... | collective-permute-start | bytes 12296 | tf_op jit(solution)/shard_map/ppermute | solution.py:337
  18.6 10.9 %copy-start.6 = (bf16[1,128,2048]{2,1,0:T(8,128)(2,1)S(1)}, bf16[1,128,2048]{2,1,0:T(8,128)(2,1)}, u32[]{:S(2)}) copy-start(bf16[1,128,2048]{2,1,0:T(8,128)(2,1)} %param.6) | copy-start | bytes 1572868
  20.0 9.5 %copy-start.1 = (bf16[1,128,2048]{2,1,0:T(8,128)(2,1)S(1)}, bf16[1,128,2048]{2,1,0:T(8,128)(2,1)}, u32[]{:S(2)}) copy-start(bf16[1,128,2048]{2,1,0:T(8,128)(2,1)} %param.8) | copy-start | bytes 1572868
  20.0 9.5 %copy-start.4 = (bf16[1,128,2048]{2,1,0:T(8,128)(2,1)S(1)}, bf16[1,128,2048]{2,1,0:T(8,128)(2,1)}, u32[]{:S(2)}) copy-start(bf16[1,128,2048]{2,1,0:T(8,128)(2,1)} %param.7) | copy-start | bytes 1572868
  20.0 21.3 %all-to-all-start = ((f32[8,128,128]{2,1,0:T(8,128)}), f32[8,128,128]{2,1,0:T(8,128)S(1)}, u32[]{:S(2)}, u32[]{:S(2)}) async-start(f32[8,128,128]{2,1,0:T(8,128)} %shard_map.102), calls=%async_computation | async-start | bytes 1048576 | tf_op jit(solution)/shard_map/all_to_all | solution.py:329
  24.8 16.5 %collective-permute-start.2 = (f32[8,128]{1,0:T(8,128)S(1)}, f32[8,128]{1,0:T(8,128)S(1)}, u32[]{:S(2)}, u32[]{:S(2)}) collective-permute-start(f32[8,128]{1,0:T(8,128)S(1)} %fusion.1), channel_id=1, source_target_pairs={{0,0},{257,1},{18,2},{275,3},{36,4},{293,5},{54,6},{311,7},{72,8},... | collective-permute-start | bytes 12296 | tf_op jit(solution)/shard_map/ppermute | solution.py:349
  42.0 27.3 %copy-start.11 = (bf16[1,128,2048]{2,1,0:T(8,128)(2,1)S(1)}, bf16[1,128,2048]{2,1,0:T(8,128)(2,1)}, u32[]{:S(2)}) copy-start(bf16[1,128,2048]{2,1,0:T(8,128)(2,1)} %param.9) | copy-start | bytes 1572868
  64.4 4.8 %copy-start.7 = (bf16[128,2048]{1,0:T(8,128)(2,1)S(1)}, bf16[128,2048]{1,0:T(8,128)(2,1)}, u32[]{:S(2)}) copy-start(bf16[128,2048]{1,0:T(8,128)(2,1)} %get-tuple-element.37.qf.refs_2_) | copy-start | bytes 1572868
  64.4 4.8 %copy-start.8 = (f32[128,2048]{1,0:T(8,128)S(1)}, f32[128,2048]{1,0:T(8,128)}, u32[]{:S(2)}) copy-start(f32[128,2048]{1,0:T(8,128)} %get-tuple-element.38.intra) | copy-start | bytes 3145732
  65.1 4.2 %collective-permute-start.3 = (f32[1088,128]{1,0:T(8,128)S(1)}, f32[1088,128]{1,0:T(8,128)S(1)}, u32[]{:S(2)}, u32[]{:S(2)}) collective-permute-start(f32[1088,128]{1,0:T(8,128)S(1)} %shard_map.105), channel_id=1, source_target_pairs={{0,1},{1,0},{2,3},{3,2},{4,5},{5,4},{6,7},{7,6},{8,9},{9,8},{10,11... | collective-permute-start | bytes 1671176 | tf_op jit(solution)/shard_map/ppermute | solution.py:326
  71.8 0.8 copy-start.12
  72.6 0.8 copy-start.13
  73.4 7.6 %collective-permute-start.4 = (f32[8,128,128]{2,1,0:T(8,128)S(1)}, f32[8,128,128]{2,1,0:T(8,128)S(1)}, u32[]{:S(2)}, u32[]{:S(2)}) collective-permute-start(f32[8,128,128]{2,1,0:T(8,128)S(1)} %get-tuple-element.45), channel_id=1, source_target_pairs={{0,1},{1,0},{2,3},{3,2},{4,5},{5,4},{6,7},{7,6},{8,9},{9,8},{10,11... | collective-permute-start | bytes 1572872 | tf_op jit(solution)/shard_map/ppermute | solution.py:326
  75.7 12.2 %all-to-all-start.2 = ((f32[8,8,128]{2,1,0:T(8,128)}), f32[8,8,128]{2,1,0:T(8,128)S(1)}, u32[]{:S(2)}, u32[]{:S(2)}) async-start(f32[8,8,128]{2,1,0:T(8,128)} %bitcast.5), calls=%async_computation.2 | async-start | bytes 65536 | tf_op jit(solution)/shard_map/all_to_all | solution.py:371
  87.9 19.5 %all-to-all-start.3 = ((f32[8,128,128]{2,1,0:T(8,128)}), f32[8,128,128]{2,1,0:T(8,128)S(1)}, u32[]{:S(2)}, u32[]{:S(2)}) async-start(f32[8,128,128]{2,1,0:T(8,128)} %shard_map.107), calls=%async_computation.3 | async-start | bytes 1048576 | tf_op jit(solution)/shard_map/all_to_all | solution.py:329
  91.4 5.9 %collective-permute-start.5 = (f32[8,128]{1,0:T(8,128)S(1)}, f32[8,128]{1,0:T(8,128)S(1)}, u32[]{:S(2)}, u32[]{:S(2)}) collective-permute-start(f32[8,128]{1,0:T(8,128)S(1)} %bitcast_reduce_fusion), channel_id=1, source_target_pairs={{0,256},{16,272},{32,288},{48,304},{64,320},{80,336},{96,352},{112... | collective-permute-start | bytes 12296 | tf_op jit(solution)/shard_map/ppermute | solution.py:378
  97.3 4.6 %collective-permute-start.6 = (f32[8,128]{1,0:T(8,128)S(1)}, f32[8,128]{1,0:T(8,128)S(1)}, u32[]{:S(2)}, u32[]{:S(2)}) collective-permute-start(f32[8,128]{1,0:T(8,128)S(1)} %add.22), channel_id=1, source_target_pairs={{0,128},{16,144},{32,160},{48,176},{64,192},{80,208},{96,224},{112... | collective-permute-start | bytes 12296 | tf_op jit(solution)/shard_map/ppermute | solution.py:378
  108.9 19.6 %all-to-all-start.4 = ((f32[8,136,128]{2,1,0:T(8,128)}), f32[8,136,128]{2,1,0:T(8,128)S(1)}, u32[]{:S(2)}, u32[]{:S(2)}) async-start(f32[8,136,128]{2,1,0:T(8,128)} %shard_map.108), calls=%async_computation.4 | async-start | bytes 1114112 | tf_op jit(solution)/shard_map/all_to_all | solution.py:329
  128.4 7.1 %copy-start.2 = (bf16[1,128,2048]{2,1,0:T(8,128)(2,1)S(1)}, bf16[1,128,2048]{2,1,0:T(8,128)(2,1)}, u32[]{:S(2)}) copy-start(bf16[1,128,2048]{2,1,0:T(8,128)(2,1)} %param.8) | copy-start | bytes 1572868
  128.4 7.1 %copy-start.5 = (bf16[128,2048]{1,0:T(8,128)(2,1)S(1)}, bf16[128,2048]{1,0:T(8,128)(2,1)}, u32[]{:S(2)}) copy-start(bf16[128,2048]{1,0:T(8,128)(2,1)} %get-tuple-element.50.refs_3_.kf) | copy-start | bytes 1572868
  129.1 6.5 %collective-permute-start.7 = (f32[1032,128]{1,0:T(8,128)S(1)}, f32[1032,128]{1,0:T(8,128)S(1)}, u32[]{:S(2)}, u32[]{:S(2)}) collective-permute-start(f32[1032,128]{1,0:T(8,128)S(1)} %shard_map.110), channel_id=1, source_target_pairs={{0,1},{1,0},{2,3},{3,2},{4,5},{5,4},{6,7},{7,6},{8,9},{9,8},{10,11... | collective-permute-start | bytes 1585160 | tf_op jit(solution)/shard_map/ppermute | solution.py:326
  135.6 1.2 copy-start.9
  136.8 1.2 copy-start.10

commit v7 on v6

--- a/solution.py
+++ b/solution.py
@@ -286,10 +286,22 @@
 
 
 def last_body(
-    starts, k, v, kf, dk_part, dv_part, theirs, coming, ready,
-    dk_out, dv_out, gain_out,
+    starts, k, v, kf, dk_far, dv_far, theirs, coming, ready,
+    dk_out, dv_out, gain_out, dk_part, dv_part, sems,
 ):
     idx, core = place()
+    fetches = []
+    for g in range(2):
+        these = []
+        for n, side in enumerate((core, 1 - core)):
+            at = pl.ds(pl.multiple_of((side * HALF + 4 * g) * FEAT, 4 * FEAT), 4 * FEAT)
+            for m, (src, dst) in enumerate(((dk_far, dk_part), (dv_far, dv_part))):
+                these.append(
+                    pltpu.make_async_copy(src.at[:, at], dst.at[:, at], sems.at[4 * g + 2 * n + m])
+                )
+        for c in these:
+            c.start()
+        fetches.append(these)
     last = leaves(starts, idx)
     flag = carry_of(starts, idx - core + 1)
     a = jnp.where(core == 0, 1.0, 0.0)
@@ -297,6 +309,9 @@
     gsum = ready[HALF * FEAT :]
     for j in range(HALF):
         gsum = gsum + coming[j, FEAT:]
+        if j % 4 == 0:
+            for c in fetches[j // 4]:
+                c.wait()
         for mine, side in ((True, core), (False, 1 - core)):
             at = cols(side * HALF + j)
             if mine:
@@ -398,8 +413,13 @@
     )(starts, keep3, coming4)
     ready4 = other(send4)
     dk, dv, gain_grad = call(
-        last_body, [(wide, BF16)] * 2 + [((1, 64), F32)], 9, 32 * mm, 5 << 20, 1 << 18
-    )(starts, k, v, kf, dk_part, dv_part, recv3, coming4, ready4)
+        last_body, [(wide, BF16)] * 2 + [((1, 64), F32)], 9, 32 * mm, 5 << 20, 1 << 18,
+        far_in=(4, 5), scratch=[pltpu.VMEM(wide, F32)] * 2 + [pltpu.SemaphoreType.DMA((8,))],
+    )(
+        starts, k, v, kf,
+        *(pltpu.with_memory_space_constraint(x, pltpu.HBM) for x in (dk_part, dv_part)),
+        recv3, coming4, ready4,
+    )
     full = (1, TOK, HEADS * FEAT)
     return (
         att.reshape(full),

time: 141 us -> 140 us (level)
  local copies, waits for them, and re-layouts: 7.46 us -> 4.99 us
    unnamed x32 -> x28, local copies, waits for them, and re-layouts: 7.46 us -> 4.99 us
where the time goes in v7:
time: 140 us; the launch traced here: 139 us
  starting transfers between devices  50.1 us (36%)
  waiting for transfers between devices  36 us (26%)
  Pallas kernels  24.7 us (18%)
  blocking collectives  22.5 us (16%)
  local copies, waits for them, and re-layouts  4.99 us (4%)
    all_to_all x1, blocking collectives, across(): return lax.all_to_all(x, 'seq', 0, 0, axis_index_groups=zgroups, tiled=True)  22.5 us
    all_to_all x3, waiting for transfers between devices, across(): return lax.all_to_all(x, 'seq', 0, 0, axis_index_groups=zgroups, tiled=True)  22.3 us
    ppermute x4, starting transfers between devices, other(): return lax.ppermute(x, 'seq', swap)  18.6 us
    all_to_all x3, starting transfers between devices, across(): return lax.all_to_all(x, 'seq', 0, 0, axis_index_groups=zgroups, tiled=True)  11.8 us
    ppermute x2, starting transfers between devices, shards(): lax.ppermute(total, 'dp', [(i, i ^ step) for i in range(4 * CHIPS)])  7.76 us
    pallas_call x1, Pallas kernels, shards(): call(grads_body, [(wide, BF16), (wide, F32), (wide, F32)], 8, 80 * mm, 7...  7 us
    all_to_all x1, waiting for transfers between devices, shards(): lax.all_to_all(terms, 'dp', 0, 0, axis_index_groups=lines, tiled=True)  5.45 us
    all_to_all x1, starting transfers between devices, shards(): lax.all_to_all(terms, 'dp', 0, 0, axis_index_groups=lines, tiled=True)  5.3 us
  transfers between devices with their start and end apart: 12, of which 9 were waited for; matrix products, arithmetic and copies ran while one was open for 0% of the time, Pallas kernels for 9%

profile of v7, /device:TPU:1, one launch (start us, length us, event | category | flops | bytes accessed | tf_op | source)
XLA Modules:
  0.0 139.3 jit_solution(10352423552135367718)
XLA Ops:
  1.3 1.0 copy-done
  2.3 1.0 copy-done.3
  3.4 1.1 shard_map.101
  4.5 8.8 %collective-permute-start = (f32[8,128,128]{2,1,0:T(8,128)S(1)}, f32[8,128,128]{2,1,0:T(8,128)S(1)}, u32[]{:S(2)}, u32[]{:S(2)}) collective-permute-start(f32[8,128,128]{2,1,0:T(8,128)S(1)} %get-tuple-element.35), channel_id=1, source_target_pairs={{0,1},{1,0},{2,3},{3,2},{4,5},{5,4},{6,7},{7,6},{8,9},{9,8},{10,11... | collective-permute-start | bytes 1572872 | tf_op jit(solution)/shard_map/ppermute | solution.py:341
  14.2 1.9 %collective-permute-start.1 = (f32[8,128]{1,0:T(8,128)S(1)}, f32[8,128]{1,0:T(8,128)S(1)}, u32[]{:S(2)}, u32[]{:S(2)}) collective-permute-start(f32[8,128]{1,0:T(8,128)S(1)} %and_select_fusion), channel_id=1, source_target_pairs={{0,128},{16,144},{32,160},{48,176},{64,192},{80,208},{96,224},{112... | collective-permute-start | bytes 12296 | tf_op jit(solution)/shard_map/ppermute | solution.py:352
  16.1 2.4 %collective-permute-done.1 = f32[8,128]{1,0:T(8,128)S(1)} collective-permute-done((f32[8,128]{1,0:T(8,128)S(1)}, f32[8,128]{1,0:T(8,128)S(1)}, u32[]{:S(2)}, u32[]{:S(2)}) %collective-permute-start.1) | collective-permute-done | bytes 4128 | tf_op jit(solution)/shard_map/ppermute | solution.py:352
  18.6 1.4 %shard_map.102 = f32[8,128,128]{2,1,0:T(8,128)} custom-call(s32[1,8]{1,0:T(1,128)S(1)} %copy-done.12, f32[8,128,128]{2,1,0:T(8,128)S(1)} %get-tuple-element.34.keep, f32[8,128,128]{2,1,0:T(8,128)S(1)} %collective-permute-done.recv.theirs), custom_call_target="tpu_custom_call" | custom-call | flops 262144 | bytes 1572864 | tf_op jit(solution)/shard_map/pallas_call | solution.py:357
  20.0 4.8 %all-to-all-start = ((f32[8,128,128]{2,1,0:T(8,128)}), f32[8,128,128]{2,1,0:T(8,128)S(1)}, u32[]{:S(2)}, u32[]{:S(2)}) async-start(f32[8,128,128]{2,1,0:T(8,128)} %shard_map.102), calls=%async_computation | async-start | bytes 1048576 | tf_op jit(solution)/shard_map/all_to_all | solution.py:344
  24.8 4.6 %collective-permute-start.2 = (f32[8,128]{1,0:T(8,128)S(1)}, f32[8,128]{1,0:T(8,128)S(1)}, u32[]{:S(2)}, u32[]{:S(2)}) collective-permute-start(f32[8,128]{1,0:T(8,128)S(1)} %fusion.1), channel_id=1, source_target_pairs={{0,0},{257,1},{18,2},{275,3},{36,4},{293,5},{54,6},{311,7},{72,8},... | collective-permute-start | bytes 12296 | tf_op jit(solution)/shard_map/ppermute | solution.py:364
  29.5 4.0 %shard_map.103 = (bf16[128,2048]{1,0:T(8,128)(2,1)}, bf16[128,2048]{1,0:T(8,128)(2,1)}, bf16[128,2048]{1,0:T(8,128)(2,1)}, f32[128,2048]{1,0:T(8,128)}) custom-call(s32[1,8]{1,0:T(1,128)S(1)} %copy-done.12, bf16[128,2048]{1,0:T(8,128)(2,1)S(1)} %bitcast.21, bf16[128,2048]{1,0:T(8,128)(2,1)S(1)} %bitcast.18, bf16[128,2048]{1,0:T(8,128)(2,1)S(1)} %bitcast.15), custom_call_target="tpu_custom_call" | custom-call | flops 134217728 | bytes 4194304 | tf_op jit(solution)/shard_map/pallas_call | solution.py:365
  33.5 7.8 %all-to-all-done.parts = f32[8,128,128]{2,1,0:T(8,128)S(1)} async-done(((f32[8,128,128]{2,1,0:T(8,128)}), f32[8,128,128]{2,1,0:T(8,128)S(1)}, u32[]{:S(2)}, u32[]{:S(2)}) %all-to-all-start) | async-done | bytes 524320 | tf_op jit(solution)/shard_map/all_to_all | solution.py:344
  42.0 22.5 %all_to_all.32.coming = f32[8,136,128]{2,1,0:T(8,128)S(1)} all-to-all(f32[8,136,128]{2,1,0:T(8,128)S(1)} %shard_map.104), channel_id=1, replica_groups={{0,2,4,6,8,10,12,14},{1,3,5,7,9,11,13,15},{16,18,20,22,24,26,28,30},{17..., dimensions={0} | all-to-all | bytes 1114112 | tf_op jit(solution)/shard_map/all_to_all | solution.py:344
  65.1 2.6 %collective-permute-start.3 = (f32[1088,128]{1,0:T(8,128)S(1)}, f32[1088,128]{1,0:T(8,128)S(1)}, u32[]{:S(2)}, u32[]{:S(2)}) collective-permute-start(f32[1088,128]{1,0:T(8,128)S(1)} %shard_map.105), channel_id=1, source_target_pairs={{0,1},{1,0},{2,3},{3,2},{4,5},{5,4},{6,7},{7,6},{8,9},{9,8},{10,11... | collective-permute-start | bytes 1671176 | tf_op jit(solution)/shard_map/ppermute | solution.py:341
  67.7 1.6 %collective-permute-done.3.ready = f32[1088,128]{1,0:T(8,128)S(1)} collective-permute-done((f32[1088,128]{1,0:T(8,128)S(1)}, f32[1088,128]{1,0:T(8,128)S(1)}, u32[]{:S(2)}, u32[]{:S(2)}) %collective-permute-start.3) | collective-permute-done | bytes 557088 | tf_op jit(solution)/shard_map/ppermute | solution.py:341
  69.3 2.6 %shard_map.106 = (bf16[128,2048]{1,0:T(8,128)(2,1)}, bf16[128,2048]{1,0:T(8,128)(2,1)S(1)}, bf16[16,128,128]{2,1,0:T(8,128)(2,1)S(1)}, f32[8,128,128]{2,1,0:T(8,...) custom-call(s32[1,8]{1,0:T(1,128)S(1)} %copy-done.12, bf16[128,2048]{1,0:T(8,128)(2,1)S(1)} %copy-done.7, ...), custom_call_target="tpu_custom_call" | custom-call | flops 134217728 | bytes 5242880 | tf_op jit(solution)/shard_map/pallas_call | solution.py:378
  73.4 2.3 %collective-permute-start.4 = (f32[8,128,128]{2,1,0:T(8,128)S(1)}, f32[8,128,128]{2,1,0:T(8,128)S(1)}, u32[]{:S(2)}, u32[]{:S(2)}) collective-permute-start(f32[8,128,128]{2,1,0:T(8,128)S(1)} %get-tuple-element.45), channel_id=1, source_target_pairs={{0,1},{1,0},{2,3},{3,2},{4,5},{5,4},{6,7},{7,6},{8,9},{9,8},{10,11... | collective-permute-start | bytes 1572872 | tf_op jit(solution)/shard_map/ppermute | solution.py:341
  75.7 5.3 %all-to-all-start.2 = ((f32[8,8,128]{2,1,0:T(8,128)}), f32[8,8,128]{2,1,0:T(8,128)S(1)}, u32[]{:S(2)}, u32[]{:S(2)}) async-start(f32[8,8,128]{2,1,0:T(8,128)} %bitcast.5), calls=%async_computation.2 | async-start | bytes 65536 | tf_op jit(solution)/shard_map/all_to_all | solution.py:386
  81.0 1.4 %shard_map.107 = f32[8,128,128]{2,1,0:T(8,128)} custom-call(s32[1,8]{1,0:T(1,128)S(1)} %copy-done.12, f32[8,128,128]{2,1,0:T(8,128)S(1)} %get-tuple-element.44.keep, f32[8,128,128]{2,1,0:T(8,128)S(1)} %collective-permute-done.4.recv.theirs), custom_call_target="tpu_custom_call" | custom-call | flops 262144 | bytes 1572864 | tf_op jit(solution)/shard_map/pallas_call | solution.py:388
  82.5 5.4 %all-to-all-done.2 = f32[8,8,128]{2,1,0:T(8,128)S(1)} async-done(((f32[8,8,128]{2,1,0:T(8,128)}), f32[8,8,128]{2,1,0:T(8,128)S(1)}, u32[]{:S(2)}, u32[]{:S(2)}) %all-to-all-start.2) | async-done | bytes 32800 | tf_op jit(solution)/shard_map/all_to_all | solution.py:386
  87.9 3.5 %all-to-all-start.3 = ((f32[8,128,128]{2,1,0:T(8,128)}), f32[8,128,128]{2,1,0:T(8,128)S(1)}, u32[]{:S(2)}, u32[]{:S(2)}) async-start(f32[8,128,128]{2,1,0:T(8,128)} %shard_map.107), calls=%async_computation.3 | async-start | bytes 1048576 | tf_op jit(solution)/shard_map/all_to_all | solution.py:344
  91.4 4.7 %collective-permute-start.5 = (f32[8,128]{1,0:T(8,128)S(1)}, f32[8,128]{1,0:T(8,128)S(1)}, u32[]{:S(2)}, u32[]{:S(2)}) collective-permute-start(f32[8,128]{1,0:T(8,128)S(1)} %bitcast_reduce_fusion), channel_id=1, source_target_pairs={{0,256},{16,272},{32,288},{48,304},{64,320},{80,336},{96,352},{112... | collective-permute-start | bytes 12296 | tf_op jit(solution)/shard_map/ppermute | solution.py:393
  96.1 1.2 collective-permute-done.5
  97.3 3.1 %collective-permute-start.6 = (f32[8,128]{1,0:T(8,128)S(1)}, f32[8,128]{1,0:T(8,128)S(1)}, u32[]{:S(2)}, u32[]{:S(2)}) collective-permute-start(f32[8,128]{1,0:T(8,128)S(1)} %add.22), channel_id=1, source_target_pairs={{0,128},{16,144},{32,160},{48,176},{64,192},{80,208},{96,224},{112... | collective-permute-start | bytes 12296 | tf_op jit(solution)/shard_map/ppermute | solution.py:393
  100.4 1.5 %collective-permute-done.6 = f32[8,128]{1,0:T(8,128)S(1)} collective-permute-done((f32[8,128]{1,0:T(8,128)S(1)}, f32[8,128]{1,0:T(8,128)S(1)}, u32[]{:S(2)}, u32[]{:S(2)}) %collective-permute-start.6) | collective-permute-done | bytes 4128 | tf_op jit(solution)/shard_map/ppermute | solution.py:393
  101.9 5.5 %all-to-all-done.3.parts = f32[8,128,128]{2,1,0:T(8,128)S(1)} async-done(((f32[8,128,128]{2,1,0:T(8,128)}), f32[8,128,128]{2,1,0:T(8,128)S(1)}, u32[]{:S(2)}, u32[]{:S(2)}) %all-to-all-start.3) | async-done | bytes 524320 | tf_op jit(solution)/shard_map/all_to_all | solution.py:344
  107.4 1.5 %shard_map.108 = f32[8,136,128]{2,1,0:T(8,128)} custom-call(s32[1,8]{1,0:T(1,128)S(1)} %copy-done.12, f32[8,128,128]{2,1,0:T(8,128)S(1)} %all-to-all-done.3.parts, f32[8,128]{1,0:T(8,128)S(1)} %add.23.terms), custom_call_target="tpu_custom_call" | custom-call | flops 262144 | bytes 1048576 | tf_op jit(solution)/shard_map/pallas_call | solution.py:394
  108.8 3.5 %all-to-all-start.4 = ((f32[8,136,128]{2,1,0:T(8,128)}), f32[8,136,128]{2,1,0:T(8,128)S(1)}, u32[]{:S(2)}, u32[]{:S(2)}) async-start(f32[8,136,128]{2,1,0:T(8,128)} %shard_map.108), calls=%async_computation.4 | async-start | bytes 1114112 | tf_op jit(solution)/shard_map/all_to_all | solution.py:344
  112.4 7.0 %shard_map.109 = (bf16[128,2048]{1,0:T(8,128)(2,1)}, f32[128,2048]{1,0:T(8,128)}, f32[128,2048]{1,0:T(8,128)}) custom-call(s32[1,8]{1,0:T(1,128)S(1)} %copy-done.12, bf16[128,2048]{1,0:T(8,128)(2,1)} %bitcast.20, bf16[128,2048]{1,0:T(8,128)(2,1)} %bitcast.13, bf16[128,2048]{1,0:T(8,128)(2,1)} %get-tuple-element.37.qf.refs_2_, ...), custom_call_target="tpu_custom_call" | custom-call | flops 335544320 | bytes 7340032 | tf_op jit(solution)/shard_map/pallas_call | solution.py:399
  119.4 9.0 %all-to-all-done.4.coming = f32[8,136,128]{2,1,0:T(8,128)S(1)} async-done(((f32[8,136,128]{2,1,0:T(8,128)}), f32[8,136,128]{2,1,0:T(8,128)S(1)}, u32[]{:S(2)}, u32[]{:S(2)}) %all-to-all-start.4) | async-done | bytes 557088 | tf_op jit(solution)/shard_map/all_to_all | solution.py:344
  129.0 4.9 %collective-permute-start.7 = (f32[1032,128]{1,0:T(8,128)S(1)}, f32[1032,128]{1,0:T(8,128)S(1)}, u32[]{:S(2)}, u32[]{:S(2)}) collective-permute-start(f32[1032,128]{1,0:T(8,128)S(1)} %shard_map.110), channel_id=1, source_target_pairs={{0,1},{1,0},{2,3},{3,2},{4,5},{5,4},{6,7},{7,6},{8,9},{9,8},{10,11... | collective-permute-start | bytes 1585160 | tf_op jit(solution)/shard_map/ppermute | solution.py:341
  134.0 1.5 %collective-permute-done.7.ready = f32[1032,128]{1,0:T(8,128)S(1)} collective-permute-done((f32[1032,128]{1,0:T(8,128)S(1)}, f32[1032,128]{1,0:T(8,128)S(1)}, u32[]{:S(2)}, u32[]{:S(2)}) %collective-permute-start.7) | collective-permute-done | bytes 528416 | tf_op jit(solution)/shard_map/ppermute | solution.py:341
  135.5 3.8 %shard_map.111 = (bf16[128,2048]{1,0:T(8,128)(2,1)}, bf16[128,2048]{1,0:T(8,128)(2,1)}, f32[1,64]{1,0:T(1,128)}) custom-call(s32[1,8]{1,0:T(1,128)S(1)} %copy-done.12, bf16[128,2048]{1,0:T(8,128)(2,1)S(1)} %bitcast.19, bf16[128,2048]{1,0:T(8,128)(2,1)S(1)} %bitcast.16, bf16[128,2048]{1,0:T(8,128)(2,1)S(1)} %copy-done.5, ...), custom_call_target="tpu_custom_call" | custom-call | flops 134217728 | bytes 5242880 | tf_op jit(solution)/shard_map/pallas_call | solution.py:415
  (40 shorter events, 5.1 us)
Async XLA Ops:
  0.6 0.7 copy-start.12
  1.3 1.0 copy-start
  2.3 1.0 copy-start.3
  4.5 14.1 %collective-permute-start = (f32[8,128,128]{2,1,0:T(8,128)S(1)}, f32[8,128,128]{2,1,0:T(8,128)S(1)}, u32[]{:S(2)}, u32[]{:S(2)}) collective-permute-start(f32[8,128,128]{2,1,0:T(8,128)S(1)} %get-tuple-element.35), channel_id=1, source_target_pairs={{0,1},{1,0},{2,3},{3,2},{4,5},{5,4},{6,7},{7,6},{8,9},{9,8},{10,11... | collective-permute-start | bytes 1572872 | tf_op jit(solution)/shard_map/ppermute | solution.py:341
  13.4 0.7 copy-start.13
  14.2 4.3 %collective-permute-start.1 = (f32[8,128]{1,0:T(8,128)S(1)}, f32[8,128]{1,0:T(8,128)S(1)}, u32[]{:S(2)}, u32[]{:S(2)}) collective-permute-start(f32[8,128]{1,0:T(8,128)S(1)} %and_select_fusion), channel_id=1, source_target_pairs={{0,128},{16,144},{32,160},{48,176},{64,192},{80,208},{96,224},{112... | collective-permute-start | bytes 12296 | tf_op jit(solution)/shard_map/ppermute | solution.py:352
  18.6 10.9 %copy-start.6 = (bf16[1,128,2048]{2,1,0:T(8,128)(2,1)S(1)}, bf16[1,128,2048]{2,1,0:T(8,128)(2,1)}, u32[]{:S(2)}) copy-start(bf16[1,128,2048]{2,1,0:T(8,128)(2,1)} %param.6) | copy-start | bytes 1572868
  20.0 9.5 %copy-start.1 = (bf16[1,128,2048]{2,1,0:T(8,128)(2,1)S(1)}, bf16[1,128,2048]{2,1,0:T(8,128)(2,1)}, u32[]{:S(2)}) copy-start(bf16[1,128,2048]{2,1,0:T(8,128)(2,1)} %param.8) | copy-start | bytes 1572868
  20.0 9.5 %copy-start.4 = (bf16[1,128,2048]{2,1,0:T(8,128)(2,1)S(1)}, bf16[1,128,2048]{2,1,0:T(8,128)(2,1)}, u32[]{:S(2)}) copy-start(bf16[1,128,2048]{2,1,0:T(8,128)(2,1)} %param.7) | copy-start | bytes 1572868
  20.0 21.3 %all-to-all-start = ((f32[8,128,128]{2,1,0:T(8,128)}), f32[8,128,128]{2,1,0:T(8,128)S(1)}, u32[]{:S(2)}, u32[]{:S(2)}) async-start(f32[8,128,128]{2,1,0:T(8,128)} %shard_map.102), calls=%async_computation | async-start | bytes 1048576 | tf_op jit(solution)/shard_map/all_to_all | solution.py:344
  24.8 16.5 %collective-permute-start.2 = (f32[8,128]{1,0:T(8,128)S(1)}, f32[8,128]{1,0:T(8,128)S(1)}, u32[]{:S(2)}, u32[]{:S(2)}) collective-permute-start(f32[8,128]{1,0:T(8,128)S(1)} %fusion.1), channel_id=1, source_target_pairs={{0,0},{257,1},{18,2},{275,3},{36,4},{293,5},{54,6},{311,7},{72,8},... | collective-permute-start | bytes 12296 | tf_op jit(solution)/shard_map/ppermute | solution.py:364
  42.0 27.3 %copy-start.9 = (bf16[1,128,2048]{2,1,0:T(8,128)(2,1)S(1)}, bf16[1,128,2048]{2,1,0:T(8,128)(2,1)}, u32[]{:S(2)}) copy-start(bf16[1,128,2048]{2,1,0:T(8,128)(2,1)} %param.9) | copy-start | bytes 1572868
  64.4 4.8 %copy-start.7 = (bf16[128,2048]{1,0:T(8,128)(2,1)S(1)}, bf16[128,2048]{1,0:T(8,128)(2,1)}, u32[]{:S(2)}) copy-start(bf16[128,2048]{1,0:T(8,128)(2,1)} %get-tuple-element.37.qf.refs_2_) | copy-start | bytes 1572868
  64.4 4.8 %copy-start.8 = (f32[128,2048]{1,0:T(8,128)S(1)}, f32[128,2048]{1,0:T(8,128)}, u32[]{:S(2)}) copy-start(f32[128,2048]{1,0:T(8,128)} %get-tuple-element.38.intra) | copy-start | bytes 3145732
  65.1 4.2 %collective-permute-start.3 = (f32[1088,128]{1,0:T(8,128)S(1)}, f32[1088,128]{1,0:T(8,128)S(1)}, u32[]{:S(2)}, u32[]{:S(2)}) collective-permute-start(f32[1088,128]{1,0:T(8,128)S(1)} %shard_map.105), channel_id=1, source_target_pairs={{0,1},{1,0},{2,3},{3,2},{4,5},{5,4},{6,7},{7,6},{8,9},{9,8},{10,11... | collective-permute-start | bytes 1671176 | tf_op jit(solution)/shard_map/ppermute | solution.py:341
  71.8 0.8 copy-start.10
  72.6 0.8 copy-start.11
  73.4 7.6 %collective-permute-start.4 = (f32[8,128,128]{2,1,0:T(8,128)S(1)}, f32[8,128,128]{2,1,0:T(8,128)S(1)}, u32[]{:S(2)}, u32[]{:S(2)}) collective-permute-start(f32[8,128,128]{2,1,0:T(8,128)S(1)} %get-tuple-element.45), channel_id=1, source_target_pairs={{0,1},{1,0},{2,3},{3,2},{4,5},{5,4},{6,7},{7,6},{8,9},{9,8},{10,11... | collective-permute-start | bytes 1572872 | tf_op jit(solution)/shard_map/ppermute | solution.py:341
  75.7 12.2 %all-to-all-start.2 = ((f32[8,8,128]{2,1,0:T(8,128)}), f32[8,8,128]{2,1,0:T(8,128)S(1)}, u32[]{:S(2)}, u32[]{:S(2)}) async-start(f32[8,8,128]{2,1,0:T(8,128)} %bitcast.5), calls=%async_computation.2 | async-start | bytes 65536 | tf_op jit(solution)/shard_map/all_to_all | solution.py:386
  87.9 19.5 %all-to-all-start.3 = ((f32[8,128,128]{2,1,0:T(8,128)}), f32[8,128,128]{2,1,0:T(8,128)S(1)}, u32[]{:S(2)}, u32[]{:S(2)}) async-start(f32[8,128,128]{2,1,0:T(8,128)} %shard_map.107), calls=%async_computation.3 | async-start | bytes 1048576 | tf_op jit(solution)/shard_map/all_to_all | solution.py:344
  91.4 5.9 %collective-permute-start.5 = (f32[8,128]{1,0:T(8,128)S(1)}, f32[8,128]{1,0:T(8,128)S(1)}, u32[]{:S(2)}, u32[]{:S(2)}) collective-permute-start(f32[8,128]{1,0:T(8,128)S(1)} %bitcast_reduce_fusion), channel_id=1, source_target_pairs={{0,256},{16,272},{32,288},{48,304},{64,320},{80,336},{96,352},{112... | collective-permute-start | bytes 12296 | tf_op jit(solution)/shard_map/ppermute | solution.py:393
  97.3 4.6 %collective-permute-start.6 = (f32[8,128]{1,0:T(8,128)S(1)}, f32[8,128]{1,0:T(8,128)S(1)}, u32[]{:S(2)}, u32[]{:S(2)}) collective-permute-start(f32[8,128]{1,0:T(8,128)S(1)} %add.22), channel_id=1, source_target_pairs={{0,128},{16,144},{32,160},{48,176},{64,192},{80,208},{96,224},{112... | collective-permute-start | bytes 12296 | tf_op jit(solution)/shard_map/ppermute | solution.py:393
  108.8 19.6 %all-to-all-start.4 = ((f32[8,136,128]{2,1,0:T(8,128)}), f32[8,136,128]{2,1,0:T(8,128)S(1)}, u32[]{:S(2)}, u32[]{:S(2)}) async-start(f32[8,136,128]{2,1,0:T(8,128)} %shard_map.108), calls=%async_computation.4 | async-start | bytes 1114112 | tf_op jit(solution)/shard_map/all_to_all | solution.py:344
  128.4 7.1 %copy-start.2 = (bf16[1,128,2048]{2,1,0:T(8,128)(2,1)S(1)}, bf16[1,128,2048]{2,1,0:T(8,128)(2,1)}, u32[]{:S(2)}) copy-start(bf16[1,128,2048]{2,1,0:T(8,128)(2,1)} %param.8) | copy-start | bytes 1572868
  128.4 7.1 %copy-start.5 = (bf16[128,2048]{1,0:T(8,128)(2,1)S(1)}, bf16[128,2048]{1,0:T(8,128)(2,1)}, u32[]{:S(2)}) copy-start(bf16[128,2048]{1,0:T(8,128)(2,1)} %get-tuple-element.50.refs_3_.kf) | copy-start | bytes 1572868
  129.0 6.5 %collective-permute-start.7 = (f32[1032,128]{1,0:T(8,128)S(1)}, f32[1032,128]{1,0:T(8,128)S(1)}, u32[]{:S(2)}, u32[]{:S(2)}) collective-permute-start(f32[1032,128]{1,0:T(8,128)S(1)} %shard_map.110), channel_id=1, source_target_pairs={{0,1},{1,0},{2,3},{3,2},{4,5},{5,4},{6,7},{7,6},{8,9},{9,8},{10,11... | collective-permute-start | bytes 1585160 | tf_op jit(solution)/shard_map/ppermute | solution.py:341
